TPU v7x, 256 devices: a whole 4x4x8 slice. The times are simulated.
256 devices in a mesh: queue: 16 (over y, z_lo), seq: 16 (over z_hi, x, core).
Axes of the slice: x: 4, y: 4, z: 8 (z_hi: 2, z_lo: 4; z = z_hi * 4 + z_lo), core: 2. Of those that a mesh axis runs over, the one named last changes fastest.
Arguments:
- latent: bfloat16 [16, 3072, 4096], P('queue', 'seq'), may hold values from -6 to 6
- queries: bfloat16 [16, 3072, 4096], P('queue', 'seq'), may hold values from -80.991455 to 80.991455
- key_rows: bfloat16 [16, 3072, 4096], P('queue', 'seq'), may hold values from -4 to 4
- values: bfloat16 [16, 3072, 4096], P('queue', 'seq'), may hold values from -6 to 6
- mod_table: float32 [50, 2, 4096], replicated, may hold values from -3 to 3
- levels: int32 [16], P('queue'), may hold values from 0 to 49
- fresh_noise: bfloat16 [3072, 4096], P('seq'), may hold values from -6 to 6
Outputs:
- next_latent: bfloat16 [16, 3072, 4096], P('queue', 'seq')
All inputs are finite; a program needn't handle non-finite values.
Results may differ from a plain program's by a relative error of at most 0.0048.
Values may be sent and summed in bfloat16 or wider, within the bound.
No kernel may reach another device: no remote copies, remote signals or barrier semaphores. Data moves between devices by JAX's collectives and lax.ppermute only.
A program may use at most 64 MiB of HBM per device.

v0:
```python
import math

import jax
import jax.numpy as jnp
from jax import lax
from jax.sharding import PartitionSpec as P

HEADS = 32
HEAD_DIM = 128
STEPS = 50


def shifted_2(value, axis, steps):
    count = lax.axis_size(axis)
    leading, last = (max(0, -steps), min(count, count - steps))
    return lax.ppermute(value, axis, [(source, source + steps) for source in range(leading, last)])


def attend(queries, key_rows, values):
    length = queries.shape[0]
    block_rows = math.gcd(length, 512)
    block_count = length // block_rows
    factor = queries.shape[2] ** (-0.5)
    blocks = queries.reshape(block_count, block_rows, queries.shape[1], queries.shape[2])

    def one_block(row_block):
        scores = (
            jnp.einsum("qhd,khd->hqk", row_block, key_rows, preferred_element_type=jnp.float32)
            * factor
        )
        largest = jnp.max(scores, axis=-1, keepdims=True)
        powers = jnp.exp(scores - largest)
        weights = (powers / jnp.sum(powers, axis=-1, keepdims=True)).astype(jnp.bfloat16)
        mixed = jnp.einsum("hqk,khd->qhd", weights, values, preferred_element_type=jnp.float32)
        return mixed.astype(jnp.bfloat16)

    return lax.map(one_block, blocks).reshape(queries.shape)


def per_heads(pieces):
    query_part, key_part, value_part = pieces
    mixed = attend(query_part[:, 0], key_part[:, 0], value_part[:, 0])
    return mixed[:, None]


def velocity_of(queries, key_rows, values, mod_table, levels):
    local_rows = queries.shape[1]
    devices = lax.axis_size("seq")
    per_device = HEADS // devices
    arranged = [
        part[0].reshape(local_rows, devices, per_device, HEAD_DIM)
        for part in (queries, key_rows, values)
    ]
    headwise = per_heads(
        (
            lax.all_to_all(arranged[0], "seq", split_axis=1, concat_axis=0, tiled=True),
            lax.all_to_all(arranged[1], "seq", split_axis=1, concat_axis=0, tiled=True),
            lax.all_to_all(arranged[2], "seq", split_axis=1, concat_axis=0, tiled=True),
        )
    )
    tokenwise = lax.all_to_all(headwise, "seq", split_axis=0, concat_axis=1, tiled=True)
    attended = tokenwise.reshape(local_rows, HEADS * HEAD_DIM).astype(jnp.float32)
    meansq = jnp.mean(attended * attended, axis=-1, keepdims=True)
    modrow = lax.dynamic_index_in_dim(mod_table, levels[0], 0, keepdims=False)
    velocity = (attended * lax.rsqrt(meansq + 1e-06) * (1.0 + modrow[0]) + modrow[1]).astype(
        jnp.bfloat16
    )
    return lax.optimization_barrier(velocity[None])


def update(latent, velocity, levels):
    step_size = (levels[0] + 1).astype(jnp.float32) / STEPS
    return (latent.astype(jnp.float32) - step_size * velocity.astype(jnp.float32)).astype(
        jnp.bfloat16
    )


def on_device(latent, queries, key_rows, values, mod_table, levels, fresh_noise):
    velocity = velocity_of(queries, key_rows, values, mod_table, levels)
    shifted = shifted_2(update(latent, velocity, levels), "queue", 1)
    leading = lax.axis_index("queue") == 0
    return jnp.where(leading, fresh_noise[None], shifted)


def solution(mesh):
    return jax.shard_map(
        on_device,
        mesh=mesh,
        in_specs=(
            P("queue", "seq", None),
            P("queue", "seq", None),
            P("queue", "seq", None),
            P("queue", "seq", None),
            P(),
            P("queue"),
            P("seq", None),
        ),
        out_specs=P("queue", "seq", None),
        check_vma=False,
    )
```

profile of v0, /device:TPU:1, one launch (start us, length us, event | category | flops | bytes accessed | tf_op | source)
XLA Modules:
  0.0 352.4 jit_solution(15093576817597660464)
XLA Ops:
  0.0 2.8 reshape_squeeze.12
  2.8 2.7 copy.49
  5.5 12.4 %all-to-all-start = ((bf16[192,16,2,128]{3,2,0,1:T(2,128)(2,1)}), bf16[192,16,2,128]{3,2,0,1:T(2,128)(2,1)S(1)}, u32[]{:S(2)}, u32[]{:S(2)}) async-start(bf16[192,16,2,128]{3,2,0,1:T(2,128)(2,1)} %copy.49), calls=%async_computation | async-start | bytes 3145728 | tf_op jit(solution)/shard_map/all_to_all | solution.py:56
  17.9 2.8 reshape_squeeze.14
  20.8 1.8 copy.51
  22.5 24.1 %all-to-all-done = bf16[192,16,2,128]{3,2,0,1:T(2,128)(2,1)S(1)} async-done(((bf16[192,16,2,128]{3,2,0,1:T(2,128)(2,1)}), bf16[192,16,2,128]{3,2,0,1:T(2,128)(2,1)S(1)}, u32[]{:S(2)}, u32[]{:S(2)}) %all-to-all-start) | async-done | bytes 1572896 | tf_op jit(solution)/shard_map/all_to_all | solution.py:56
  46.7 14.7 %all-to-all-start.1 = ((bf16[192,16,2,128]{3,0,2,1:T(8,128)(2,1)}), bf16[192,16,2,128]{3,0,2,1:T(8,128)(2,1)S(1)}, u32[]{:S(2)}, u32[]{:S(2)}) async-start(bf16[192,16,2,128]{3,0,2,1:T(8,128)(2,1)} %copy.51), calls=%async_computation.1 | async-start | bytes 3145728 | tf_op jit(solution)/shard_map/all_to_all | solution.py:57
  61.4 3.8 %reshape_squeeze.15 = bf16[192,16,2,128]{3,2,1,0:T(2,128)(2,1)} reshape(bf16[1,192,4096]{2,1,0:T(8,128)(2,1)} %param.12) | data formatting | bytes 3145728 | tf_op jit(solution)/shard_map/reshape;squeeze | solution.py:51
  65.1 3.2 copy.53
  68.3 18.4 %all-to-all-done.1 = bf16[192,16,2,128]{3,0,2,1:T(8,128)(2,1)S(1)} async-done(((bf16[192,16,2,128]{3,0,2,1:T(8,128)(2,1)}), bf16[192,16,2,128]{3,0,2,1:T(8,128)(2,1)S(1)}, u32[]{:S(2)}, u32[]{:S(2)}) %all-to-all-start.1) | async-done | bytes 1572896 | tf_op jit(solution)/shard_map/all_to_all | solution.py:57
  86.8 18.8 %all-to-all-start.2 = ((bf16[192,16,2,128]{3,0,2,1:T(8,128)(2,1)}), bf16[192,16,2,128]{3,0,2,1:T(8,128)(2,1)}, u32[]{:S(2)}, u32[]{:S(2)}) async-start(bf16[192,16,2,128]{3,0,2,1:T(8,128)(2,1)} %copy.53), calls=%async_computation.2 | async-start | bytes 3145728 | tf_op jit(solution)/shard_map/all_to_all | solution.py:58
  105.6 1.6 copy.50
  107.2 0.1 copy.52
  107.3 23.8 %all-to-all-done.2 = bf16[192,16,2,128]{3,0,2,1:T(8,128)(2,1)} async-done(((bf16[192,16,2,128]{3,0,2,1:T(8,128)(2,1)}), bf16[192,16,2,128]{3,0,2,1:T(8,128)(2,1)}, u32[]{:S(2)}, u32[]{:S(2)}) %all-to-all-start.2) | async-done | bytes 1572896 | tf_op jit(solution)/shard_map/all_to_all | solution.py:58
  131.1 1.5 copy.54
  132.6 99.5 %while.10 = (s32[]{:T(128)}, bf16[6,512,2,128]{3,1,0,2:T(8,128)(2,1)}, bf16[6,512,2,128]{3,1,0,2:T(8,128)(2,1)}, bf16[3072,2,128]{2,0,1:T(8,128)(2,1)S(1)}, bf16[3072,2,128]{2,0,1:T(8,128)(2,1)S(1)}, /*index=5*/s32[]{:T(128)}) while((s32[]{:T(128)}, bf16[6,512,2,128]{3,1,0,2:T(8,128)(2,1)}, bf16[6,512,2,128]{3,1,0,2:T(8,128)(2,1)}, ...), condition=%wide.region_3.4_spmd, body=%wide.region_0.3_spmd.sunk | while | flops 1626475520 | bytes 28844116 | solution.py:37
  132.6 9.5 %fusion.46 = (f32[2,512]{1,0:T(2,128)S(1)}, f32[2,512,3072]{2,1,0:T(8,128)}) fusion(bf16[3072,2,128]{2,0,1:T(8,128)(2,1)S(1)} %get-tuple-element.127, bf16[6,512,2,128]{3,1,0,2:T(8,128)(2,1)} %get-tuple-element.126, s32[]{:T(128)S(6)} %copy.77), kind=kOutput, calls=%fused_computation.30.clone.1 | convolution fusion | flops 814746624 | bytes 14422020 | tf_op jit(solution)/shard_map/while/body/eval_jaxpr/sub | solution.py:32
  142.1 7.1 %fusion.47 = bf16[6,512,2,128]{3,1,0,2:T(8,128)(2,1)} fusion(bf16[6,512,2,128]{3,1,0,2:T(8,128)(2,1)} %get-tuple-element.119, s32[]{:T(128)S(6)} %copy.77, bf16[3072,2,128]{2,0,1:T(8,128)(2,1)S(1)} %get-tuple-element.128, f32[2,512,3072]{2,1,0:T(8,128)} %get-tuple-element.110, f32[2,512]{1,0:T(2,128)S(1)} %get-tuple-element.111), kind=kOutput, calls=%fused_computation.10.clone.1 | convolution fusion | flops 811728896 | bytes 14422020 | tf_op jit(solution)/shard_map/while/body/eval_jaxpr/hqk,khd->qhd/dot_general | solution.py:34
  149.2 9.5 %fusion.46 = (f32[2,512]{1,0:T(2,128)S(1)}, f32[2,512,3072]{2,1,0:T(8,128)}) fusion(bf16[3072,2,128]{2,0,1:T(8,128)(2,1)S(1)} %get-tuple-element.127, bf16[6,512,2,128]{3,1,0,2:T(8,128)(2,1)} %get-tuple-element.126, s32[]{:T(128)S(6)} %copy.77), kind=kOutput, calls=%fused_computation.30.clone.1 | convolution fusion | flops 814746624 | bytes 14422020 | tf_op jit(solution)/shard_map/while/body/eval_jaxpr/sub | solution.py:32
  158.7 7.1 %fusion.47 = bf16[6,512,2,128]{3,1,0,2:T(8,128)(2,1)} fusion(bf16[6,512,2,128]{3,1,0,2:T(8,128)(2,1)} %get-tuple-element.119, s32[]{:T(128)S(6)} %copy.77, bf16[3072,2,128]{2,0,1:T(8,128)(2,1)S(1)} %get-tuple-element.128, f32[2,512,3072]{2,1,0:T(8,128)} %get-tuple-element.110, f32[2,512]{1,0:T(2,128)S(1)} %get-tuple-element.111), kind=kOutput, calls=%fused_computation.10.clone.1 | convolution fusion | flops 811728896 | bytes 14422020 | tf_op jit(solution)/shard_map/while/body/eval_jaxpr/hqk,khd->qhd/dot_general | solution.py:34
  165.8 9.5 %fusion.46 = (f32[2,512]{1,0:T(2,128)S(1)}, f32[2,512,3072]{2,1,0:T(8,128)}) fusion(bf16[3072,2,128]{2,0,1:T(8,128)(2,1)S(1)} %get-tuple-element.127, bf16[6,512,2,128]{3,1,0,2:T(8,128)(2,1)} %get-tuple-element.126, s32[]{:T(128)S(6)} %copy.77), kind=kOutput, calls=%fused_computation.30.clone.1 | convolution fusion | flops 814746624 | bytes 14422020 | tf_op jit(solution)/shard_map/while/body/eval_jaxpr/sub | solution.py:32
  175.2 7.1 %fusion.47 = bf16[6,512,2,128]{3,1,0,2:T(8,128)(2,1)} fusion(bf16[6,512,2,128]{3,1,0,2:T(8,128)(2,1)} %get-tuple-element.119, s32[]{:T(128)S(6)} %copy.77, bf16[3072,2,128]{2,0,1:T(8,128)(2,1)S(1)} %get-tuple-element.128, f32[2,512,3072]{2,1,0:T(8,128)} %get-tuple-element.110, f32[2,512]{1,0:T(2,128)S(1)} %get-tuple-element.111), kind=kOutput, calls=%fused_computation.10.clone.1 | convolution fusion | flops 811728896 | bytes 14422020 | tf_op jit(solution)/shard_map/while/body/eval_jaxpr/hqk,khd->qhd/dot_general | solution.py:34
  182.4 9.5 %fusion.46 = (f32[2,512]{1,0:T(2,128)S(1)}, f32[2,512,3072]{2,1,0:T(8,128)}) fusion(bf16[3072,2,128]{2,0,1:T(8,128)(2,1)S(1)} %get-tuple-element.127, bf16[6,512,2,128]{3,1,0,2:T(8,128)(2,1)} %get-tuple-element.126, s32[]{:T(128)S(6)} %copy.77), kind=kOutput, calls=%fused_computation.30.clone.1 | convolution fusion | flops 814746624 | bytes 14422020 | tf_op jit(solution)/shard_map/while/body/eval_jaxpr/sub | solution.py:32
  191.8 7.1 %fusion.47 = bf16[6,512,2,128]{3,1,0,2:T(8,128)(2,1)} fusion(bf16[6,512,2,128]{3,1,0,2:T(8,128)(2,1)} %get-tuple-element.119, s32[]{:T(128)S(6)} %copy.77, bf16[3072,2,128]{2,0,1:T(8,128)(2,1)S(1)} %get-tuple-element.128, f32[2,512,3072]{2,1,0:T(8,128)} %get-tuple-element.110, f32[2,512]{1,0:T(2,128)S(1)} %get-tuple-element.111), kind=kOutput, calls=%fused_computation.10.clone.1 | convolution fusion | flops 811728896 | bytes 14422020 | tf_op jit(solution)/shard_map/while/body/eval_jaxpr/hqk,khd->qhd/dot_general | solution.py:34
  198.9 9.5 %fusion.46 = (f32[2,512]{1,0:T(2,128)S(1)}, f32[2,512,3072]{2,1,0:T(8,128)}) fusion(bf16[3072,2,128]{2,0,1:T(8,128)(2,1)S(1)} %get-tuple-element.127, bf16[6,512,2,128]{3,1,0,2:T(8,128)(2,1)} %get-tuple-element.126, s32[]{:T(128)S(6)} %copy.77), kind=kOutput, calls=%fused_computation.30.clone.1 | convolution fusion | flops 814746624 | bytes 14422020 | tf_op jit(solution)/shard_map/while/body/eval_jaxpr/sub | solution.py:32
  208.4 7.1 %fusion.47 = bf16[6,512,2,128]{3,1,0,2:T(8,128)(2,1)} fusion(bf16[6,512,2,128]{3,1,0,2:T(8,128)(2,1)} %get-tuple-element.119, s32[]{:T(128)S(6)} %copy.77, bf16[3072,2,128]{2,0,1:T(8,128)(2,1)S(1)} %get-tuple-element.128, f32[2,512,3072]{2,1,0:T(8,128)} %get-tuple-element.110, f32[2,512]{1,0:T(2,128)S(1)} %get-tuple-element.111), kind=kOutput, calls=%fused_computation.10.clone.1 | convolution fusion | flops 811728896 | bytes 14422020 | tf_op jit(solution)/shard_map/while/body/eval_jaxpr/hqk,khd->qhd/dot_general | solution.py:34
  215.5 9.5 %fusion.46 = (f32[2,512]{1,0:T(2,128)S(1)}, f32[2,512,3072]{2,1,0:T(8,128)}) fusion(bf16[3072,2,128]{2,0,1:T(8,128)(2,1)S(1)} %get-tuple-element.127, bf16[6,512,2,128]{3,1,0,2:T(8,128)(2,1)} %get-tuple-element.126, s32[]{:T(128)S(6)} %copy.77), kind=kOutput, calls=%fused_computation.30.clone.1 | convolution fusion | flops 814746624 | bytes 14422020 | tf_op jit(solution)/shard_map/while/body/eval_jaxpr/sub | solution.py:32
  225.0 7.1 %fusion.47 = bf16[6,512,2,128]{3,1,0,2:T(8,128)(2,1)} fusion(bf16[6,512,2,128]{3,1,0,2:T(8,128)(2,1)} %get-tuple-element.119, s32[]{:T(128)S(6)} %copy.77, bf16[3072,2,128]{2,0,1:T(8,128)(2,1)S(1)} %get-tuple-element.128, f32[2,512,3072]{2,1,0:T(8,128)} %get-tuple-element.110, f32[2,512]{1,0:T(2,128)S(1)} %get-tuple-element.111), kind=kOutput, calls=%fused_computation.10.clone.1 | convolution fusion | flops 811728896 | bytes 14422020 | tf_op jit(solution)/shard_map/while/body/eval_jaxpr/hqk,khd->qhd/dot_general | solution.py:34
  232.1 4.8 %copy.57 = bf16[3072,1,2,128]{3,2,1,0:T(2,128)(2,1)} copy(bf16[3072,1,2,128]{3,0,2,1:T(8,128)(2,1)} %bitcast.68) | data formatting | bytes 3145728 | tf_op jit(solution)/shard_map/broadcast_in_dim;reshape | solution.py:43
  236.9 18.9 %all-to-all-start.3 = ((bf16[3072,1,2,128]{3,2,1,0:T(2,128)(2,1)}), bf16[3072,1,2,128]{3,2,1,0:T(2,128)(2,1)S(1)}, u32[]{:S(2)}, u32[]{:S(2)}) async-start(bf16[3072,1,2,128]{3,2,1,0:T(2,128)(2,1)} %copy.57), calls=%async_computation.3 | async-start | bytes 3145728 | tf_op jit(solution)/shard_map/all_to_all | solution.py:61
  256.5 0.9 dynamic-slice_add_fusion
  257.4 23.8 %all-to-all-done.3 = bf16[3072,1,2,128]{3,2,1,0:T(2,128)(2,1)S(1)} async-done(((bf16[3072,1,2,128]{3,2,1,0:T(2,128)(2,1)}), bf16[3072,1,2,128]{3,2,1,0:T(2,128)(2,1)S(1)}, u32[]{:S(2)}, u32[]{:S(2)}) %all-to-all-start.3) | async-done | bytes 1572896 | tf_op jit(solution)/shard_map/all_to_all | solution.py:61
  281.2 0.2 copy_convert_fusion
  281.4 4.1 %copy.59 = f32[192,16,1,2,128]{4,3,1,2,0:T(2,128)} copy(f32[192,16,1,2,128]{4,0,1,3,2:T(8,128)S(1)} %bitcast.63) | data formatting | bytes 6291456 | tf_op jit(solution)/shard_map/convert_element_type | solution.py:62
  285.5 0.5 multiply_reduce_fusion.1
  286.0 0.1 reduce_sum.26
  286.1 0.0 copy-start
  286.1 4.4 %fusion.29 = bf16[1,192,4096]{2,1,0:T(8,128)(2,1)S(1)} fusion(f32[1,192,4096]{2,0,1:T(1,128)} %bitcast.64, f32[4096]{0:T(1024)S(1)} %bitcast.70, f32[4096]{0:T(1024)S(1)} %bitcast.69, f32[192]{0:T(256)S(1)} %add_rsqrt_fusion), kind=kLoop, calls=%fused_computation.22 | loop fusion | flops 3145728 | bytes 4752128 | tf_op jit(solution)/shard_map/convert_element_type | solution.py:65
  290.5 0.0 copy-done
  290.5 0.0 copy-start.1
  290.5 0.5 subtract_convert_fusion
  291.0 28.3 %collective-permute-start = (bf16[1,192,4096]{2,1,0:T(8,128)(2,1)S(1)}, bf16[1,192,4096]{2,1,0:T(8,128)(2,1)}, u32[]{:S(2)}, u32[]{:S(2)}) collective-permute-start(bf16[1,192,4096]{2,1,0:T(8,128)(2,1)S(1)} %subtract_convert_fusion), channel_id=1, source_target_pairs={{0,16},{16,32},{32,48},{48,64},{64,80},{80,96},{96,112},{112,128},... | collective-permute-start | bytes 4718600 | tf_op jit(solution)/shard_map/ppermute | solution.py:16
  319.3 31.8 %collective-permute-done = bf16[1,192,4096]{2,1,0:T(8,128)(2,1)} collective-permute-done((bf16[1,192,4096]{2,1,0:T(8,128)(2,1)S(1)}, bf16[1,192,4096]{2,1,0:T(8,128)(2,1)}, u32[]{:S(2)}, u32[]{:S(2)}) %collective-permute-start) | collective-permute-done | bytes 1572896 | tf_op jit(solution)/shard_map/ppermute | solution.py:16
  351.1 0.0 copy-done.1
  351.1 1.3 bitcast_select_fusion
  (3 shorter events, 0.0 us)
Async XLA Ops:
  5.5 41.2 %all-to-all-start = ((bf16[192,16,2,128]{3,2,0,1:T(2,128)(2,1)}), bf16[192,16,2,128]{3,2,0,1:T(2,128)(2,1)S(1)}, u32[]{:S(2)}, u32[]{:S(2)}) async-start(bf16[192,16,2,128]{3,2,0,1:T(2,128)(2,1)} %copy.49), calls=%async_computation | async-start | bytes 3145728 | tf_op jit(solution)/shard_map/all_to_all | solution.py:56
  46.7 40.1 %all-to-all-start.1 = ((bf16[192,16,2,128]{3,0,2,1:T(8,128)(2,1)}), bf16[192,16,2,128]{3,0,2,1:T(8,128)(2,1)S(1)}, u32[]{:S(2)}, u32[]{:S(2)}) async-start(bf16[192,16,2,128]{3,0,2,1:T(8,128)(2,1)} %copy.51), calls=%async_computation.1 | async-start | bytes 3145728 | tf_op jit(solution)/shard_map/all_to_all | solution.py:57
  86.8 44.3 %all-to-all-start.2 = ((bf16[192,16,2,128]{3,0,2,1:T(8,128)(2,1)}), bf16[192,16,2,128]{3,0,2,1:T(8,128)(2,1)}, u32[]{:S(2)}, u32[]{:S(2)}) async-start(bf16[192,16,2,128]{3,0,2,1:T(8,128)(2,1)} %copy.53), calls=%async_computation.2 | async-start | bytes 3145728 | tf_op jit(solution)/shard_map/all_to_all | solution.py:58
  236.9 44.2 %all-to-all-start.3 = ((bf16[3072,1,2,128]{3,2,1,0:T(2,128)(2,1)}), bf16[3072,1,2,128]{3,2,1,0:T(2,128)(2,1)S(1)}, u32[]{:S(2)}, u32[]{:S(2)}) async-start(bf16[3072,1,2,128]{3,2,1,0:T(2,128)(2,1)} %copy.57), calls=%async_computation.3 | async-start | bytes 3145728 | tf_op jit(solution)/shard_map/all_to_all | solution.py:61
  286.1 4.4 %copy-start = (bf16[1,192,4096]{2,1,0:T(8,128)(2,1)S(1)}, bf16[1,192,4096]{2,1,0:T(8,128)(2,1)}, u32[]{:S(2)}) copy-start(bf16[1,192,4096]{2,1,0:T(8,128)(2,1)} %param.9) | copy-start | bytes 4718596
  290.5 60.6 %copy-start.1 = (bf16[192,4096]{1,0:T(8,128)(2,1)S(1)}, bf16[192,4096]{1,0:T(8,128)(2,1)}, u32[]{:S(2)}) copy-start(bf16[192,4096]{1,0:T(8,128)(2,1)} %param.15) | copy-start | bytes 4718596
  291.0 60.0 %collective-permute-start = (bf16[1,192,4096]{2,1,0:T(8,128)(2,1)S(1)}, bf16[1,192,4096]{2,1,0:T(8,128)(2,1)}, u32[]{:S(2)}, u32[]{:S(2)}) collective-permute-start(bf16[1,192,4096]{2,1,0:T(8,128)(2,1)S(1)} %subtract_convert_fusion), channel_id=1, source_target_pairs={{0,16},{16,32},{32,48},{48,64},{64,80},{80,96},{96,112},{112,128},... | collective-permute-start | bytes 4718600 | tf_op jit(solution)/shard_map/ppermute | solution.py:16
where the time goes:
time: 357 us; the launch traced here: 352 us
  waiting for transfers between devices  122 us (34%)
  matrix products  99.5 us (28%)
  starting transfers between devices  93.1 us (26%)
  local copies, waits for them, and re-layouts  29.2 us (8%)
  other arithmetic  7.83 us (2%)
    sub x6, matrix products, one_block(): powers = jnp.exp(scores - largest)  56.8 us
    dot_general x6, matrix products, one_block(): jnp.einsum('hqk,khd->qhd', weights, values, preferred_element_type=jnp.fl...  42.7 us
    ppermute x1, waiting for transfers between devices, shifted_2(): lax.ppermute(value, axis, [(source, source + steps) for source in range(l...  31.8 us
    ppermute x1, starting transfers between devices, shifted_2(): lax.ppermute(value, axis, [(source, source + steps) for source in range(l...  28.3 us
    all_to_all x1, waiting for transfers between devices, velocity_of(): lax.all_to_all(arranged[0], 'seq', split_axis=1, concat_axis=0, tiled=True)  24.1 us
    all_to_all x1, waiting for transfers between devices, velocity_of(): lax.all_to_all(headwise, 'seq', split_axis=0, concat_axis=1, tiled=True)  23.8 us
    all_to_all x1, waiting for transfers between devices, velocity_of(): lax.all_to_all(arranged[2], 'seq', split_axis=1, concat_axis=0, tiled=True)  23.8 us
    all_to_all x1, starting transfers between devices, velocity_of(): lax.all_to_all(headwise, 'seq', split_axis=0, concat_axis=1, tiled=True)  18.9 us
  transfers between devices with their start and end apart: 5, of which 5 were waited for; matrix products, arithmetic and copies ran while one was open for 4% of the time, Pallas kernels for 0%

commit v1 on v0

v1 whole, which is shorter than its diff:
```python
import functools
import math

import jax
import jax.numpy as jnp
from jax import lax
from jax.experimental import pallas as pl
from jax.experimental.pallas import tpu as pltpu
from jax.sharding import PartitionSpec as P

HEADS = 32
HEAD_DIM = 128
STEPS = 50
HALF = 8
WIDE = 256
ROWS = 192
FEATURES = HEADS * HEAD_DIM
EXPONENT = HEAD_DIM ** (-0.5) * math.log2(math.e)
GROUPS8 = [[half * HALF + k for k in range(HALF)] for half in range(2)]
NT = (((1,), (1,)), ((), ()))
PARAMS = pltpu.CompilerParams(vmem_limit_bytes=40 << 20)


def arrange(parts, half, first, rows, name):
    count = len(parts)

    def body(half_ref, *refs):
        out = refs[count]
        for i in range(count):
            out[0, :, i * WIDE : (i + 1) * WIDE] = refs[i][...]

    return pl.pallas_call(
        body,
        grid_spec=pltpu.PrefetchScalarGridSpec(
            num_scalar_prefetch=1,
            grid=(HALF,),
            in_specs=[
                pl.BlockSpec((rows, WIDE), lambda d, half_ref: (first, half_ref[0] * HALF + d))
            ]
            * count,
            out_specs=pl.BlockSpec((1, rows, count * WIDE), lambda d, half_ref: (d, 0, 0)),
        ),
        out_shape=jax.ShapeDtypeStruct((HALF, rows, count * WIDE), jnp.bfloat16),
        compiler_params=PARAMS,
        cost_estimate=pl.CostEstimate(
            flops=0, bytes_accessed=HALF * rows * count * WIDE * 4, transcendentals=0
        ),
        name=name,
    )(half, *parts)


def attend_body(chunk, q_ref, kl_ref, kr_ref, vl_ref, vr_ref, o_ref, s_ref):
    queries = q_ref[...]
    side = kl_ref.shape[0]
    largest = None
    for i, keys in enumerate((kl_ref, kr_ref)):
        for at in range(0, side, chunk):
            scores = lax.dot_general(
                queries, keys[at : at + chunk, :], NT, preferred_element_type=jnp.float32
            )
            s_ref[:, i * side + at : i * side + at + chunk] = scores
            for j in range(0, chunk, 128):
                part = scores[:, j : j + 128]
                largest = part if largest is None else jnp.maximum(largest, part)
    shift = jnp.max(largest, axis=1, keepdims=True) * EXPONENT
    total = None
    mixed = None
    for i, values in enumerate((vl_ref, vr_ref)):
        for at in range(0, side, chunk):
            powers = jnp.exp2(
                s_ref[:, i * side + at : i * side + at + chunk] * EXPONENT - shift
            )
            for j in range(0, chunk, 128):
                part = powers[:, j : j + 128]
                total = part if total is None else total + part
            product = jnp.dot(
                powers.astype(jnp.bfloat16),
                values[at : at + chunk, :],
                preferred_element_type=jnp.float32,
            )
            mixed = product if mixed is None else mixed + product
    o_ref[...] = (mixed / jnp.sum(total, axis=1, keepdims=True)).astype(jnp.bfloat16)


def attend(queries, local, remote_keys, remote_values, name):
    rows = queries.shape[0]
    side = remote_keys.shape[0]
    tile = 256
    return pl.pallas_call(
        functools.partial(attend_body, 512),
        grid=(2, rows // tile),
        in_specs=[
            pl.BlockSpec((tile, HEAD_DIM), lambda h, i: (i, h)),
            pl.BlockSpec((side, HEAD_DIM), lambda h, i: (0, h)),
            pl.BlockSpec((side, HEAD_DIM), lambda h, i: (0, h)),
            pl.BlockSpec((side, HEAD_DIM), lambda h, i: (0, 2 + h)),
            pl.BlockSpec((side, HEAD_DIM), lambda h, i: (0, h)),
        ],
        out_specs=pl.BlockSpec((tile, HEAD_DIM), lambda h, i: (i, h)),
        out_shape=jax.ShapeDtypeStruct((rows, WIDE), jnp.bfloat16),
        scratch_shapes=[pltpu.VMEM((tile, 2 * side), jnp.float32)],
        compiler_params=PARAMS,
        cost_estimate=pl.CostEstimate(
            flops=rows * 2 * side * WIDE * 4 * 3,
            bytes_accessed=6 * side * WIDE * 2,
            transcendentals=rows * 2 * side * 2,
        ),
        name=name,
    )(queries, local, remote_keys, local, remote_values)


def update_body(meta, near_ref, far_ref, latent_ref, mod_ref, fresh_ref, o_ref):
    half = meta[0]
    step_size = (meta[1] + 1).astype(jnp.float32) / STEPS
    squares = None
    for ref in (near_ref, far_ref):
        for d in range(HALF):
            part = ref[d].astype(jnp.float32)
            squares = part * part if squares is None else squares + part * part
    meansq = jnp.sum(squares, axis=1, keepdims=True) / FEATURES
    inverse = lax.rsqrt(meansq + 1e-06)
    for side, ref in enumerate((near_ref, far_ref)):
        start = (half if side == 0 else 1 - half) * (HALF * WIDE)
        for d in range(HALF):
            at = pl.ds(pl.multiple_of(start + d * WIDE, WIDE), WIDE)
            velocity = (
                ref[d].astype(jnp.float32) * inverse * (1.0 + mod_ref[0, 0:1, at])
                + mod_ref[0, 1:2, at]
            ).astype(jnp.bfloat16)
            o_ref[:, at] = (
                latent_ref[:, at].astype(jnp.float32) - step_size * velocity.astype(jnp.float32)
            ).astype(jnp.bfloat16)

    @pl.when(meta[2] == 1)
    def _():
        o_ref[...] = fresh_ref[...]


def update(meta, near, far, latent, mod_table, fresh, first, rows, name):
    tile = 48
    steps = rows // tile
    return pl.pallas_call(
        update_body,
        grid_spec=pltpu.PrefetchScalarGridSpec(
            num_scalar_prefetch=1,
            grid=(steps,),
            in_specs=[
                pl.BlockSpec((HALF, tile, WIDE), lambda i, m: (0, first * steps + i, 0)),
                pl.BlockSpec((HALF, tile, WIDE), lambda i, m: (0, i, 0)),
                pl.BlockSpec((tile, FEATURES), lambda i, m: (first * steps + i, 0)),
                pl.BlockSpec((1, 2, FEATURES), lambda i, m: (m[1], 0, 0)),
                pl.BlockSpec((tile, FEATURES), lambda i, m: (first * steps + i, 0)),
            ],
            out_specs=pl.BlockSpec((tile, FEATURES), lambda i, m: (i, 0)),
        ),
        out_shape=jax.ShapeDtypeStruct((rows, FEATURES), jnp.bfloat16),
        compiler_params=PARAMS,
        cost_estimate=pl.CostEstimate(
            flops=rows * FEATURES * 10, bytes_accessed=rows * FEATURES * 10, transcendentals=0
        ),
        name=name,
    )(meta, near, far, latent, mod_table, fresh)


def across(value):
    return lax.ppermute(value, "seq", [(s, (s + HALF) % (2 * HALF)) for s in range(2 * HALF)])


def within(value):
    return lax.all_to_all(value, "seq", 0, 0, axis_index_groups=GROUPS8)


def on_device(latent, queries, key_rows, values, mod_table, levels, fresh_noise):
    latent, queries, key_rows, values = (x[0] for x in (latent, queries, key_rows, values))
    half = lax.axis_index("seq") // HALF
    near = half.reshape(1)
    far = (1 - half).reshape(1)
    count = lax.axis_size("queue")
    group = lax.axis_index("queue")
    meta = jnp.stack([half, levels[0], (group == count - 1).astype(jnp.int32)])
    part = ROWS // 2

    far_keys = across(arrange([key_rows], far, 0, ROWS, "far_keys"))
    far_values = across(arrange([values], far, 0, ROWS, "far_values"))
    far_queries = [
        across(arrange([queries], far, i, part, f"far_queries{i}")) for i in range(2)
    ]
    local = within(arrange([key_rows, values], near, 0, ROWS, "near_keys_values"))
    local_queries = within(arrange([queries], near, 0, ROWS, "near_queries"))

    flat = lambda x: x.reshape(-1, x.shape[2])
    local = flat(local)
    far_keys = flat(within(far_keys))
    far_values = flat(within(far_values))
    mixed_near = attend(flat(local_queries), local, far_keys, far_values, "attend_near")
    mixed_near = within(mixed_near.reshape(HALF, ROWS, WIDE))
    shifted = []
    ring = [(g, (g + 1) % count) for g in range(count)]
    for i in range(2):
        rows = flat(within(far_queries[i]))
        mixed = attend(rows, local, far_keys, far_values, f"attend_far{i}")
        mixed = across(within(mixed.reshape(HALF, part, WIDE)))
        denoised = update(
            meta, mixed_near, mixed, latent, mod_table, fresh_noise, i, part, f"update{i}"
        )
        shifted.append(lax.ppermute(denoised, "queue", ring))
    return jnp.concatenate(shifted)[None]


def solution(mesh):
    return jax.shard_map(
        on_device,
        mesh=mesh,
        in_specs=(
            P("queue", "seq", None),
            P("queue", "seq", None),
            P("queue", "seq", None),
            P("queue", "seq", None),
            P(),
            P("queue"),
            P("seq", None),
        ),
        out_specs=P("queue", "seq", None),
        check_vma=False,
    )
```

time: 357 us -> 299 us (0.84)
  matrix products: 99.5 us -> 0 us
  Pallas kernels: 0 us -> 49.9 us
  starting transfers between devices: 93.1 us -> 136 us
  waiting for transfers between devices: 122 us -> 99.6 us
  local copies, waits for them, and re-layouts: 29.2 us -> 9.55 us
  other arithmetic: 7.83 us -> 1.37 us
    all_to_all x4 -> x9, waiting for transfers between devices: 90.2 us -> 4.95 us  [within(): return lax.all_to_all(value, 'seq', 0, 0, axis_index_groups=GROUPS8)]
    ppermute x1 -> x8, waiting for transfers between devices: 31.8 us -> 94.6 us  [the longest x6 60.2 us: across(): lax.ppermute(value, 'seq', [(s, (s + HALF) % (2 * HALF)) for s in range(2...]
    ppermute x1 -> x8, starting transfers between devices: 28.3 us -> 88 us  [the longest x6 68.3 us: across(): lax.ppermute(value, 'seq', [(s, (s + HALF) % (2 * HALF)) for s in range(2...]
    sub x6 -> x0, matrix products: 56.8 us -> none  [one_block(): powers = jnp.exp(scores - largest)]
    pallas_call x0 -> x11, Pallas kernels: none -> 49.9 us  [the longest x3 42.5 us: attend(): pl.pallas_call(functools.partial(attend_body, 512), grid=(2, rows // tile...]
    dot_general x6 -> x0, matrix products: 42.7 us -> none  [one_block(): jnp.einsum('hqk,khd->qhd', weights, values, preferred_element_type=jnp.fl...]
    another operation x7 -> x0, local copies, waits for them, and re-layouts: 21.9 us -> none  [the longest x6 17.1 us: velocity_of(): part[0].reshape(local_rows, devices, per_device, HEAD_DIM)]
    all_to_all x4 -> x9, starting transfers between devices: 64.8 us -> 48.3 us  [within(): return lax.all_to_all(value, 'seq', 0, 0, axis_index_groups=GROUPS8)]
  transfers between devices with their start and end apart: 5 -> 17, of which waited for: 5 -> 8; matrix products, arithmetic and copies ran while one was open for 4% -> 0% of each run, Pallas kernels for 0% -> 16%
where the time goes in v1:
time: 299 us; the launch traced here: 298 us
  starting transfers between devices  136 us (45%)
  waiting for transfers between devices  99.6 us (33%)
  Pallas kernels  49.9 us (17%)
  local copies, waits for them, and re-layouts  9.55 us (3%)
    ppermute x6, starting transfers between devices, across(): lax.ppermute(value, 'seq', [(s, (s + HALF) % (2 * HALF)) for s in range(2...  68.3 us
    ppermute x6, waiting for transfers between devices, across(): lax.ppermute(value, 'seq', [(s, (s + HALF) % (2 * HALF)) for s in range(2...  60.2 us
    all_to_all x9, starting transfers between devices, within(): return lax.all_to_all(value, 'seq', 0, 0, axis_index_groups=GROUPS8)  48.3 us
    pallas_call x3, Pallas kernels, attend(): pl.pallas_call(functools.partial(attend_body, 512), grid=(2, rows // tile...  42.5 us
    ppermute x2, waiting for transfers between devices, on_device(): shifted.append(lax.ppermute(denoised, 'queue', ring))  34.5 us
    ppermute x2, starting transfers between devices, on_device(): shifted.append(lax.ppermute(denoised, 'queue', ring))  19.7 us
    unnamed x26, local copies, waits for them, and re-layouts  9.55 us
  transfers between devices with their start and end apart: 17, of which 8 were waited for; matrix products, arithmetic and copies ran while one was open for 0% of the time, Pallas kernels for 16%

profile of v1, /device:TPU:1, one launch (start us, length us, event | category | flops | bytes accessed | tf_op | source)
XLA Modules:
  0.0 297.6 jit_solution(13384025778835222518)
XLA Ops:
  0.0 1.4 copy-done
  1.4 2.7 near_queries.1
  4.1 7.3 %all-to-all-start = ((bf16[8,192,256]{2,1,0:T(8,128)(2,1)}), bf16[8,192,256]{2,1,0:T(8,128)(2,1)}, u32[]{:S(2)}, u32[]{:S(2)}) async-start(bf16[8,192,256]{2,1,0:T(8,128)(2,1)} %near_queries.1), calls=%async_computation | async-start | bytes 1572864 | tf_op jit(solution)/shard_map/all_to_all | solution.py:170
  11.5 0.3 far_queries0.1
  11.8 5.5 %collective-permute-start.2 = (bf16[8,96,256]{2,1,0:T(8,128)(2,1)S(1)}, bf16[8,96,256]{2,1,0:T(8,128)(2,1)}, u32[]{:S(2)}, u32[]{:S(2)}) collective-permute-start(bf16[8,96,256]{2,1,0:T(8,128)(2,1)S(1)} %far_queries0.1), channel_id=1, source_target_pairs={{0,8},{1,9},{2,10},{3,11},{4,12},{5,13},{6,14},{7,15},{8,0},{9,1},... | collective-permute-start | bytes 1179656 | tf_op jit(solution)/shard_map/ppermute | solution.py:166
  17.2 10.3 %collective-permute-done.2 = bf16[8,96,256]{2,1,0:T(8,128)(2,1)} collective-permute-done((bf16[8,96,256]{2,1,0:T(8,128)(2,1)S(1)}, bf16[8,96,256]{2,1,0:T(8,128)(2,1)}, u32[]{:S(2)}, u32[]{:S(2)}) %collective-permute-start.2) | collective-permute-done | bytes 393248 | tf_op jit(solution)/shard_map/ppermute | solution.py:166
  27.5 5.5 %all-to-all-start.5 = ((bf16[8,96,256]{2,1,0:T(8,128)(2,1)}), bf16[8,96,256]{2,1,0:T(8,128)(2,1)S(1)}, u32[]{:S(2)}, u32[]{:S(2)}) async-start(bf16[8,96,256]{2,1,0:T(8,128)(2,1)} %collective-permute-done.2), calls=%async_computation.5 | async-start | bytes 786432 | tf_op jit(solution)/shard_map/all_to_all | solution.py:170
  33.0 1.4 copy-done.4
  34.4 0.6 near_keys_values.1
  35.0 0.0 copy-start.6
  35.0 1.1 copy-done.6
  36.1 4.9 %all-to-all-done.5 = bf16[8,96,256]{2,1,0:T(8,128)(2,1)S(1)} async-done(((bf16[8,96,256]{2,1,0:T(8,128)(2,1)}), bf16[8,96,256]{2,1,0:T(8,128)(2,1)S(1)}, u32[]{:S(2)}, u32[]{:S(2)}) %all-to-all-start.5) | async-done | bytes 393248 | tf_op jit(solution)/shard_map/all_to_all | solution.py:170
  41.1 5.0 %all-to-all-start.1 = ((bf16[8,192,512]{2,1,0:T(8,128)(2,1)}), bf16[8,192,512]{2,1,0:T(8,128)(2,1)}, u32[]{:S(2)}, u32[]{:S(2)}) async-start(bf16[8,192,512]{2,1,0:T(8,128)(2,1)} %copy-done.6), calls=%async_computation.1 | async-start | bytes 3145728 | tf_op jit(solution)/shard_map/all_to_all | solution.py:170
  46.1 0.4 far_keys.1
  46.5 12.1 %collective-permute-start = (bf16[8,192,256]{2,1,0:T(8,128)(2,1)S(1)}, bf16[8,192,256]{2,1,0:T(8,128)(2,1)}, u32[]{:S(2)}, u32[]{:S(2)}) collective-permute-start(bf16[8,192,256]{2,1,0:T(8,128)(2,1)S(1)} %far_keys.1), channel_id=1, source_target_pairs={{0,8},{1,9},{2,10},{3,11},{4,12},{5,13},{6,14},{7,15},{8,0},{9,1},... | collective-permute-start | bytes 2359304 | tf_op jit(solution)/shard_map/ppermute | solution.py:166
  58.6 0.4 far_values.1
  59.0 1.0 collective-permute-start.1
  60.0 17.7 %collective-permute-done = bf16[8,192,256]{2,1,0:T(8,128)(2,1)} collective-permute-done((bf16[8,192,256]{2,1,0:T(8,128)(2,1)S(1)}, bf16[8,192,256]{2,1,0:T(8,128)(2,1)}, u32[]{:S(2)}, u32[]{:S(2)}) %collective-permute-start) | collective-permute-done | bytes 786464 | tf_op jit(solution)/shard_map/ppermute | solution.py:166
  77.7 5.7 %all-to-all-start.2 = ((bf16[8,192,256]{2,1,0:T(8,128)(2,1)}), bf16[8,192,256]{2,1,0:T(8,128)(2,1)S(1)}, u32[]{:S(2)}, u32[]{:S(2)}) async-start(bf16[8,192,256]{2,1,0:T(8,128)(2,1)} %collective-permute-done), calls=%async_computation.2 | async-start | bytes 1572864 | tf_op jit(solution)/shard_map/all_to_all | solution.py:170
  83.4 12.7 %collective-permute-done.1 = bf16[8,192,256]{2,1,0:T(8,128)(2,1)} collective-permute-done((bf16[8,192,256]{2,1,0:T(8,128)(2,1)S(1)}, bf16[8,192,256]{2,1,0:T(8,128)(2,1)}, u32[]{:S(2)}, u32[]{:S(2)}) %collective-permute-start.1) | collective-permute-done | bytes 786464 | tf_op jit(solution)/shard_map/ppermute | solution.py:166
  96.0 5.2 %all-to-all-start.3 = ((bf16[8,192,256]{2,1,0:T(8,128)(2,1)}), bf16[8,192,256]{2,1,0:T(8,128)(2,1)S(1)}, u32[]{:S(2)}, u32[]{:S(2)}) async-start(bf16[8,192,256]{2,1,0:T(8,128)(2,1)} %collective-permute-done.1), calls=%async_computation.3 | async-start | bytes 1572864 | tf_op jit(solution)/shard_map/all_to_all | solution.py:170
  101.3 0.3 far_queries1.1
  101.6 36.4 %collective-permute-start.5 = (bf16[8,96,256]{2,1,0:T(8,128)(2,1)S(1)}, bf16[8,96,256]{2,1,0:T(8,128)(2,1)}, u32[]{:S(2)}, u32[]{:S(2)}) collective-permute-start(bf16[8,96,256]{2,1,0:T(8,128)(2,1)S(1)} %far_queries1.1), channel_id=1, source_target_pairs={{0,8},{1,9},{2,10},{3,11},{4,12},{5,13},{6,14},{7,15},{8,0},{9,1},... | collective-permute-start | bytes 1179656 | tf_op jit(solution)/shard_map/ppermute | solution.py:166
  138.0 10.0 %collective-permute-done.5 = bf16[8,96,256]{2,1,0:T(8,128)(2,1)} collective-permute-done((bf16[8,96,256]{2,1,0:T(8,128)(2,1)S(1)}, bf16[8,96,256]{2,1,0:T(8,128)(2,1)}, u32[]{:S(2)}, u32[]{:S(2)}) %collective-permute-start.5) | collective-permute-done | bytes 393248 | tf_op jit(solution)/shard_map/ppermute | solution.py:166
  148.0 5.1 %all-to-all-start.7 = ((bf16[8,96,256]{2,1,0:T(8,128)(2,1)}), bf16[8,96,256]{2,1,0:T(8,128)(2,1)S(1)}, u32[]{:S(2)}, u32[]{:S(2)}) async-start(bf16[8,96,256]{2,1,0:T(8,128)(2,1)} %collective-permute-done.5), calls=%async_computation.7 | async-start | bytes 786432 | tf_op jit(solution)/shard_map/all_to_all | solution.py:170
  153.1 11.2 %attend_far0.1 = bf16[768,256]{1,0:T(8,128)(2,1)} custom-call(bf16[768,256]{1,0:T(8,128)(2,1)S(1)} %bitcast.34, bf16[1536,512]{1,0:T(8,128)(2,1)} %bitcast.6.kl_ref.vl_ref, bf16[1536,256]{1,0:T(8,128)(2,1)S(1)} %bitcast.27, bf16[1536,512]{1,0:T(8,128)(2,1)} %bitcast.6.kl_ref.vl_ref, bf16[1536,256]{1,0:T(8,128)(2,1)S(1)} %bitcast.30), custom_call_target="tpu_custom_call" | custom-call | flops 7247757312 | bytes 4718592 | tf_op jit(solution)/shard_map/attend_far0/pallas_call | solution.py:89
  164.3 4.8 %all-to-all-start.6 = ((bf16[8,96,256]{2,1,0:T(8,128)(2,1)}), bf16[8,96,256]{2,1,0:T(8,128)(2,1)}, u32[]{:S(2)}, u32[]{:S(2)}) async-start(bf16[8,96,256]{2,1,0:T(8,128)(2,1)} %bitcast.12), calls=%async_computation.6 | async-start | bytes 786432 | tf_op jit(solution)/shard_map/all_to_all | solution.py:170
  169.1 11.2 %attend_far1.1 = bf16[768,256]{1,0:T(8,128)(2,1)} custom-call(bf16[768,256]{1,0:T(8,128)(2,1)S(1)} %bitcast.35, bf16[1536,512]{1,0:T(8,128)(2,1)} %bitcast.6.kl_ref.vl_ref, bf16[1536,256]{1,0:T(8,128)(2,1)S(1)} %bitcast.28, bf16[1536,512]{1,0:T(8,128)(2,1)} %bitcast.6.kl_ref.vl_ref, bf16[1536,256]{1,0:T(8,128)(2,1)S(1)} %bitcast.31), custom_call_target="tpu_custom_call" | custom-call | flops 7247757312 | bytes 4718592 | tf_op jit(solution)/shard_map/attend_far1/pallas_call | solution.py:89
  180.3 4.8 %all-to-all-start.8 = ((bf16[8,96,256]{2,1,0:T(8,128)(2,1)}), bf16[8,96,256]{2,1,0:T(8,128)(2,1)S(1)}, u32[]{:S(2)}, u32[]{:S(2)}) async-start(bf16[8,96,256]{2,1,0:T(8,128)(2,1)} %bitcast.15), calls=%async_computation.8 | async-start | bytes 786432 | tf_op jit(solution)/shard_map/all_to_all | solution.py:170
  185.1 1.1 copy-done.10
  186.2 20.0 %attend_near.1 = bf16[1536,256]{1,0:T(8,128)(2,1)S(1)} custom-call(bf16[1536,256]{1,0:T(8,128)(2,1)} %bitcast.3.q_ref, bf16[1536,512]{1,0:T(8,128)(2,1)} %bitcast.6.kl_ref.vl_ref, bf16[1536,256]{1,0:T(8,128)(2,1)S(1)} %bitcast.29, bf16[1536,512]{1,0:T(8,128)(2,1)} %bitcast.6.kl_ref.vl_ref, bf16[1536,256]{1,0:T(8,128)(2,1)S(1)} %bitcast.32), custom_call_target="tpu_custom_call" | custom-call | flops 14495514624 | bytes 4718592 | tf_op jit(solution)/shard_map/attend_near/pallas_call | solution.py:89
  206.3 0.0 copy-start.11
  206.3 0.9 copy-done.11
  207.2 0.8 copy-done.12
  207.9 4.8 %all-to-all-start.4 = ((bf16[8,192,256]{2,1,0:T(8,128)(2,1)}), bf16[8,192,256]{2,1,0:T(8,128)(2,1)S(1)}, u32[]{:S(2)}, u32[]{:S(2)}) async-start(bf16[8,192,256]{2,1,0:T(8,128)(2,1)} %bitcast.33), calls=%async_computation.4 | async-start | bytes 1572864 | tf_op jit(solution)/shard_map/all_to_all | solution.py:170
  212.7 13.3 %collective-permute-start.3 = (bf16[8,96,256]{2,1,0:T(8,128)(2,1)}, bf16[8,96,256]{2,1,0:T(8,128)(2,1)S(1)}, u32[]{:S(2)}, u32[]{:S(2)}) collective-permute-start(bf16[8,96,256]{2,1,0:T(8,128)(2,1)} %all-to-all-done.6), channel_id=1, source_target_pairs={{0,8},{1,9},{2,10},{3,11},{4,12},{5,13},{6,14},{7,15},{8,0},{9,1},... | collective-permute-start | bytes 1179656 | tf_op jit(solution)/shard_map/ppermute | solution.py:166
  226.1 0.0 collective-permute-start.6
  226.7 0.1 pad_add_fusion.meta
  226.8 9.6 %collective-permute-done.3.far_ref = bf16[8,96,256]{2,1,0:T(8,128)(2,1)S(1)} collective-permute-done((bf16[8,96,256]{2,1,0:T(8,128)(2,1)}, bf16[8,96,256]{2,1,0:T(8,128)(2,1)S(1)}, u32[]{:S(2)}, u32[]{:S(2)}) %collective-permute-start.3) | collective-permute-done | bytes 393248 | tf_op jit(solution)/shard_map/ppermute | solution.py:166
  236.4 1.4 copy-done.7
  237.8 1.4 copy-done.8
  239.2 1.4 update0.1
  240.6 15.5 %collective-permute-start.4 = (bf16[96,4096]{1,0:T(8,128)(2,1)S(1)}, bf16[96,4096]{1,0:T(8,128)(2,1)S(1)}, u32[]{:S(2)}, u32[]{:S(2)}) collective-permute-start(bf16[96,4096]{1,0:T(8,128)(2,1)S(1)} %update0.1), channel_id=1, source_target_pairs={{0,16},{16,32},{32,48},{48,64},{64,80},{80,96},{96,112},{112,128},... | collective-permute-start | bytes 2359304 | tf_op jit(solution)/shard_map/ppermute | solution.py:206
  256.1 1.4 update1.1
  257.5 4.2 %collective-permute-start.7 = (bf16[96,4096]{1,0:T(8,128)(2,1)S(1)}, bf16[96,4096]{1,0:T(8,128)(2,1)S(1)}, u32[]{:S(2)}, u32[]{:S(2)}) collective-permute-start(bf16[96,4096]{1,0:T(8,128)(2,1)S(1)} %update1.1), channel_id=1, source_target_pairs={{0,16},{16,32},{32,48},{48,64},{64,80},{80,96},{96,112},{112,128},... | collective-permute-start | bytes 2359304 | tf_op jit(solution)/shard_map/ppermute | solution.py:206
  261.8 17.6 %collective-permute-done.4 = bf16[96,4096]{1,0:T(8,128)(2,1)S(1)} collective-permute-done((bf16[96,4096]{1,0:T(8,128)(2,1)S(1)}, bf16[96,4096]{1,0:T(8,128)(2,1)S(1)}, u32[]{:S(2)}, u32[]{:S(2)}) %collective-permute-start.4) | collective-permute-done | bytes 786464 | tf_op jit(solution)/shard_map/ppermute | solution.py:206
  279.4 16.9 %collective-permute-done.7 = bf16[96,4096]{1,0:T(8,128)(2,1)S(1)} collective-permute-done((bf16[96,4096]{1,0:T(8,128)(2,1)S(1)}, bf16[96,4096]{1,0:T(8,128)(2,1)S(1)}, u32[]{:S(2)}, u32[]{:S(2)}) %collective-permute-start.7) | collective-permute-done | bytes 786464 | tf_op jit(solution)/shard_map/ppermute | solution.py:206
  296.3 1.3 maximum_bitcast_fusion
  (25 shorter events, 0.1 us)
Async XLA Ops:
  0.0 1.4 copy-start
  1.4 10.0 %copy-start.1 = (bf16[1,192,4096]{2,1,0:T(8,128)(2,1)S(1)}, bf16[1,192,4096]{2,1,0:T(8,128)(2,1)}, u32[]{:S(2)}) copy-start(bf16[1,192,4096]{2,1,0:T(8,128)(2,1)} %param.8) | copy-start | bytes 4718596
  4.1 23.4 %all-to-all-start = ((bf16[8,192,256]{2,1,0:T(8,128)(2,1)}), bf16[8,192,256]{2,1,0:T(8,128)(2,1)}, u32[]{:S(2)}, u32[]{:S(2)}) async-start(bf16[8,192,256]{2,1,0:T(8,128)(2,1)} %near_queries.1), calls=%async_computation | async-start | bytes 1572864 | tf_op jit(solution)/shard_map/all_to_all | solution.py:170
  11.4 21.5 %copy-start.3 = (bf16[1,192,4096]{2,1,0:T(8,128)(2,1)S(1)}, bf16[1,192,4096]{2,1,0:T(8,128)(2,1)}, u32[]{:S(2)}) copy-start(bf16[1,192,4096]{2,1,0:T(8,128)(2,1)} %param.9) | copy-start | bytes 4718596
  11.8 15.7 %collective-permute-start.2 = (bf16[8,96,256]{2,1,0:T(8,128)(2,1)S(1)}, bf16[8,96,256]{2,1,0:T(8,128)(2,1)}, u32[]{:S(2)}, u32[]{:S(2)}) collective-permute-start(bf16[8,96,256]{2,1,0:T(8,128)(2,1)S(1)} %far_queries0.1), channel_id=1, source_target_pairs={{0,8},{1,9},{2,10},{3,11},{4,12},{5,13},{6,14},{7,15},{8,0},{9,1},... | collective-permute-start | bytes 1179656 | tf_op jit(solution)/shard_map/ppermute | solution.py:166
  27.5 13.6 %all-to-all-start.5 = ((bf16[8,96,256]{2,1,0:T(8,128)(2,1)}), bf16[8,96,256]{2,1,0:T(8,128)(2,1)S(1)}, u32[]{:S(2)}, u32[]{:S(2)}) async-start(bf16[8,96,256]{2,1,0:T(8,128)(2,1)} %collective-permute-done.2), calls=%async_computation.5 | async-start | bytes 786432 | tf_op jit(solution)/shard_map/all_to_all | solution.py:170
  33.0 1.4 copy-start.4
  35.0 1.1 copy-start.6
  41.1 36.6 %all-to-all-start.1 = ((bf16[8,192,512]{2,1,0:T(8,128)(2,1)}), bf16[8,192,512]{2,1,0:T(8,128)(2,1)}, u32[]{:S(2)}, u32[]{:S(2)}) async-start(bf16[8,192,512]{2,1,0:T(8,128)(2,1)} %copy-done.6), calls=%async_computation.1 | async-start | bytes 3145728 | tf_op jit(solution)/shard_map/all_to_all | solution.py:170
  46.1 12.5 %copy-start.5 = (bf16[1,192,4096]{2,1,0:T(8,128)(2,1)S(1)}, bf16[1,192,4096]{2,1,0:T(8,128)(2,1)}, u32[]{:S(2)}) copy-start(bf16[1,192,4096]{2,1,0:T(8,128)(2,1)} %param.10) | copy-start | bytes 4718596
  46.5 31.2 %collective-permute-start = (bf16[8,192,256]{2,1,0:T(8,128)(2,1)S(1)}, bf16[8,192,256]{2,1,0:T(8,128)(2,1)}, u32[]{:S(2)}, u32[]{:S(2)}) collective-permute-start(bf16[8,192,256]{2,1,0:T(8,128)(2,1)S(1)} %far_keys.1), channel_id=1, source_target_pairs={{0,8},{1,9},{2,10},{3,11},{4,12},{5,13},{6,14},{7,15},{8,0},{9,1},... | collective-permute-start | bytes 2359304 | tf_op jit(solution)/shard_map/ppermute | solution.py:166
  59.0 37.1 %collective-permute-start.1 = (bf16[8,192,256]{2,1,0:T(8,128)(2,1)S(1)}, bf16[8,192,256]{2,1,0:T(8,128)(2,1)}, u32[]{:S(2)}, u32[]{:S(2)}) collective-permute-start(bf16[8,192,256]{2,1,0:T(8,128)(2,1)S(1)} %far_values.1), channel_id=1, source_target_pairs={{0,8},{1,9},{2,10},{3,11},{4,12},{5,13},{6,14},{7,15},{8,0},{9,1},... | collective-permute-start | bytes 2359304 | tf_op jit(solution)/shard_map/ppermute | solution.py:166
  77.7 18.4 %all-to-all-start.2 = ((bf16[8,192,256]{2,1,0:T(8,128)(2,1)}), bf16[8,192,256]{2,1,0:T(8,128)(2,1)S(1)}, u32[]{:S(2)}, u32[]{:S(2)}) async-start(bf16[8,192,256]{2,1,0:T(8,128)(2,1)} %collective-permute-done), calls=%async_computation.2 | async-start | bytes 1572864 | tf_op jit(solution)/shard_map/all_to_all | solution.py:170
  96.0 52.0 %all-to-all-start.3 = ((bf16[8,192,256]{2,1,0:T(8,128)(2,1)}), bf16[8,192,256]{2,1,0:T(8,128)(2,1)S(1)}, u32[]{:S(2)}, u32[]{:S(2)}) async-start(bf16[8,192,256]{2,1,0:T(8,128)(2,1)} %collective-permute-done.1), calls=%async_computation.3 | async-start | bytes 1572864 | tf_op jit(solution)/shard_map/all_to_all | solution.py:170
  101.6 46.4 %collective-permute-start.5 = (bf16[8,96,256]{2,1,0:T(8,128)(2,1)S(1)}, bf16[8,96,256]{2,1,0:T(8,128)(2,1)}, u32[]{:S(2)}, u32[]{:S(2)}) collective-permute-start(bf16[8,96,256]{2,1,0:T(8,128)(2,1)S(1)} %far_queries1.1), channel_id=1, source_target_pairs={{0,8},{1,9},{2,10},{3,11},{4,12},{5,13},{6,14},{7,15},{8,0},{9,1},... | collective-permute-start | bytes 1179656 | tf_op jit(solution)/shard_map/ppermute | solution.py:166
  148.0 21.1 %copy-start.9 = (bf16[8,192,256]{2,1,0:T(8,128)(2,1)}, bf16[8,192,256]{2,1,0:T(8,128)(2,1)S(1)}, u32[]{:S(2)}) copy-start(bf16[8,192,256]{2,1,0:T(8,128)(2,1)S(1)} %all-to-all-done.3) | copy-start | bytes 2359300
  148.0 16.3 %all-to-all-start.7 = ((bf16[8,96,256]{2,1,0:T(8,128)(2,1)}), bf16[8,96,256]{2,1,0:T(8,128)(2,1)S(1)}, u32[]{:S(2)}, u32[]{:S(2)}) async-start(bf16[8,96,256]{2,1,0:T(8,128)(2,1)} %collective-permute-done.5), calls=%async_computation.7 | async-start | bytes 786432 | tf_op jit(solution)/shard_map/all_to_all | solution.py:170
  164.3 16.0 %all-to-all-start.6 = ((bf16[8,96,256]{2,1,0:T(8,128)(2,1)}), bf16[8,96,256]{2,1,0:T(8,128)(2,1)}, u32[]{:S(2)}, u32[]{:S(2)}) async-start(bf16[8,96,256]{2,1,0:T(8,128)(2,1)} %bitcast.12), calls=%async_computation.6 | async-start | bytes 786432 | tf_op jit(solution)/shard_map/all_to_all | solution.py:170
  180.3 26.9 %all-to-all-start.8 = ((bf16[8,96,256]{2,1,0:T(8,128)(2,1)}), bf16[8,96,256]{2,1,0:T(8,128)(2,1)S(1)}, u32[]{:S(2)}, u32[]{:S(2)}) async-start(bf16[8,96,256]{2,1,0:T(8,128)(2,1)} %bitcast.15), calls=%async_computation.8 | async-start | bytes 786432 | tf_op jit(solution)/shard_map/all_to_all | solution.py:170
  185.1 1.1 copy-start.10
  186.2 50.1 %copy-start.2 = (f32[50,2,4096]{2,1,0:T(2,128)S(1)}, f32[50,2,4096]{2,1,0:T(2,128)}, u32[]{:S(2)}) copy-start(f32[50,2,4096]{2,1,0:T(2,128)} %mod_ref.3) | copy-start | bytes 4915204
  206.3 0.9 copy-start.11
  207.2 0.8 copy-start.12
  207.9 18.9 %all-to-all-start.4 = ((bf16[8,192,256]{2,1,0:T(8,128)(2,1)}), bf16[8,192,256]{2,1,0:T(8,128)(2,1)S(1)}, u32[]{:S(2)}, u32[]{:S(2)}) async-start(bf16[8,192,256]{2,1,0:T(8,128)(2,1)} %bitcast.33), calls=%async_computation.4 | async-start | bytes 1572864 | tf_op jit(solution)/shard_map/all_to_all | solution.py:170
  212.7 23.6 %collective-permute-start.3 = (bf16[8,96,256]{2,1,0:T(8,128)(2,1)}, bf16[8,96,256]{2,1,0:T(8,128)(2,1)S(1)}, u32[]{:S(2)}, u32[]{:S(2)}) collective-permute-start(bf16[8,96,256]{2,1,0:T(8,128)(2,1)} %all-to-all-done.6), channel_id=1, source_target_pairs={{0,8},{1,9},{2,10},{3,11},{4,12},{5,13},{6,14},{7,15},{8,0},{9,1},... | collective-permute-start | bytes 1179656 | tf_op jit(solution)/shard_map/ppermute | solution.py:166
  226.1 30.0 %collective-permute-start.6 = (bf16[8,96,256]{2,1,0:T(8,128)(2,1)}, bf16[8,96,256]{2,1,0:T(8,128)(2,1)S(1)}, u32[]{:S(2)}, u32[]{:S(2)}) collective-permute-start(bf16[8,96,256]{2,1,0:T(8,128)(2,1)} %copy-done.12), channel_id=1, source_target_pairs={{0,8},{1,9},{2,10},{3,11},{4,12},{5,13},{6,14},{7,15},{8,0},{9,1},... | collective-permute-start | bytes 1179656 | tf_op jit(solution)/shard_map/ppermute | solution.py:166
  236.4 1.4 copy-start.7
  237.8 1.4 copy-start.8
  240.6 38.8 %collective-permute-start.4 = (bf16[96,4096]{1,0:T(8,128)(2,1)S(1)}, bf16[96,4096]{1,0:T(8,128)(2,1)S(1)}, u32[]{:S(2)}, u32[]{:S(2)}) collective-permute-start(bf16[96,4096]{1,0:T(8,128)(2,1)S(1)} %update0.1), channel_id=1, source_target_pairs={{0,16},{16,32},{32,48},{48,64},{64,80},{80,96},{96,112},{112,128},... | collective-permute-start | bytes 2359304 | tf_op jit(solution)/shard_map/ppermute | solution.py:206
  257.5 38.7 %collective-permute-start.7 = (bf16[96,4096]{1,0:T(8,128)(2,1)S(1)}, bf16[96,4096]{1,0:T(8,128)(2,1)S(1)}, u32[]{:S(2)}, u32[]{:S(2)}) collective-permute-start(bf16[96,4096]{1,0:T(8,128)(2,1)S(1)} %update1.1), channel_id=1, source_target_pairs={{0,16},{16,32},{32,48},{48,64},{64,80},{80,96},{96,112},{112,128},... | collective-permute-start | bytes 2359304 | tf_op jit(solution)/shard_map/ppermute | solution.py:206

commit v2 on v0

v2 whole, which is shorter than its diff:
```python
import functools
import math

import jax
import jax.numpy as jnp
from jax import lax
from jax.experimental import pallas as pl
from jax.experimental.pallas import tpu as pltpu
from jax.sharding import PartitionSpec as P

HEADS = 32
HEAD_DIM = 128
STEPS = 50
HALF = 8
WIDE = 256
ROWS = 192
FEATURES = HEADS * HEAD_DIM
EXPONENT = HEAD_DIM ** (-0.5) * math.log2(math.e)
GROUPS8 = [[half * HALF + k for k in range(HALF)] for half in range(2)]
NT = (((1,), (1,)), ((), ()))
SMALL = pl.CostEstimate(flops=1000, bytes_accessed=1000, transcendentals=0)
PARAMS = pltpu.CompilerParams(vmem_limit_bytes=60_000_000)


def arrange(arrays, half, layout, name):
    count = len(layout)
    width = count * WIDE

    def body(half_ref, *refs):
        sources, out, sem = refs[:count], refs[count], refs[count + 1]
        copies = [
            pltpu.make_async_copy(
                source.at[:, pl.ds(d * WIDE, WIDE)],
                out.at[d, :, pl.ds(i * WIDE, WIDE)],
                sem.at[i * HALF + d],
            )
            for i, source in enumerate(sources)
            for d in range(HALF)
        ]
        for copy in copies:
            copy.start()
        for copy in copies:
            copy.wait()

    def spec(other):
        return pl.BlockSpec((ROWS, HALF * WIDE), lambda i, h: (0, 1 - h[0] if other else h[0]))

    return pl.pallas_call(
        body,
        grid_spec=pltpu.PrefetchScalarGridSpec(
            num_scalar_prefetch=1,
            grid=(1,),
            in_specs=[spec(other) for _, other in layout],
            out_specs=pl.BlockSpec(memory_space=pl.ANY),
            scratch_shapes=[pltpu.SemaphoreType.DMA((count * HALF,))],
        ),
        out_shape=jax.ShapeDtypeStruct((HALF, ROWS, width), jnp.bfloat16),
        compiler_params=PARAMS,
        cost_estimate=SMALL,
        name=name,
    )(half, *[arrays[which] for which, _ in layout])


def attend_body(q_ref, kl_ref, kr_ref, vl_ref, vr_ref, o_ref, *s_refs):
    chunk = 512
    tile = s_refs[0].shape[0]
    queries = q_ref[...].reshape(-1, HEAD_DIM)
    side = kl_ref.shape[0]
    tiles = len(s_refs)
    states = [{} for _ in range(tiles)]
    outs = []

    def add(state, name, part, op):
        state[name] = op(state[name], part) if name in state else part

    def scores_of(t, i, at):
        keys = (kl_ref, kr_ref)[i][at : at + chunk, :]
        scores = lax.dot_general(
            queries[t * tile : (t + 1) * tile], keys, NT, preferred_element_type=jnp.float32
        )
        s_refs[t][:, i * side + at : i * side + at + chunk] = scores
        for j in range(0, chunk, 128):
            add(states[t], "largest", scores[:, j : j + 128], jnp.maximum)

    def mix(t, i, at):
        scores = s_refs[t][:, i * side + at : i * side + at + chunk]
        powers = jnp.exp2(scores * EXPONENT - states[t]["shift"])
        for j in range(0, chunk, 128):
            add(states[t], "total", powers[:, j : j + 128], jnp.add)
        product = jnp.dot(
            powers.astype(jnp.bfloat16),
            (vl_ref, vr_ref)[i][at : at + chunk, :],
            preferred_element_type=jnp.float32,
        )
        add(states[t], "mixed", product, jnp.add)

    for phase in range(tiles + 1):
        for i in range(2):
            for at in range(0, side, chunk):
                if phase < tiles:
                    scores_of(phase, i, at)
                if phase > 0:
                    mix(phase - 1, i, at)
        if phase < tiles:
            state = states[phase]
            state["shift"] = jnp.max(state["largest"], axis=1, keepdims=True) * EXPONENT
        if phase > 0:
            state = states[phase - 1]
            total = jnp.sum(state["total"], axis=1, keepdims=True)
            outs.append((state["mixed"] / total).astype(jnp.bfloat16))
    o_ref[...] = jnp.concatenate(outs).reshape(o_ref.shape)


def attend(meta, queries, near, far, rows, side_of, name, into=None, after=()):
    array, row_block, start = queries
    side = near.shape[0]
    tile = 256
    extra = ([] if into is None else [into]) + list(after)

    def body(m_ref, q_ref, kl, kr, vl, vr, *refs):
        attend_body(q_ref, kl, kr, vl, vr, *refs[len(extra) :])

    def out_index(h, m):
        return (m[0] if side_of == 0 else 1 - m[0], 0, h)

    keys = pl.BlockSpec((side, HEAD_DIM), lambda h, m: (0, h))
    values = pl.BlockSpec((side, HEAD_DIM), lambda h, m: (0, 2 + h))
    return pl.pallas_call(
        body,
        grid_spec=pltpu.PrefetchScalarGridSpec(
            num_scalar_prefetch=1,
            grid=(2,),
            in_specs=[
                pl.BlockSpec((HALF, rows, HEAD_DIM), lambda h, m: (0, row_block, start + h)),
                keys,
                keys,
                values,
                values,
            ]
            + [pl.BlockSpec(memory_space=pl.ANY)] * len(extra),
            out_specs=pl.BlockSpec((HALF, rows, HEAD_DIM), out_index),
            scratch_shapes=[pltpu.VMEM((tile, 2 * side), jnp.float32)] * (HALF * rows // tile),
        ),
        out_shape=jax.ShapeDtypeStruct((2 * HALF, rows, WIDE), jnp.bfloat16),
        input_output_aliases={} if into is None else {6: 0},
        compiler_params=PARAMS,
        cost_estimate=SMALL,
        name=name,
    )(meta, array, near, far, near, far, *extra)


def update_body(meta, mixed_ref, latent_ref, mod_ref, fresh_ref, o_ref):
    step_size = (meta[1] + 1).astype(jnp.float32) / STEPS
    squares = None
    for d in range(2 * HALF):
        part = mixed_ref[d].astype(jnp.float32)
        squares = part * part if squares is None else squares + part * part
    meansq = jnp.sum(squares, axis=1, keepdims=True) / FEATURES
    inverse = lax.rsqrt(meansq + 1e-06)
    for d in range(2 * HALF):
        at = slice(d * WIDE, (d + 1) * WIDE)
        velocity = (
            mixed_ref[d].astype(jnp.float32) * inverse * (1.0 + mod_ref[0, 0:1, at])
            + mod_ref[0, 1:2, at]
        ).astype(jnp.bfloat16)
        o_ref[:, at] = (
            latent_ref[:, at].astype(jnp.float32) - step_size * velocity.astype(jnp.float32)
        ).astype(jnp.bfloat16)

    @pl.when(meta[2] == 1)
    def _():
        o_ref[...] = fresh_ref[...]


def update(meta, mixed, latent, mod_table, fresh, first, name):
    rows = mixed.shape[1]
    tile = 48
    steps = rows // tile
    return pl.pallas_call(
        update_body,
        grid_spec=pltpu.PrefetchScalarGridSpec(
            num_scalar_prefetch=1,
            grid=(steps,),
            in_specs=[
                pl.BlockSpec((2 * HALF, tile, WIDE), lambda i, m: (0, i, 0)),
                pl.BlockSpec((tile, FEATURES), lambda i, m: (first // tile + i, 0)),
                pl.BlockSpec((1, 2, FEATURES), lambda i, m: (m[1], 0, 0)),
                pl.BlockSpec((tile, FEATURES), lambda i, m: (first // tile + i, 0)),
            ],
            out_specs=pl.BlockSpec((tile, FEATURES), lambda i, m: (i, 0)),
        ),
        out_shape=jax.ShapeDtypeStruct((rows, FEATURES), jnp.bfloat16),
        compiler_params=PARAMS,
        cost_estimate=SMALL,
        name=name,
    )(meta, mixed, latent, mod_table, fresh)


def across(value):
    return lax.ppermute(value, "seq", [(s, (s + HALF) % (2 * HALF)) for s in range(2 * HALF)])


def within(value):
    return lax.all_to_all(value, "seq", 0, 0, axis_index_groups=GROUPS8)


def on_device(latent, queries, key_rows, values, mod_table, levels, fresh_noise):
    latent, queries, key_rows, values = (x[0] for x in (latent, queries, key_rows, values))
    half = lax.axis_index("seq") // HALF
    near = half.reshape(1)
    count = lax.axis_size("queue")
    group = lax.axis_index("queue")
    meta = jnp.stack([half, levels[0], (group == count - 1).astype(jnp.int32)])
    tie = lambda x, *after: lax.optimization_barrier((x, *after))[0]
    flat = lambda x: x.reshape(-1, x.shape[2])
    always = (levels[0] | 1) != 0

    def fenced(f, *operands):
        shapes = jax.eval_shape(f, *operands)
        empty = lambda *x: jax.tree.map(lambda t: jnp.zeros(t.shape, t.dtype), shapes)
        return lax.cond(always, f, empty, *operands)

    inputs = (key_rows, values, queries)
    sent = arrange(inputs, near, [(0, True), (1, True)], "send")
    own = arrange(inputs, near, [(0, False), (1, False), (2, False)], "keep")
    out_q = arrange(inputs, near, [(2, True)], "send_q")

    far_kv = across(sent)

    def first_stage(x, y):
        x = within(x)
        return x, within(tie(y, x))

    own, far_q = fenced(first_stage, own, out_q)
    far_q = across(tie(far_q, far_kv))
    far_kv = flat(fenced(within, far_kv))
    near_kv = flat(own)
    ring = [(g, (g + 1) % count) for g in range(count)]
    chunks = ((0, 96), (96, 96))
    back = []
    last = []
    for i, (first, rows) in enumerate(chunks):
        m = attend(
            meta, (own, first // rows, 4), near_kv, far_kv, rows, 0, f"near{i}", after=last
        )
        m = attend(meta, (far_q, first // rows, 0), near_kv, far_kv, rows, 1, f"far{i}", m)
        last = [m]
        back.append(lax.all_to_all(tie(m, *back), "seq", 0, 0))
    shifted = []
    for i, (first, rows) in enumerate(chunks):
        denoised = update(meta, back[i], latent, mod_table, fresh_noise, first, f"update{i}")
        shifted.append(lax.ppermute(denoised, "queue", ring))
    return jnp.concatenate(shifted)[None]


def solution(mesh):
    return jax.shard_map(
        on_device,
        mesh=mesh,
        in_specs=(
            P("queue", "seq", None),
            P("queue", "seq", None),
            P("queue", "seq", None),
            P("queue", "seq", None),
            P(),
            P("queue"),
            P("seq", None),
        ),
        out_specs=P("queue", "seq", None),
        check_vma=False,
    )
```

time: 357 us -> 218 us (0.61); the launches traced: 352 us -> 217 us
  matrix products: 99.5 us -> 0 us
  blocking collectives: 0 us -> 77.9 us
  waiting for transfers between devices: 122 us -> 51.3 us
  starting transfers between devices: 93.1 us -> 29.8 us
  Pallas kernels: 0 us -> 52.2 us
  local copies, waits for them, and re-layouts: 29.2 us -> 3.43 us
  other arithmetic: 7.83 us -> 1.84 us
    all_to_all x0 -> x2, blocking collectives: none -> 77.9 us  [within(): return lax.all_to_all(value, 'seq', 0, 0, axis_index_groups=GROUPS8)]
    all_to_all x4 -> x3, waiting for transfers between devices: 90.2 us -> 24.6 us  [the longest x2 13.9 us: on_device(): back.append(lax.all_to_all(tie(m, *back), 'seq', 0, 0))]
    sub x6 -> x0, matrix products: 56.8 us -> none  [one_block(): powers = jnp.exp(scores - largest)]
    pallas_call x0 -> x9, Pallas kernels: none -> 52.2 us  [the longest x4 38.5 us: attend(): pl.pallas_call(body, grid_spec=pltpu.PrefetchScalarGridSpec(num_scalar_pr...]
    all_to_all x4 -> x3, starting transfers between devices: 64.8 us -> 18.5 us  [the longest x2 13.6 us: on_device(): back.append(lax.all_to_all(tie(m, *back), 'seq', 0, 0))]
    dot_general x6 -> x0, matrix products: 42.7 us -> none  [one_block(): jnp.einsum('hqk,khd->qhd', weights, values, preferred_element_type=jnp.fl...]
    another operation x7 -> x0, local copies, waits for them, and re-layouts: 21.9 us -> none  [the longest x6 17.1 us: velocity_of(): part[0].reshape(local_rows, devices, per_device, HEAD_DIM)]
    ppermute x1 -> x4, starting transfers between devices: 28.3 us -> 11.4 us  [the longest x2 7.83 us: across(): lax.ppermute(value, 'seq', [(s, (s + HALF) % (2 * HALF)) for s in range(2...]
  transfers between devices with their start and end apart: 5 -> 7, of which waited for: 5 -> 5; matrix products, arithmetic and copies ran while one was open for 4% -> 1% of each run, Pallas kernels for 0% -> 19%
where the time goes in v2:
time: 218 us; the launch traced here: 217 us
  blocking collectives  77.9 us (36%)
  Pallas kernels  52.2 us (24%)
  waiting for transfers between devices  51.3 us (24%)
  starting transfers between devices  29.8 us (14%)
  local copies, waits for them, and re-layouts  3.43 us (2%)
    all_to_all x2, blocking collectives, within(): return lax.all_to_all(value, 'seq', 0, 0, axis_index_groups=GROUPS8)  77.9 us
    pallas_call x4, Pallas kernels, attend(): pl.pallas_call(body, grid_spec=pltpu.PrefetchScalarGridSpec(num_scalar_pr...  38.5 us
    ppermute x2, waiting for transfers between devices, on_device(): shifted.append(lax.ppermute(denoised, 'queue', ring))  26.7 us
    all_to_all x2, waiting for transfers between devices, on_device(): back.append(lax.all_to_all(tie(m, *back), 'seq', 0, 0))  13.9 us
    all_to_all x2, starting transfers between devices, on_device(): back.append(lax.all_to_all(tie(m, *back), 'seq', 0, 0))  13.6 us
    all_to_all x1, waiting for transfers between devices, within(): return lax.all_to_all(value, 'seq', 0, 0, axis_index_groups=GROUPS8)  10.7 us
    ppermute x2, starting transfers between devices, across(): lax.ppermute(value, 'seq', [(s, (s + HALF) % (2 * HALF)) for s in range(2...  7.83 us
    pallas_call x3, Pallas kernels, arrange(): pl.pallas_call(body, grid_spec=pltpu.PrefetchScalarGridSpec(num_scalar_pr...  6.92 us
  transfers between devices with their start and end apart: 7, of which 5 were waited for; matrix products, arithmetic and copies ran while one was open for 1% of the time, Pallas kernels for 19%

profile of v2, /device:TPU:1, one launch (start us, length us, event | category | flops | bytes accessed | tf_op | source)
XLA Modules:
  0.0 217.3 jit_solution(13986702582211647468)
XLA Ops:
  0.0 2.6 %send.1 = bf16[8,192,512]{2,1,0:T(8,128)(2,1)} custom-call(s32[1]{0:T(128)} %bitcast.2.half_ref, bf16[192,4096]{1,0:T(8,128)(2,1)} %bitcast.12, bf16[192,4096]{1,0:T(8,128)(2,1)} %bitcast.14), custom_call_target="tpu_custom_call" | custom-call | flops 1000 | bytes 1000 | tf_op jit(solution)/shard_map/send/pallas_call | solution.py:48
  2.6 7.8 %collective-permute-start = (bf16[8,192,512]{2,1,0:T(8,128)(2,1)}, bf16[8,192,512]{2,1,0:T(8,128)(2,1)}, u32[]{:S(2)}, u32[]{:S(2)}) collective-permute-start(bf16[8,192,512]{2,1,0:T(8,128)(2,1)} %send.1), channel_id=1, source_target_pairs={{0,8},{1,9},{2,10},{3,11},{4,12},{5,13},{6,14},{7,15},{8,0},{9,1},... | collective-permute-start | bytes 4718600 | tf_op jit(solution)/shard_map/ppermute | solution.py:200
  10.5 2.2 %keep.1 = bf16[8,192,768]{2,1,0:T(8,128)(2,1)S(1)} custom-call(s32[1]{0:T(128)} %bitcast.2.half_ref, bf16[192,4096]{1,0:T(8,128)(2,1)} %bitcast.13, bf16[192,4096]{1,0:T(8,128)(2,1)} %bitcast.15, bf16[192,4096]{1,0:T(8,128)(2,1)} %bitcast.16), custom_call_target="tpu_custom_call" | custom-call | flops 1000 | bytes 1000 | tf_op jit(solution)/shard_map/keep/pallas_call | solution.py:48
  12.7 2.1 send_q.1
  15.4 52.0 %conditional.2 = (bf16[8,192,768]{2,1,0:T(8,128)(2,1)}, bf16[8,192,256]{2,1,0:T(8,128)(2,1)}, bf16[1536,768]{1,0:T(8,128)(2,1)S(1)}) conditional(s32[]{:T(128)} %bitcast.4, () %tuple.26, (bf16[8,192,768]{2,1,0:T(8,128)(2,1)S(1)}, bf16[8,192,256]{2,1,0:T(8,128)(2,1)}) %tuple.27), branch_computations={%region_0.1_spmd, %region_1.2_spmd} | conditional | bytes 11796536 | solution.py:221
  15.4 34.8 %all_to_all.22 = bf16[8,192,768]{2,1,0:T(8,128)(2,1)} all-to-all(bf16[8,192,768]{2,1,0:T(8,128)(2,1)S(1)} %get-tuple-element.15), channel_id=1, replica_groups={{0,1,2,3,4,5,6,7},{8,9,10,11,12,13,14,15},{16,17,18,19,20,21,22,23},{24..., dimensions={0} | all-to-all | bytes 4718592 | tf_op jit(solution)/shard_map/cond/branch_1_fun/all_to_all | solution.py:204
  50.2 4.8 %all-to-all-start.1 = ((bf16[8,192,256]{2,1,0:T(8,128)(2,1)}), bf16[8,192,256]{2,1,0:T(8,128)(2,1)}, u32[]{:S(2)}, u32[]{:S(2)}) async-start(bf16[8,192,256]{2,1,0:T(8,128)(2,1)} %get-tuple-element.17), calls=%async_computation.1 | async-start | bytes 1572864 | tf_op jit(solution)/shard_map/cond/branch_1_fun/all_to_all | solution.py:204
  55.1 1.7 copy.15
  56.7 10.7 %all-to-all-done.1 = bf16[8,192,256]{2,1,0:T(8,128)(2,1)} async-done(((bf16[8,192,256]{2,1,0:T(8,128)(2,1)}), bf16[8,192,256]{2,1,0:T(8,128)(2,1)}, u32[]{:S(2)}, u32[]{:S(2)}) %all-to-all-start.1) | async-done | bytes 786464 | tf_op jit(solution)/shard_map/cond/branch_1_fun/all_to_all | solution.py:204
  67.5 0.0 collective-permute-done
  67.5 0.0 collective-permute-start.1
  67.5 0.6 pad_add_fusion.m_ref.meta
  68.1 43.1 %conditional.3 = (bf16[1536,512]{1,0:T(8,128)(2,1)}) conditional(s32[]{:T(128)} %bitcast.4, () %tuple.29, bf16[8,192,512]{2,1,0:T(8,128)(2,1)} %collective-permute-done), branch_computations={%region_2.3_spmd, %region_3.4_spmd} | conditional | bytes 3145736 | solution.py:221
  68.1 43.1 %all_to_all.23 = bf16[8,192,512]{2,1,0:T(8,128)(2,1)} all-to-all(bf16[8,192,512]{2,1,0:T(8,128)(2,1)} %param.3), channel_id=1, replica_groups={{0,1,2,3,4,5,6,7},{8,9,10,11,12,13,14,15},{16,17,18,19,20,21,22,23},{24..., dimensions={0} | all-to-all | bytes 3145728 | tf_op jit(solution)/shard_map/cond/branch_1_fun/all_to_all | solution.py:204
  111.2 0.0 copy-start
  111.2 9.9 %near0.1.refs_0_ = bf16[16,96,256]{2,1,0:T(8,128)(2,1)} custom-call(s32[3]{0:T(128)} %pad_add_fusion.m_ref.meta, bf16[8,192,768]{2,1,0:T(8,128)(2,1)} %get-tuple-element.26.q_ref, bf16[1536,768]{1,0:T(8,128)(2,1)S(1)} %get-tuple-element.25.kl.vl, bf16[1536,512]{1,0:T(8,128)(2,1)} %get-tuple-element.34.kr.vr, bf16[1536,768]{1,0:T(8,128)(2,1)S(1)} %get-tuple-element.25.kl.vl, ...), custom_call_target="tpu_custom_call" | custom-call | flops 1000 | bytes 1000 | tf_op jit(solution)/shard_map/near0/pallas_call | solution.py:128
  121.1 0.0 collective-permute-done.1.q_ref
  121.1 0.0 copy-start.2
  121.1 0.9 copy-done.2
  122.0 0.0 copy-done
  122.0 9.4 %far0.1.refs_0_ = bf16[16,96,256]{2,1,0:T(8,128)(2,1)} custom-call(s32[3]{0:T(128)} %pad_add_fusion.m_ref.meta, bf16[8,192,256]{2,1,0:T(8,128)(2,1)} %copy-done.2, bf16[1536,768]{1,0:T(8,128)(2,1)S(1)} %get-tuple-element.25.kl.vl, bf16[1536,512]{1,0:T(8,128)(2,1)S(1)} %copy-done, ...), custom_call_target="tpu_custom_call", output_to_operand_aliasing={{}: (6, {})} | custom-call | flops 1000 | bytes 1000 | tf_op jit(solution)/shard_map/far0/pallas_call | solution.py:128
  131.3 4.4 %all-to-all-start.3 = ((bf16[16,96,256]{2,1,0:T(8,128)(2,1)}), bf16[16,96,256]{2,1,0:T(8,128)(2,1)S(1)}, u32[]{:S(2)}, u32[]{:S(2)}) async-start(bf16[16,96,256]{2,1,0:T(8,128)(2,1)} %far0.1.refs_0_), calls=%async_computation.3 | async-start | bytes 1572864 | tf_op jit(solution)/shard_map/all_to_all | solution.py:248
  135.8 0.0 copy-start.1
  135.8 9.9 %near1.1.refs_0_ = bf16[16,96,256]{2,1,0:T(8,128)(2,1)} custom-call(s32[3]{0:T(128)} %pad_add_fusion.m_ref.meta, bf16[8,192,768]{2,1,0:T(8,128)(2,1)} %get-tuple-element.26.q_ref, bf16[1536,768]{1,0:T(8,128)(2,1)S(1)} %get-tuple-element.25.kl.vl, bf16[1536,512]{1,0:T(8,128)(2,1)} %get-tuple-element.34.kr.vr, bf16[1536,768]{1,0:T(8,128)(2,1)S(1)} %get-tuple-element.25.kl.vl, ...), custom_call_target="tpu_custom_call" | custom-call | flops 1000 | bytes 1000 | tf_op jit(solution)/shard_map/near1/pallas_call | solution.py:128
  145.6 0.0 copy-done.1
  145.6 9.4 %far1.1 = bf16[16,96,256]{2,1,0:T(8,128)(2,1)} custom-call(s32[3]{0:T(128)} %pad_add_fusion.m_ref.meta, bf16[8,192,256]{2,1,0:T(8,128)(2,1)} %copy-done.2, bf16[1536,768]{1,0:T(8,128)(2,1)S(1)} %get-tuple-element.25.kl.vl, bf16[1536,512]{1,0:T(8,128)(2,1)S(1)} %copy-done.1, ...), custom_call_target="tpu_custom_call", output_to_operand_aliasing={{}: (6, {})} | custom-call | flops 1000 | bytes 1000 | tf_op jit(solution)/shard_map/far1/pallas_call | solution.py:128
  155.0 0.5 all-to-all-done.3.mixed_ref
  155.5 0.0 copy-start.3
  155.5 9.2 %all-to-all-start.4 = ((bf16[16,96,256]{2,1,0:T(8,128)(2,1)}), bf16[16,96,256]{2,1,0:T(8,128)(2,1)S(1)}, u32[]{:S(2)}, u32[]{:S(2)}) async-start(bf16[16,96,256]{2,1,0:T(8,128)(2,1)} %far1.1), calls=%async_computation.4 | async-start | bytes 1572864 | tf_op jit(solution)/shard_map/all_to_all | solution.py:248
  164.7 0.0 copy-done.3
  164.7 3.4 %update0.1 = bf16[96,4096]{1,0:T(8,128)(2,1)} custom-call(s32[3]{0:T(128)} %pad_add_fusion.m_ref.meta, bf16[16,96,256]{2,1,0:T(8,128)(2,1)} %copy-done.3, bf16[192,4096]{1,0:T(8,128)(2,1)} %bitcast.18, f32[50,2,4096]{2,1,0:T(2,128)} %mod_ref.3, bf16[192,4096]{1,0:T(8,128)(2,1)} %fresh_ref.3), custom_call_target="tpu_custom_call" | custom-call | flops 1000 | bytes 1000 | tf_op jit(solution)/shard_map/update0/pallas_call | solution.py:179
  168.1 1.0 collective-permute-start.2
  169.2 13.4 %all-to-all-done.4.mixed_ref = bf16[16,96,256]{2,1,0:T(8,128)(2,1)S(1)} async-done(((bf16[16,96,256]{2,1,0:T(8,128)(2,1)}), bf16[16,96,256]{2,1,0:T(8,128)(2,1)S(1)}, u32[]{:S(2)}, u32[]{:S(2)}) %all-to-all-start.4) | async-done | bytes 786464 | tf_op jit(solution)/shard_map/all_to_all | solution.py:248
  182.5 0.0 copy-start.4
  182.5 0.9 copy-done.4
  183.4 3.4 %update1.1 = bf16[96,4096]{1,0:T(8,128)(2,1)} custom-call(s32[3]{0:T(128)} %pad_add_fusion.m_ref.meta, bf16[16,96,256]{2,1,0:T(8,128)(2,1)} %copy-done.4, bf16[192,4096]{1,0:T(8,128)(2,1)} %bitcast.19, f32[50,2,4096]{2,1,0:T(2,128)} %mod_ref.3, bf16[192,4096]{1,0:T(8,128)(2,1)} %fresh_ref.3), custom_call_target="tpu_custom_call" | custom-call | flops 1000 | bytes 1000 | tf_op jit(solution)/shard_map/update1/pallas_call | solution.py:179
  186.9 2.5 %collective-permute-start.3 = (bf16[96,4096]{1,0:T(8,128)(2,1)}, bf16[96,4096]{1,0:T(8,128)(2,1)S(1)}, u32[]{:S(2)}, u32[]{:S(2)}) collective-permute-start(bf16[96,4096]{1,0:T(8,128)(2,1)} %update1.1), channel_id=1, source_target_pairs={{0,16},{16,32},{32,48},{48,64},{64,80},{80,96},{96,112},{112,128},... | collective-permute-start | bytes 2359304 | tf_op jit(solution)/shard_map/ppermute | solution.py:252
  189.4 10.5 %collective-permute-done.2 = bf16[96,4096]{1,0:T(8,128)(2,1)S(1)} collective-permute-done((bf16[96,4096]{1,0:T(8,128)(2,1)}, bf16[96,4096]{1,0:T(8,128)(2,1)S(1)}, u32[]{:S(2)}, u32[]{:S(2)}) %collective-permute-start.2) | collective-permute-done | bytes 786464 | tf_op jit(solution)/shard_map/ppermute | solution.py:252
  199.8 16.2 %collective-permute-done.3 = bf16[96,4096]{1,0:T(8,128)(2,1)S(1)} collective-permute-done((bf16[96,4096]{1,0:T(8,128)(2,1)}, bf16[96,4096]{1,0:T(8,128)(2,1)S(1)}, u32[]{:S(2)}, u32[]{:S(2)}) %collective-permute-start.3) | collective-permute-done | bytes 786464 | tf_op jit(solution)/shard_map/ppermute | solution.py:252
  216.0 1.2 maximum_bitcast_fusion
Async XLA Ops:
  2.6 64.8 %collective-permute-start = (bf16[8,192,512]{2,1,0:T(8,128)(2,1)}, bf16[8,192,512]{2,1,0:T(8,128)(2,1)}, u32[]{:S(2)}, u32[]{:S(2)}) collective-permute-start(bf16[8,192,512]{2,1,0:T(8,128)(2,1)} %send.1), channel_id=1, source_target_pairs={{0,8},{1,9},{2,10},{3,11},{4,12},{5,13},{6,14},{7,15},{8,0},{9,1},... | collective-permute-start | bytes 4718600 | tf_op jit(solution)/shard_map/ppermute | solution.py:200
  50.2 17.3 %all-to-all-start.1 = ((bf16[8,192,256]{2,1,0:T(8,128)(2,1)}), bf16[8,192,256]{2,1,0:T(8,128)(2,1)}, u32[]{:S(2)}, u32[]{:S(2)}) async-start(bf16[8,192,256]{2,1,0:T(8,128)(2,1)} %get-tuple-element.17), calls=%async_computation.1 | async-start | bytes 1572864 | tf_op jit(solution)/shard_map/cond/branch_1_fun/all_to_all | solution.py:204
  67.5 53.6 %collective-permute-start.1 = (bf16[8,192,256]{2,1,0:T(8,128)(2,1)}, bf16[8,192,256]{2,1,0:T(8,128)(2,1)S(1)}, u32[]{:S(2)}, u32[]{:S(2)}) collective-permute-start(bf16[8,192,256]{2,1,0:T(8,128)(2,1)} %get-tuple-element.24), channel_id=1, source_target_pairs={{0,8},{1,9},{2,10},{3,11},{4,12},{5,13},{6,14},{7,15},{8,0},{9,1},... | collective-permute-start | bytes 2359304 | tf_op jit(solution)/shard_map/ppermute | solution.py:200
  111.2 10.7 %copy-start = (bf16[1536,512]{1,0:T(8,128)(2,1)S(1)}, bf16[1536,512]{1,0:T(8,128)(2,1)}, u32[]{:S(2)}) copy-start(bf16[1536,512]{1,0:T(8,128)(2,1)} %get-tuple-element.34.kr.vr) | copy-start | bytes 4718596
  121.1 0.9 copy-start.2
  131.3 24.2 %all-to-all-start.3 = ((bf16[16,96,256]{2,1,0:T(8,128)(2,1)}), bf16[16,96,256]{2,1,0:T(8,128)(2,1)S(1)}, u32[]{:S(2)}, u32[]{:S(2)}) async-start(bf16[16,96,256]{2,1,0:T(8,128)(2,1)} %far0.1.refs_0_), calls=%async_computation.3 | async-start | bytes 1572864 | tf_op jit(solution)/shard_map/all_to_all | solution.py:248
  135.8 9.9 %copy-start.1 = (bf16[1536,512]{1,0:T(8,128)(2,1)S(1)}, bf16[1536,512]{1,0:T(8,128)(2,1)}, u32[]{:S(2)}) copy-start(bf16[1536,512]{1,0:T(8,128)(2,1)} %get-tuple-element.34.kr.vr) | copy-start | bytes 4718596
  155.5 9.2 %copy-start.3 = (bf16[16,96,256]{2,1,0:T(8,128)(2,1)}, bf16[16,96,256]{2,1,0:T(8,128)(2,1)S(1)}, u32[]{:S(2)}) copy-start(bf16[16,96,256]{2,1,0:T(8,128)(2,1)S(1)} %all-to-all-done.3.mixed_ref) | copy-start | bytes 2359300
  155.5 27.0 %all-to-all-start.4 = ((bf16[16,96,256]{2,1,0:T(8,128)(2,1)}), bf16[16,96,256]{2,1,0:T(8,128)(2,1)S(1)}, u32[]{:S(2)}, u32[]{:S(2)}) async-start(bf16[16,96,256]{2,1,0:T(8,128)(2,1)} %far1.1), calls=%async_computation.4 | async-start | bytes 1572864 | tf_op jit(solution)/shard_map/all_to_all | solution.py:248
  168.1 31.7 %collective-permute-start.2 = (bf16[96,4096]{1,0:T(8,128)(2,1)}, bf16[96,4096]{1,0:T(8,128)(2,1)S(1)}, u32[]{:S(2)}, u32[]{:S(2)}) collective-permute-start(bf16[96,4096]{1,0:T(8,128)(2,1)} %update0.1), channel_id=1, source_target_pairs={{0,16},{16,32},{32,48},{48,64},{64,80},{80,96},{96,112},{112,128},... | collective-permute-start | bytes 2359304 | tf_op jit(solution)/shard_map/ppermute | solution.py:252
  182.5 0.9 copy-start.4
  186.9 29.2 %collective-permute-start.3 = (bf16[96,4096]{1,0:T(8,128)(2,1)}, bf16[96,4096]{1,0:T(8,128)(2,1)S(1)}, u32[]{:S(2)}, u32[]{:S(2)}) collective-permute-start(bf16[96,4096]{1,0:T(8,128)(2,1)} %update1.1), channel_id=1, source_target_pairs={{0,16},{16,32},{32,48},{48,64},{64,80},{80,96},{96,112},{112,128},... | collective-permute-start | bytes 2359304 | tf_op jit(solution)/shard_map/ppermute | solution.py:252

commit v3 on v2

v3 whole, which is shorter than its diff:
```python
import functools
import math

import jax
import jax.numpy as jnp
from jax import lax
from jax.experimental import pallas as pl
from jax.experimental.pallas import tpu as pltpu
from jax.sharding import PartitionSpec as P

HEADS = 32
HEAD_DIM = 128
STEPS = 50
HALF = 8
WIDE = 256
ROWS = 192
FEATURES = HEADS * HEAD_DIM
EXPONENT = HEAD_DIM ** (-0.5) * math.log2(math.e)
GROUPS8 = [[half * HALF + k for k in range(HALF)] for half in range(2)]
NT = (((1,), (1,)), ((), ()))
SMALL = pl.CostEstimate(flops=1000, bytes_accessed=1000, transcendentals=0)
PARAMS = pltpu.CompilerParams(vmem_limit_bytes=60_000_000)


def arrange(arrays, half, layout, rows, width, name, after=()):
    count = len(layout)
    width_of = lambda head: WIDE if head is None else HEAD_DIM

    def body(half_ref, *refs):
        sources, out, sem = refs[:count], refs[-2], refs[-1]
        copies = []
        for source, (_, _, head, row, at, first, taken) in zip(sources, layout):
            w = width_of(head)
            for d in range(HALF):
                copies.append(
                    pltpu.make_async_copy(
                        source.at[
                            pl.ds(first, taken), pl.ds(d * WIDE + (head or 0) * HEAD_DIM, w)
                        ],
                        out.at[d, pl.ds(row, taken), pl.ds(at, w)],
                        sem.at[len(copies)],
                    )
                )
        for copy in copies:
            copy.start()
        for copy in copies:
            copy.wait()

    def spec(other):
        return pl.BlockSpec((ROWS, HALF * WIDE), lambda i, h: (0, 1 - h[0] if other else h[0]))

    return pl.pallas_call(
        body,
        grid_spec=pltpu.PrefetchScalarGridSpec(
            num_scalar_prefetch=1,
            grid=(1,),
            in_specs=[spec(other) for _, other, *_ in layout]
            + [pl.BlockSpec(memory_space=pl.ANY)] * len(after),
            out_specs=pl.BlockSpec(memory_space=pl.ANY),
            scratch_shapes=[pltpu.SemaphoreType.DMA((count * HALF,))],
        ),
        out_shape=jax.ShapeDtypeStruct((HALF, rows, width), jnp.bfloat16),
        compiler_params=PARAMS,
        cost_estimate=SMALL,
        name=name,
    )(half, *[arrays[which] for which, *_ in layout], *after)


def attend_body(q_ref, kl_ref, kr_ref, vl_ref, vr_ref, o_ref, *s_refs):
    chunk = 512
    tile = s_refs[0].shape[0]
    queries = q_ref[...].reshape(-1, HEAD_DIM)
    side = kl_ref.shape[0]
    tiles = len(s_refs)
    states = [{} for _ in range(tiles)]
    outs = []

    def add(state, name, part, op):
        state[name] = op(state[name], part) if name in state else part

    def scores_of(t, i, at):
        keys = (kl_ref, kr_ref)[i][at : at + chunk, :]
        scores = lax.dot_general(
            queries[t * tile : (t + 1) * tile], keys, NT, preferred_element_type=jnp.float32
        )
        s_refs[t][:, i * side + at : i * side + at + chunk] = scores
        for j in range(0, chunk, 128):
            add(states[t], "largest", scores[:, j : j + 128], jnp.maximum)

    def mix(t, i, at):
        scores = s_refs[t][:, i * side + at : i * side + at + chunk]
        powers = jnp.exp2(scores * EXPONENT - states[t]["shift"])
        for j in range(0, chunk, 128):
            add(states[t], "total", powers[:, j : j + 128], jnp.add)
        product = jnp.dot(
            powers.astype(jnp.bfloat16),
            (vl_ref, vr_ref)[i][at : at + chunk, :],
            preferred_element_type=jnp.float32,
        )
        add(states[t], "mixed", product, jnp.add)

    for phase in range(tiles + 1):
        for i in range(2):
            for at in range(0, side, chunk):
                if phase < tiles:
                    scores_of(phase, i, at)
                if phase > 0:
                    mix(phase - 1, i, at)
        if phase < tiles:
            state = states[phase]
            state["shift"] = jnp.max(state["largest"], axis=1, keepdims=True) * EXPONENT
        if phase > 0:
            state = states[phase - 1]
            total = jnp.sum(state["total"], axis=1, keepdims=True)
            outs.append((state["mixed"] / total).astype(jnp.bfloat16))
    o_ref[...] = jnp.concatenate(outs).reshape(o_ref.shape)


def attend(queries, near, far, rows, name, after=()):
    array, row_block, start = queries
    side = near.shape[0]
    tile = 256
    extra = list(after)

    def body(q_ref, kl, vl, k0, v0, k1, v1, *refs):
        o_ref, k_ref, v_ref, *s_refs = refs[len(extra) :]

        def choose(k, v):
            k_ref[...] = k[...].reshape(k_ref.shape)
            v_ref[...] = v[...].reshape(v_ref.shape)

        for h, (k, v) in enumerate(((k0, v0), (k1, v1))):
            pl.when(pl.program_id(0) == h)(functools.partial(choose, k, v))
        attend_body(q_ref, kl, k_ref, vl, v_ref, o_ref, *s_refs)

    column = lambda at: pl.BlockSpec((side, HEAD_DIM), at)
    far_columns = [
        pl.BlockSpec((HALF, ROWS, HEAD_DIM), lambda h, at=at: (0, 0, at)) for at in range(2)
    ]
    return pl.pallas_call(
        body,
        grid=(2,),
        in_specs=[
            pl.BlockSpec((HALF, rows, HEAD_DIM), lambda h: (0, row_block, start + h)),
            column(lambda h: (0, h)),
            column(lambda h: (0, 2 + h)),
        ]
        + far_columns * 2
        + [pl.BlockSpec(memory_space=pl.ANY)] * len(extra),
        out_specs=pl.BlockSpec((HALF, rows, HEAD_DIM), lambda h: (0, 0, h)),
        out_shape=jax.ShapeDtypeStruct((HALF, rows, WIDE), jnp.bfloat16),
        scratch_shapes=[pltpu.VMEM((side, HEAD_DIM), jnp.bfloat16)] * 2
        + [pltpu.VMEM((tile, 2 * side), jnp.float32)] * (HALF * rows // tile),
        compiler_params=PARAMS,
        cost_estimate=SMALL,
        name=name,
    )(array, near, near, far[0], far[0], far[1], far[1], *extra)


def update_body(half_ref, levels, mixed_ref, latent_ref, mod_ref, fresh_ref, o_ref):
    half = half_ref[0]
    step_size = (levels[0] + 1).astype(jnp.float32) / STEPS
    squares = None
    for d in range(HALF):
        for i in range(2):
            part = mixed_ref[d, :, i * WIDE : (i + 1) * WIDE].astype(jnp.float32)
            squares = part * part if squares is None else squares + part * part
    meansq = jnp.sum(squares, axis=1, keepdims=True) / FEATURES
    inverse = lax.rsqrt(meansq + 1e-06)
    for i in range(2):
        start = (half if i == 0 else 1 - half) * (HALF * WIDE)
        for d in range(HALF):
            at = pl.ds(pl.multiple_of(start + d * WIDE, WIDE), WIDE)
            velocity = (
                mixed_ref[d, :, i * WIDE : (i + 1) * WIDE].astype(jnp.float32)
                * inverse
                * (1.0 + mod_ref[0, 0:1, at])
                + mod_ref[0, 1:2, at]
            ).astype(jnp.bfloat16)
            o_ref[:, at] = (
                latent_ref[:, at].astype(jnp.float32) - step_size * velocity.astype(jnp.float32)
            ).astype(jnp.bfloat16)

    @pl.when(lax.axis_index("queue") == lax.axis_size("queue") - 1)
    def _():
        o_ref[...] = fresh_ref[...]


def update(half, levels, mixed, latent, mod_table, fresh, first, name):
    rows = mixed.shape[1]
    tile = 48
    steps = rows // tile
    plain = pl.BlockSpec((tile, FEATURES), lambda i, h, m: (first // tile + i, 0))
    return pl.pallas_call(
        update_body,
        grid_spec=pltpu.PrefetchScalarGridSpec(
            num_scalar_prefetch=2,
            grid=(steps,),
            in_specs=[
                pl.BlockSpec((HALF, tile, 2 * WIDE), lambda i, h, m: (0, i, 0)),
                plain,
                pl.BlockSpec((1, 2, FEATURES), lambda i, h, m: (m[0], 0, 0)),
                plain,
            ],
            out_specs=pl.BlockSpec((tile, FEATURES), lambda i, h, m: (i, 0)),
        ),
        out_shape=jax.ShapeDtypeStruct((rows, FEATURES), jnp.bfloat16),
        compiler_params=PARAMS,
        cost_estimate=SMALL,
        name=name,
    )(half, levels, mixed, latent, mod_table, fresh)


def across(value):
    return lax.ppermute(value, "seq", [(s, (s + HALF) % (2 * HALF)) for s in range(2 * HALF)])


def within(value):
    return lax.all_to_all(value, "seq", 0, 0, axis_index_groups=GROUPS8)


def on_device(latent, queries, key_rows, values, mod_table, levels, fresh_noise):
    latent, queries, key_rows, values = (x[0] for x in (latent, queries, key_rows, values))
    half = lax.axis_index("seq") // HALF
    near = half.reshape(1)
    count = lax.axis_size("queue")
    tie = lambda x, *after: lax.optimization_barrier((x, *after))[0] if after else x
    flat = lambda x: x.reshape(-1, x.shape[2])
    always = (levels[0] | 1) != 0

    def fenced(f, *operands):
        shapes = jax.eval_shape(f, *operands)
        empty = lambda *x: jax.tree.map(lambda t: jnp.zeros(t.shape, t.dtype), shapes)
        return lax.cond(always, f, empty, *operands)

    inputs = (key_rows, values, queries)
    chunks = ((0, 96), (96, 96))
    part = chunks[0][1]
    sent0 = arrange(
        inputs,
        near,
        [(0, True, 0, 0, 0, 0, ROWS), (1, True, 0, 0, HEAD_DIM, 0, ROWS), (2, True, None, ROWS, 0, 0, part)],
        ROWS + part,
        WIDE,
        "send0",
    )
    sent1 = arrange(
        inputs,
        near,
        [
            (0, True, 1, 0, 0, 0, ROWS),
            (1, True, 1, 0, HEAD_DIM, 0, ROWS),
            (2, True, None, ROWS, 0, part, ROWS - part),
        ],
        2 * ROWS - part,
        WIDE,
        "send1",
        [sent0],
    )
    own = arrange(
        inputs,
        near,
        [(i, False, None, 0, i * WIDE, 0, ROWS) for i in range(3)],
        ROWS,
        3 * WIDE,
        "keep",
        [sent1],
    )

    far0 = across(sent0)
    sent1 = fenced(within, sent1)
    far1 = across(sent1[:, :ROWS])
    own = fenced(within, tie(own, sent1))
    last_q = across(tie(sent1[:, ROWS:], own))
    far0 = fenced(within, tie(far0, own))
    far_q = [(far0, ROWS // part), (last_q, 0)]

    near_kv, far_kv = flat(own), (far0, far1)
    ring = [(g, (g + 1) % count) for g in range(count)]

    def far_part(i, after=()):
        array, block = far_q[i]
        return attend((tie(array, *after), block, 0), near_kv, far_kv, chunks[i][1], f"far{i}")

    def near_part(i, after):
        first, rows = chunks[i]
        return attend((tie(own, *after), first // rows, 4), near_kv, far_kv, rows, f"near{i}")

    def finish(i, back):
        first, _ = chunks[i]
        return update(near, levels, back, latent, mod_table, fresh_noise, first, f"update{i}")

    beside = lambda x, y: jnp.concatenate([x, y], axis=2)
    of_far0 = far_part(0)
    of_near0 = near_part(0, [of_far0, last_q])
    of_far1 = far_part(1, [of_near0])
    returned0, returned1 = across(of_far0), across(of_far1)

    def third_stage(x, y):
        return within(beside(x, y)), near_part(1, [])

    back0, of_near1 = fenced(third_stage, of_near0, tie(returned0, of_far1))
    denoised0 = finish(0, back0)

    def fourth_stage(x, y, z):
        return within(beside(x, y)), lax.ppermute(z, "queue", ring)

    back1, shifted0 = fenced(fourth_stage, of_near1, returned1, denoised0)
    denoised1 = finish(1, back1)
    shifted1 = lax.ppermute(denoised1, "queue", ring)
    out = tie(jnp.pad(shifted0, ((0, ROWS - shifted0.shape[0]), (0, 0))), denoised1)
    return lax.dynamic_update_slice(out, shifted1, (shifted0.shape[0], 0))[None]


def solution(mesh):
    return jax.shard_map(
        on_device,
        mesh=mesh,
        in_specs=(
            P("queue", "seq", None),
            P("queue", "seq", None),
            P("queue", "seq", None),
            P("queue", "seq", None),
            P(),
            P("queue"),
            P("seq", None),
        ),
        out_specs=P("queue", "seq", None),
        check_vma=False,
    )
```

time: 218 us -> 207 us (0.950)
  waiting for transfers between devices: 51.3 us -> 45.1 us
  Pallas kernels: 52.2 us -> 49.3 us
  starting transfers between devices: 29.8 us -> 27.1 us
    all_to_all x2 -> x0, waiting for transfers between devices: 13.9 us -> none  [on_device(): back.append(lax.all_to_all(tie(m, *back), 'seq', 0, 0))]
    all_to_all x2 -> x0, starting transfers between devices: 13.6 us -> none  [on_device(): back.append(lax.all_to_all(tie(m, *back), 'seq', 0, 0))]
    ppermute x2, waiting for transfers between devices: 26.7 us -> 36.1 us  [the longest x1 21.4 us: on_device(): shifted1 = lax.ppermute(denoised1, 'queue', ring)]
    all_to_all x1 -> x2, waiting for transfers between devices: 10.7 us -> 3.03 us  [within(): return lax.all_to_all(value, 'seq', 0, 0, axis_index_groups=GROUPS8)]
    all_to_all x1 -> x2, starting transfers between devices: 4.84 us -> 12.1 us  [within(): return lax.all_to_all(value, 'seq', 0, 0, axis_index_groups=GROUPS8)]
    ppermute x2 -> x5, starting transfers between devices: 7.83 us -> 14.8 us  [across(): lax.ppermute(value, 'seq', [(s, (s + HALF) % (2 * HALF)) for s in range(2...]
    ppermute x2 -> x5, waiting for transfers between devices: 0.01 us -> 6.02 us  [across(): lax.ppermute(value, 'seq', [(s, (s + HALF) % (2 * HALF)) for s in range(2...]
    ppermute x2, starting transfers between devices: 3.55 us -> 0.21 us  [the longest x1 0.2 us: fourth_stage(): return (within(beside(x, y)), lax.ppermute(z, 'queue', ring))]
  transfers between devices with their start and end apart: 7 -> 9, of which waited for: 5 -> 4; matrix products, arithmetic and copies ran while one was open for 1% -> 3% of each run, Pallas kernels for 19% -> 21%
where the time goes in v3:
time: 207 us; the launch traced here: 206 us
  blocking collectives  76.6 us (37%)
  Pallas kernels  49.3 us (24%)
  waiting for transfers between devices  45.1 us (22%)
  starting transfers between devices  27.1 us (13%)
  local copies, waits for them, and re-layouts  4.48 us (2%)
  other arithmetic  2.99 us (1%)
    all_to_all x3, blocking collectives, within(): return lax.all_to_all(value, 'seq', 0, 0, axis_index_groups=GROUPS8)  76.6 us
    pallas_call x4, Pallas kernels, attend(): pl.pallas_call(body, grid=(2,), in_specs=[pl.BlockSpec((HALF, rows, HEAD_...  36.8 us
    ppermute x1, waiting for transfers between devices, on_device(): shifted1 = lax.ppermute(denoised1, 'queue', ring)  21.4 us
    ppermute x5, starting transfers between devices, across(): lax.ppermute(value, 'seq', [(s, (s + HALF) % (2 * HALF)) for s in range(2...  14.8 us
    ppermute x1, waiting for transfers between devices, fourth_stage(): return (within(beside(x, y)), lax.ppermute(z, 'queue', ring))  14.7 us
    all_to_all x2, starting transfers between devices, within(): return lax.all_to_all(value, 'seq', 0, 0, axis_index_groups=GROUPS8)  12.1 us
    pallas_call x3, Pallas kernels, arrange(): pl.pallas_call(body, grid_spec=pltpu.PrefetchScalarGridSpec(num_scalar_pr...  7.13 us
    ppermute x5, waiting for transfers between devices, across(): lax.ppermute(value, 'seq', [(s, (s + HALF) % (2 * HALF)) for s in range(2...  6.02 us
  transfers between devices with their start and end apart: 9, of which 4 were waited for; matrix products, arithmetic and copies ran while one was open for 3% of the time, Pallas kernels for 21%

profile of v3, /device:TPU:1, one launch (start us, length us, event | category | flops | bytes accessed | tf_op | source)
XLA Modules:
  0.0 206.3 jit_solution(1868309683466251531)
XLA Ops:
  0.0 2.8 %send0.1.refs_3_ = bf16[8,288,256]{2,1,0:T(8,128)(2,1)} custom-call(s32[1]{0:T(128)} %bitcast.2.half_ref, bf16[192,4096]{1,0:T(8,128)(2,1)} %bitcast.10, bf16[192,4096]{1,0:T(8,128)(2,1)} %bitcast.13, bf16[192,4096]{1,0:T(8,128)(2,1)} %bitcast.16), custom_call_target="tpu_custom_call" | custom-call | flops 1000 | bytes 1000 | tf_op jit(solution)/shard_map/send0/pallas_call | solution.py:52
  2.8 7.8 %collective-permute-start.1 = (bf16[8,288,256]{2,1,0:T(8,128)(2,1)}, bf16[8,288,256]{2,1,0:T(8,128)(2,1)}, u32[]{:S(2)}, u32[]{:S(2)}) collective-permute-start(bf16[8,288,256]{2,1,0:T(8,128)(2,1)} %send0.1.refs_3_), channel_id=1, source_target_pairs={{0,8},{1,9},{2,10},{3,11},{4,12},{5,13},{6,14},{7,15},{8,0},{9,1},... | collective-permute-start | bytes 3538952 | tf_op jit(solution)/shard_map/ppermute | solution.py:215
  10.6 2.1 %send1.1.refs_3_ = bf16[8,288,256]{2,1,0:T(8,128)(2,1)S(1)} custom-call(s32[1]{0:T(128)} %bitcast.2.half_ref, bf16[192,4096]{1,0:T(8,128)(2,1)} %bitcast.11, bf16[192,4096]{1,0:T(8,128)(2,1)} %bitcast.14, bf16[192,4096]{1,0:T(8,128)(2,1)} %bitcast.17, bf16[8,288,256]{2,1,0:T(8,128)(2,1)} %send0.1.refs_3_), custom_call_target="tpu_custom_call" | custom-call | flops 1000 | bytes 1000 | tf_op jit(solution)/shard_map/send1/pallas_call | solution.py:52
  13.4 22.1 %conditional.5 = (bf16[8,288,256]{2,1,0:T(8,128)(2,1)S(1)}) conditional(s32[]{:T(128)} %bitcast.1, () %tuple.55, bf16[8,288,256]{2,1,0:T(8,128)(2,1)S(1)} %send1.1.refs_3_), branch_computations={%region_0.1_spmd, %region_1.2_spmd} | conditional | bytes 2359304 | solution.py:234
  13.4 22.1 %all_to_all.20 = bf16[8,288,256]{2,1,0:T(8,128)(2,1)S(1)} all-to-all(bf16[8,288,256]{2,1,0:T(8,128)(2,1)S(1)} %param.1), channel_id=1, replica_groups={{0,1,2,3,4,5,6,7},{8,9,10,11,12,13,14,15},{16,17,18,19,20,21,22,23},{24..., dimensions={0} | all-to-all | bytes 2359296 | tf_op jit(solution)/shard_map/cond/branch_1_fun/all_to_all | solution.py:219
  35.5 0.9 slice.8
  36.5 0.0 collective-permute-start.2
  36.5 2.2 %keep.1 = bf16[8,192,768]{2,1,0:T(8,128)(2,1)S(1)} custom-call(s32[1]{0:T(128)} %bitcast.2.half_ref, bf16[192,4096]{1,0:T(8,128)(2,1)} %bitcast.12, bf16[192,4096]{1,0:T(8,128)(2,1)} %bitcast.15, bf16[192,4096]{1,0:T(8,128)(2,1)} %bitcast.18, bf16[8,288,256]{2,1,0:T(8,128)(2,1)S(1)} %send1.1.refs_3_), custom_call_target="tpu_custom_call" | custom-call | flops 1000 | bytes 1000 | tf_op jit(solution)/shard_map/keep/pallas_call | solution.py:52
  38.7 0.8 slice.9
  39.5 34.6 %conditional.6 = (bf16[8,192,768]{2,1,0:T(8,128)(2,1)}, bf16[1536,768]{1,0:T(8,128)(2,1)S(1)}) conditional(s32[]{:T(128)} %bitcast.1, () %tuple.54, bf16[8,192,768]{2,1,0:T(8,128)(2,1)S(1)} %keep.1), branch_computations={%region_2.3_spmd, %region_3.4_spmd} | conditional | bytes 9437200 | solution.py:234
  39.5 33.0 %all_to_all.21 = bf16[8,192,768]{2,1,0:T(8,128)(2,1)} all-to-all(bf16[8,192,768]{2,1,0:T(8,128)(2,1)S(1)} %param.3), channel_id=1, replica_groups={{0,1,2,3,4,5,6,7},{8,9,10,11,12,13,14,15},{16,17,18,19,20,21,22,23},{24..., dimensions={0} | all-to-all | bytes 4718592 | tf_op jit(solution)/shard_map/cond/branch_1_fun/all_to_all | solution.py:219
  72.5 1.7 copy.13
  74.1 5.9 %collective-permute-start.3 = (bf16[8,96,256]{2,1,0:T(8,128)(2,1)}, bf16[8,96,256]{2,1,0:T(8,128)(2,1)}, u32[]{:S(2)}, u32[]{:S(2)}) collective-permute-start(bf16[8,96,256]{2,1,0:T(8,128)(2,1)} %slice.9), channel_id=1, source_target_pairs={{0,8},{1,9},{2,10},{3,11},{4,12},{5,13},{6,14},{7,15},{8,0},{9,1},... | collective-permute-start | bytes 1179656 | tf_op jit(solution)/shard_map/ppermute | solution.py:215
  80.1 0.0 collective-permute-done.1
  80.1 21.5 %conditional.7 = (bf16[8,288,256]{2,1,0:T(8,128)(2,1)S(1)}) conditional(s32[]{:T(128)} %bitcast.1, () %tuple.57, bf16[8,288,256]{2,1,0:T(8,128)(2,1)} %collective-permute-done.1), branch_computations={%region_4.5_spmd, %region_5.6_spmd} | conditional | bytes 2359304 | solution.py:234
  80.1 21.5 %all_to_all.22 = bf16[8,288,256]{2,1,0:T(8,128)(2,1)S(1)} all-to-all(bf16[8,288,256]{2,1,0:T(8,128)(2,1)} %param.5), channel_id=1, replica_groups={{0,1,2,3,4,5,6,7},{8,9,10,11,12,13,14,15},{16,17,18,19,20,21,22,23},{24..., dimensions={0} | all-to-all | bytes 2359296 | tf_op jit(solution)/shard_map/cond/branch_1_fun/all_to_all | solution.py:219
  101.6 0.0 collective-permute-done.2.k1.v1
  101.6 9.3 %far0.1 = bf16[8,96,256]{2,1,0:T(8,128)(2,1)} custom-call(bf16[8,288,256]{2,1,0:T(8,128)(2,1)S(1)} %get-tuple-element.83.q_ref.k0.v0, bf16[1536,768]{1,0:T(8,128)(2,1)S(1)} %get-tuple-element.60.kl.vl, bf16[1536,768]{1,0:T(8,128)(2,1)S(1)} %get-tuple-element.60.kl.vl, bf16[8,288,256]{2,1,0:T(8,128)(2,1)S(1)} %get-tuple-element.83.q_ref.k0.v0, ...), custom_call_target="tpu_custom_call" | custom-call | flops 1000 | bytes 1000 | tf_op jit(solution)/shard_map/far0/pallas_call | solution.py:140
  110.9 0.0 collective-permute-start.4
  110.9 6.0 %collective-permute-done.3.q_ref = bf16[8,96,256]{2,1,0:T(8,128)(2,1)} collective-permute-done((bf16[8,96,256]{2,1,0:T(8,128)(2,1)}, bf16[8,96,256]{2,1,0:T(8,128)(2,1)}, u32[]{:S(2)}, u32[]{:S(2)}) %collective-permute-start.3) | collective-permute-done | bytes 393248 | tf_op jit(solution)/shard_map/ppermute | solution.py:215
  116.9 8.7 %near0.1 = bf16[8,96,256]{2,1,0:T(8,128)(2,1)S(1)} custom-call(bf16[8,192,768]{2,1,0:T(8,128)(2,1)} %get-tuple-element.62.q_ref, bf16[1536,768]{1,0:T(8,128)(2,1)S(1)} %get-tuple-element.60.kl.vl, bf16[1536,768]{1,0:T(8,128)(2,1)S(1)} %get-tuple-element.60.kl.vl, bf16[8,288,256]{2,1,0:T(8,128)(2,1)S(1)} %get-tuple-element.83.q_ref.k0.v0, ...), custom_call_target="tpu_custom_call" | custom-call | flops 1000 | bytes 1000 | tf_op jit(solution)/shard_map/near0/pallas_call | solution.py:140
  125.7 9.4 %far1.1 = bf16[8,96,256]{2,1,0:T(8,128)(2,1)} custom-call(bf16[8,96,256]{2,1,0:T(8,128)(2,1)} %collective-permute-done.3.q_ref, bf16[1536,768]{1,0:T(8,128)(2,1)S(1)} %get-tuple-element.60.kl.vl, bf16[1536,768]{1,0:T(8,128)(2,1)S(1)} %get-tuple-element.60.kl.vl, bf16[8,288,256]{2,1,0:T(8,128)(2,1)S(1)} %get-tuple-element.83.q_ref.k0.v0, ...), custom_call_target="tpu_custom_call" | custom-call | flops 1000 | bytes 1000 | tf_op jit(solution)/shard_map/far1/pallas_call | solution.py:140
  135.0 1.0 collective-permute-start.5
  136.1 0.0 collective-permute-done.4
  136.1 20.2 %conditional.8 = (bf16[8,96,512]{2,1,0:T(8,128)(2,1)}, bf16[8,96,256]{2,1,0:T(8,128)(2,1)}) conditional(s32[]{:T(128)} %bitcast.1, () %tuple.53, (bf16[8,96,256]{2,1,0:T(8,128)(2,1)S(1)}, bf16[8,96,256]{2,1,0:T(8,128)(2,1)S(1)}, bf16[8,192,768]{2,1,0:T(8,128)(2,1)}, bf16[1536,768]{1,0:T(8,128)(2,1)S(1)}, bf16[8,288,256]{2,1,0:T(8,128)(2,1)S(1)}, ...), branch_computations={%region_6.7_spmd, %region_7.8_spmd} | conditional | flops 1573864 | bytes 3933208 | solution.py:234
  136.1 0.9 pad_maximum_fusion
  137.0 6.8 %all-to-all-start.3 = ((bf16[8,96,512]{2,1,0:T(8,128)(2,1)}), bf16[8,96,512]{2,1,0:T(8,128)(2,1)}, u32[]{:S(2)}, u32[]{:S(2)}) async-start(bf16[8,96,512]{2,1,0:T(8,128)(2,1)} %pad_maximum_fusion), calls=%async_computation.3 | async-start | bytes 1572864 | tf_op jit(solution)/shard_map/cond/branch_1_fun/all_to_all | solution.py:219
  143.8 9.4 %near1.1 = bf16[8,96,256]{2,1,0:T(8,128)(2,1)} custom-call(bf16[8,192,768]{2,1,0:T(8,128)(2,1)} %get-tuple-element.37.q_ref, bf16[1536,768]{1,0:T(8,128)(2,1)S(1)} %get-tuple-element.38.kl.vl, bf16[1536,768]{1,0:T(8,128)(2,1)S(1)} %get-tuple-element.38.kl.vl, bf16[8,288,256]{2,1,0:T(8,128)(2,1)S(1)} %get-tuple-element.39.k0.v0, ...), custom_call_target="tpu_custom_call" | custom-call | flops 1000 | bytes 1000 | tf_op jit(solution)/shard_map/cond/branch_1_fun/near1/pallas_call | solution.py:140
  153.2 3.0 %all-to-all-done.3 = bf16[8,96,512]{2,1,0:T(8,128)(2,1)} async-done(((bf16[8,96,512]{2,1,0:T(8,128)(2,1)}), bf16[8,96,512]{2,1,0:T(8,128)(2,1)}, u32[]{:S(2)}, u32[]{:S(2)}) %all-to-all-start.3) | async-done | bytes 786464 | tf_op jit(solution)/shard_map/cond/branch_1_fun/all_to_all | solution.py:219
  156.2 2.1 %update0.1 = bf16[96,4096]{1,0:T(8,128)(2,1)S(1)} custom-call(s32[1]{0:T(128)} %bitcast.2.half_ref, s32[1]{0:T(128)S(6)} %copy.25.levels, bf16[8,96,512]{2,1,0:T(8,128)(2,1)} %get-tuple-element.66.mixed_ref, bf16[192,4096]{1,0:T(8,128)(2,1)} %bitcast.19, f32[50,2,4096]{2,1,0:T(2,128)} %mod_ref.3, bf16[192,4096]{1,0:T(8,128)(2,1)} %fresh_ref.3), custom_call_target="tpu_custom_call" | custom-call | flops 1000 | bytes 1000 | tf_op jit(solution)/shard_map/update0/pallas_call | solution.py:194
  158.3 0.0 collective-permute-done.5
  158.3 22.3 %conditional.9 = (bf16[8,96,512]{2,1,0:T(8,128)(2,1)}, bf16[192,4096]{1,0:T(8,128)(2,1)S(1)}) conditional(s32[]{:T(128)} %bitcast.1, () %tuple.52, (bf16[8,96,256]{2,1,0:T(8,128)(2,1)}, bf16[8,96,256]{2,1,0:T(8,128)(2,1)}, bf16[96,4096]{1,0:T(8,128)(2,1)S(1)}) %tuple.64), branch_computations={%region_8.9_spmd, %region_9.10_spmd} | conditional | flops 1572864 | bytes 9437274 | solution.py:234
  158.3 0.2 collective-permute-start
  158.5 2.0 pad_maximum_fusion.1
  160.6 5.2 %all-to-all-start.4 = ((bf16[8,96,512]{2,1,0:T(8,128)(2,1)}), bf16[8,96,512]{2,1,0:T(8,128)(2,1)}, u32[]{:S(2)}, u32[]{:S(2)}) async-start(bf16[8,96,512]{2,1,0:T(8,128)(2,1)} %pad_maximum_fusion.1), calls=%async_computation.4 | async-start | bytes 1572864 | tf_op jit(solution)/shard_map/cond/branch_1_fun/all_to_all | solution.py:219
  165.8 14.7 %collective-permute-done = bf16[96,4096]{1,0:T(8,128)(2,1)S(1)} collective-permute-done((bf16[96,4096]{1,0:T(8,128)(2,1)S(1)}, bf16[96,4096]{1,0:T(8,128)(2,1)S(1)}, u32[]{:S(2)}, u32[]{:S(2)}) %collective-permute-start) | collective-permute-done | bytes 786464 | tf_op jit(solution)/shard_map/cond/branch_1_fun/ppermute | solution.py:306
  180.5 0.1 pad.9
  180.7 0.0 all-to-all-done.4
  180.7 0.0 copy-start
  180.7 3.3 %update1.1 = bf16[96,4096]{1,0:T(8,128)(2,1)} custom-call(s32[1]{0:T(128)} %bitcast.2.half_ref, s32[1]{0:T(128)S(6)} %copy.25.levels, bf16[8,96,512]{2,1,0:T(8,128)(2,1)} %get-tuple-element.68.mixed_ref, bf16[192,4096]{1,0:T(8,128)(2,1)} %bitcast.20, f32[50,2,4096]{2,1,0:T(2,128)} %mod_ref.3, bf16[192,4096]{1,0:T(8,128)(2,1)} %fresh_ref.3), custom_call_target="tpu_custom_call" | custom-call | flops 1000 | bytes 1000 | tf_op jit(solution)/shard_map/update1/pallas_call | solution.py:194
  184.0 0.0 copy-done
  184.0 0.0 collective-permute-start.6
  184.0 21.4 %collective-permute-done.6 = bf16[96,4096]{1,0:T(8,128)(2,1)S(1)} collective-permute-done((bf16[96,4096]{1,0:T(8,128)(2,1)}, bf16[96,4096]{1,0:T(8,128)(2,1)S(1)}, u32[]{:S(2)}, u32[]{:S(2)}) %collective-permute-start.6) | collective-permute-done | bytes 786464 | tf_op jit(solution)/shard_map/ppermute | solution.py:310
  205.4 0.9 bitcast_dynamic-update-slice_fusion
Async XLA Ops:
  2.8 77.2 %collective-permute-start.1 = (bf16[8,288,256]{2,1,0:T(8,128)(2,1)}, bf16[8,288,256]{2,1,0:T(8,128)(2,1)}, u32[]{:S(2)}, u32[]{:S(2)}) collective-permute-start(bf16[8,288,256]{2,1,0:T(8,128)(2,1)} %send0.1.refs_3_), channel_id=1, source_target_pairs={{0,8},{1,9},{2,10},{3,11},{4,12},{5,13},{6,14},{7,15},{8,0},{9,1},... | collective-permute-start | bytes 3538952 | tf_op jit(solution)/shard_map/ppermute | solution.py:215
  36.5 65.1 %collective-permute-start.2 = (bf16[8,192,256]{2,1,0:T(8,128)(2,1)}, bf16[8,192,256]{2,1,0:T(8,128)(2,1)}, u32[]{:S(2)}, u32[]{:S(2)}) collective-permute-start(bf16[8,192,256]{2,1,0:T(8,128)(2,1)} %slice.8), channel_id=1, source_target_pairs={{0,8},{1,9},{2,10},{3,11},{4,12},{5,13},{6,14},{7,15},{8,0},{9,1},... | collective-permute-start | bytes 2359304 | tf_op jit(solution)/shard_map/ppermute | solution.py:215
  74.1 42.8 %collective-permute-start.3 = (bf16[8,96,256]{2,1,0:T(8,128)(2,1)}, bf16[8,96,256]{2,1,0:T(8,128)(2,1)}, u32[]{:S(2)}, u32[]{:S(2)}) collective-permute-start(bf16[8,96,256]{2,1,0:T(8,128)(2,1)} %slice.9), channel_id=1, source_target_pairs={{0,8},{1,9},{2,10},{3,11},{4,12},{5,13},{6,14},{7,15},{8,0},{9,1},... | collective-permute-start | bytes 1179656 | tf_op jit(solution)/shard_map/ppermute | solution.py:215
  110.9 25.1 %collective-permute-start.4 = (bf16[8,96,256]{2,1,0:T(8,128)(2,1)}, bf16[8,96,256]{2,1,0:T(8,128)(2,1)S(1)}, u32[]{:S(2)}, u32[]{:S(2)}) collective-permute-start(bf16[8,96,256]{2,1,0:T(8,128)(2,1)} %far0.1), channel_id=1, source_target_pairs={{0,8},{1,9},{2,10},{3,11},{4,12},{5,13},{6,14},{7,15},{8,0},{9,1},... | collective-permute-start | bytes 1179656 | tf_op jit(solution)/shard_map/ppermute | solution.py:215
  135.0 23.3 %collective-permute-start.5 = (bf16[8,96,256]{2,1,0:T(8,128)(2,1)}, bf16[8,96,256]{2,1,0:T(8,128)(2,1)}, u32[]{:S(2)}, u32[]{:S(2)}) collective-permute-start(bf16[8,96,256]{2,1,0:T(8,128)(2,1)} %far1.1), channel_id=1, source_target_pairs={{0,8},{1,9},{2,10},{3,11},{4,12},{5,13},{6,14},{7,15},{8,0},{9,1},... | collective-permute-start | bytes 1179656 | tf_op jit(solution)/shard_map/ppermute | solution.py:215
  137.0 19.2 %all-to-all-start.3 = ((bf16[8,96,512]{2,1,0:T(8,128)(2,1)}), bf16[8,96,512]{2,1,0:T(8,128)(2,1)}, u32[]{:S(2)}, u32[]{:S(2)}) async-start(bf16[8,96,512]{2,1,0:T(8,128)(2,1)} %pad_maximum_fusion), calls=%async_computation.3 | async-start | bytes 1572864 | tf_op jit(solution)/shard_map/cond/branch_1_fun/all_to_all | solution.py:219
  158.3 22.2 %collective-permute-start = (bf16[96,4096]{1,0:T(8,128)(2,1)S(1)}, bf16[96,4096]{1,0:T(8,128)(2,1)S(1)}, u32[]{:S(2)}, u32[]{:S(2)}) collective-permute-start(bf16[96,4096]{1,0:T(8,128)(2,1)S(1)} %get-tuple-element.43), channel_id=1, source_target_pairs={{0,16},{16,32},{32,48},{48,64},{64,80},{80,96},{96,112},{112,128},... | collective-permute-start | bytes 2359304 | tf_op jit(solution)/shard_map/cond/branch_1_fun/ppermute | solution.py:306
  160.6 20.1 %all-to-all-start.4 = ((bf16[8,96,512]{2,1,0:T(8,128)(2,1)}), bf16[8,96,512]{2,1,0:T(8,128)(2,1)}, u32[]{:S(2)}, u32[]{:S(2)}) async-start(bf16[8,96,512]{2,1,0:T(8,128)(2,1)} %pad_maximum_fusion.1), calls=%async_computation.4 | async-start | bytes 1572864 | tf_op jit(solution)/shard_map/cond/branch_1_fun/all_to_all | solution.py:219
  180.7 3.3 %copy-start = (bf16[192,4096]{1,0:T(8,128)(2,1)}, bf16[192,4096]{1,0:T(8,128)(2,1)S(1)}, u32[]{:S(2)}) copy-start(bf16[192,4096]{1,0:T(8,128)(2,1)S(1)} %get-tuple-element.69) | copy-start | bytes 4718596
  184.0 21.4 %collective-permute-start.6 = (bf16[96,4096]{1,0:T(8,128)(2,1)}, bf16[96,4096]{1,0:T(8,128)(2,1)S(1)}, u32[]{:S(2)}, u32[]{:S(2)}) collective-permute-start(bf16[96,4096]{1,0:T(8,128)(2,1)} %update1.1), channel_id=1, source_target_pairs={{0,16},{16,32},{32,48},{48,64},{64,80},{80,96},{96,112},{112,128},... | collective-permute-start | bytes 2359304 | tf_op jit(solution)/shard_map/ppermute | solution.py:310

commit v4 on v3

--- a/solution.py
+++ b/solution.py
@@ -20,6 +20,7 @@
 NT = (((1,), (1,)), ((), ()))
 SMALL = pl.CostEstimate(flops=1000, bytes_accessed=1000, transcendentals=0)
 PARAMS = pltpu.CompilerParams(vmem_limit_bytes=60_000_000)
+SLIM = pltpu.CompilerParams(vmem_limit_bytes=24 << 20)
 
 
 def arrange(arrays, half, layout, rows, width, name, after=()):
@@ -66,22 +67,25 @@
     )(half, *[arrays[which] for which, *_ in layout], *after)
 
 
-def attend_body(q_ref, kl_ref, kr_ref, vl_ref, vr_ref, o_ref, *s_refs):
+def attend_body(q_ref, keys, values, carried, o_refs, s_refs):
     chunk = 512
     tile = s_refs[0].shape[0]
     queries = q_ref[...].reshape(-1, HEAD_DIM)
-    side = kl_ref.shape[0]
+    carried = [ref[...].reshape(-1, HEAD_DIM) for ref in carried]
+    side = keys[0].shape[0]
     tiles = len(s_refs)
     states = [{} for _ in range(tiles)]
-    outs = []
+    outs = [[] for _ in o_refs]
 
     def add(state, name, part, op):
         state[name] = op(state[name], part) if name in state else part
 
     def scores_of(t, i, at):
-        keys = (kl_ref, kr_ref)[i][at : at + chunk, :]
         scores = lax.dot_general(
-            queries[t * tile : (t + 1) * tile], keys, NT, preferred_element_type=jnp.float32
+            queries[t * tile : (t + 1) * tile],
+            keys[i][at : at + chunk, :],
+            NT,
+            preferred_element_type=jnp.float32,
         )
         s_refs[t][:, i * side + at : i * side + at + chunk] = scores
         for j in range(0, chunk, 128):
@@ -94,13 +98,13 @@
             add(states[t], "total", powers[:, j : j + 128], jnp.add)
         product = jnp.dot(
             powers.astype(jnp.bfloat16),
-            (vl_ref, vr_ref)[i][at : at + chunk, :],
+            values[i][at : at + chunk, :],
             preferred_element_type=jnp.float32,
         )
         add(states[t], "mixed", product, jnp.add)
 
     for phase in range(tiles + 1):
-        for i in range(2):
+        for i in range(len(keys)):
             for at in range(0, side, chunk):
                 if phase < tiles:
                     scores_of(phase, i, at)
@@ -108,53 +112,88 @@
                     mix(phase - 1, i, at)
         if phase < tiles:
             state = states[phase]
-            state["shift"] = jnp.max(state["largest"], axis=1, keepdims=True) * EXPONENT
+            shift = jnp.max(state["largest"], axis=1, keepdims=True) * EXPONENT
+            if carried:
+                mine = slice(phase * tile, (phase + 1) * tile)
+                before = carried[2][mine]
+                shift = jnp.maximum(jnp.broadcast_to(shift, before.shape), before)
+                rescale = jnp.exp2(before - shift)
+                state["mixed"] = carried[0][mine] * rescale
+                state["total"] = carried[1][mine] * rescale
+                shift = shift[:, :1]
+            state["shift"] = shift
         if phase > 0:
             state = states[phase - 1]
-            total = jnp.sum(state["total"], axis=1, keepdims=True)
-            outs.append((state["mixed"] / total).astype(jnp.bfloat16))
-    o_ref[...] = jnp.concatenate(outs).reshape(o_ref.shape)
-
-
-def attend(queries, near, far, rows, name, after=()):
+            if len(o_refs) == 3:
+                shift = jnp.broadcast_to(state["shift"], (tile, HEAD_DIM))
+                results = (state["mixed"], state["total"], shift)
+            else:
+                total = jnp.sum(state["total"], axis=1, keepdims=True)
+                results = ((state["mixed"] / total).astype(jnp.bfloat16),)
+            for out, result in zip(outs, results):
+                out.append(result)
+    for ref, out in zip(o_refs, outs):
+        ref[...] = jnp.concatenate(out).reshape(ref.shape)
+
+
+def attend(queries, near, far, rows, name, carried=(), partial=False):
     array, row_block, start = queries
-    side = near.shape[0]
+    side = HALF * ROWS
     tile = 256
-    extra = list(after)
-
-    def body(q_ref, kl, vl, k0, v0, k1, v1, *refs):
-        o_ref, k_ref, v_ref, *s_refs = refs[len(extra) :]
-
-        def choose(k, v):
-            k_ref[...] = k[...].reshape(k_ref.shape)
-            v_ref[...] = v[...].reshape(v_ref.shape)
-
-        for h, (k, v) in enumerate(((k0, v0), (k1, v1))):
-            pl.when(pl.program_id(0) == h)(functools.partial(choose, k, v))
-        attend_body(q_ref, kl, k_ref, vl, v_ref, o_ref, *s_refs)
-
+    sides = (near is not None) + (far is not None)
     column = lambda at: pl.BlockSpec((side, HEAD_DIM), at)
-    far_columns = [
-        pl.BlockSpec((HALF, ROWS, HEAD_DIM), lambda h, at=at: (0, 0, at)) for at in range(2)
-    ]
-    return pl.pallas_call(
+    operands = []
+    if near is not None:
+        operands += [(near, column(lambda h: (0, h))), (near, column(lambda h: (0, 2 + h)))]
+    if far is not None:
+        operands += [
+            (x, pl.BlockSpec((HALF, ROWS, HEAD_DIM), lambda h, at=at: (0, 0, at)))
+            for x in far
+            for at in range(2)
+        ]
+    here = pl.BlockSpec((HALF, rows, HEAD_DIM), lambda h: (0, row_block, h))
+    plain = pl.BlockSpec((HALF, rows, HEAD_DIM), lambda h: (0, 0, h))
+    outs = 3 if partial else 1
+    kind = jnp.float32 if partial else jnp.bfloat16
+
+    def body(q_ref, *refs):
+        refs = list(refs)
+        take = lambda n: [refs.pop(0) for _ in range(n)]
+        keys, values = [], []
+        if near is not None:
+            keys += take(1)
+            values += take(1)
+        both = take(4) if far is not None else []
+        earlier = take(len(carried))
+        o_refs = take(outs)
+        if far is not None:
+            k_ref, v_ref = take(2)
+
+            def choose(k, v):
+                k_ref[...] = k[...].reshape(k_ref.shape)
+                v_ref[...] = v[...].reshape(v_ref.shape)
+
+            for h in range(2):
+                pl.when(pl.program_id(0) == h)(functools.partial(choose, *both[2 * h : 2 * h + 2]))
+            keys.append(k_ref)
+            values.append(v_ref)
+        attend_body(q_ref, keys, values, earlier, o_refs, refs)
+
+    result = pl.pallas_call(
         body,
         grid=(2,),
-        in_specs=[
-            pl.BlockSpec((HALF, rows, HEAD_DIM), lambda h: (0, row_block, start + h)),
-            column(lambda h: (0, h)),
-            column(lambda h: (0, 2 + h)),
-        ]
-        + far_columns * 2
-        + [pl.BlockSpec(memory_space=pl.ANY)] * len(extra),
-        out_specs=pl.BlockSpec((HALF, rows, HEAD_DIM), lambda h: (0, 0, h)),
-        out_shape=jax.ShapeDtypeStruct((HALF, rows, WIDE), jnp.bfloat16),
-        scratch_shapes=[pltpu.VMEM((side, HEAD_DIM), jnp.bfloat16)] * 2
-        + [pltpu.VMEM((tile, 2 * side), jnp.float32)] * (HALF * rows // tile),
-        compiler_params=PARAMS,
+        in_specs=[pl.BlockSpec((HALF, rows, HEAD_DIM), lambda h: (0, row_block, start + h))]
+        + [spec for _, spec in operands]
+        + [here] * len(carried),
+        out_specs=[plain] * outs,
+        out_shape=[jax.ShapeDtypeStruct((HALF, rows, WIDE), kind)] * outs,
+        scratch_shapes=([] if far is None else [pltpu.VMEM((side, HEAD_DIM), jnp.bfloat16)] * 2)
+        + [pltpu.VMEM((tile, sides * side), jnp.float32)] * (HALF * rows // tile),
+        compiler_params=SLIM,
         cost_estimate=SMALL,
         name=name,
-    )(array, near, near, far[0], far[0], far[1], far[1], *extra)
+    )(array, *[x for x, _ in operands], *carried)
+    return result if partial else result[0]
 
 
 def update_body(half_ref, levels, mixed_ref, latent_ref, mod_ref, fresh_ref, o_ref):
@@ -205,7 +244,7 @@
             out_specs=pl.BlockSpec((tile, FEATURES), lambda i, h, m: (i, 0)),
         ),
         out_shape=jax.ShapeDtypeStruct((rows, FEATURES), jnp.bfloat16),
-        compiler_params=PARAMS,
+        compiler_params=SLIM,
         cost_estimate=SMALL,
         name=name,
     )(half, levels, mixed, latent, mod_table, fresh)
@@ -272,7 +311,10 @@
     far1 = across(sent1[:, :ROWS])
     own = fenced(within, tie(own, sent1))
     last_q = across(tie(sent1[:, ROWS:], own))
-    far0 = fenced(within, tie(far0, own))
+    def second_stage(x, y):
+        return within(x), attend((y, 0, 4), flat(y), None, ROWS, "near", partial=True)
+
+    far0, early = fenced(second_stage, tie(far0, own), own)
     far_q = [(far0, ROWS // part), (last_q, 0)]
 
     near_kv, far_kv = flat(own), (far0, far1)
@@ -284,7 +326,8 @@
 
     def near_part(i, after):
         first, rows = chunks[i]
-        return attend((tie(own, *after), first // rows, 4), near_kv, far_kv, rows, f"near{i}")
+        queries = (tie(own, *after), first // rows, 4)
+        return attend(queries, None, far_kv, rows, f"near{i}", early)
 
     def finish(i, back):
         first, _ = chunks[i]
@@ -303,10 +346,9 @@
     denoised0 = finish(0, back0)
 
     def fourth_stage(x, y, z):
-        return within(beside(x, y)), lax.ppermute(z, "queue", ring)
-
-    back1, shifted0 = fenced(fourth_stage, of_near1, returned1, denoised0)
-    denoised1 = finish(1, back1)
+        return finish(1, within(beside(x, y))), lax.ppermute(z, "queue", ring)
+
+    denoised1, shifted0 = fenced(fourth_stage, of_near1, returned1, denoised0)
     shifted1 = lax.ppermute(denoised1, "queue", ring)
     out = tie(jnp.pad(shifted0, ((0, ROWS - shifted0.shape[0]), (0, 0))), denoised1)
     return lax.dynamic_update_slice(out, shifted1, (shifted0.shape[0], 0))[None]

time: 207 us -> 202 us (0.976)
  blocking collectives: 76.6 us -> 55 us
  waiting for transfers between devices: 45.1 us -> 52.7 us
  starting transfers between devices: 27.1 us -> 31.9 us
  Pallas kernels: 49.3 us -> 52.8 us
    all_to_all x2 -> x3, waiting for transfers between devices: 3.03 us -> 25.6 us  [within(): return lax.all_to_all(value, 'seq', 0, 0, axis_index_groups=GROUPS8)]
    all_to_all x3 -> x2, blocking collectives: 76.6 us -> 55 us  [within(): return lax.all_to_all(value, 'seq', 0, 0, axis_index_groups=GROUPS8)]
    ppermute x1, waiting for transfers between devices: 14.7 us -> 1.64 us  [fourth_stage(): return (finish(1, within(beside(x, y))), lax.ppermute(z, 'queue', ring))]
    all_to_all x2 -> x3, starting transfers between devices: 12.1 us -> 16.5 us  [within(): return lax.all_to_all(value, 'seq', 0, 0, axis_index_groups=GROUPS8)]
    pallas_call x4 -> x5, Pallas kernels: 36.8 us -> 40.3 us  [attend(): pl.pallas_call(body, grid=(2,), in_specs=[pl.BlockSpec((HALF, rows, HEAD_...]
    ppermute x1, waiting for transfers between devices: 21.4 us -> 18.7 us  [on_device(): shifted1 = lax.ppermute(denoised1, 'queue', ring)]
    pad x1, local copies, waits for them, and re-layouts: 0.13 us -> 2.42 us  [on_device(): jnp.pad(shifted0, ((0, ROWS - shifted0.shape[0]), (0, 0)))]
  transfers between devices with their start and end apart: 9 -> 10, of which waited for: 4 -> 6; matrix products, arithmetic and copies ran while one was open for 3% -> 3% of each run, Pallas kernels for 21% -> 25%
where the time goes in v4:
time: 202 us; the launch traced here: 201 us
  blocking collectives  55 us (27%)
  Pallas kernels  52.8 us (26%)
  waiting for transfers between devices  52.7 us (26%)
  starting transfers between devices  31.9 us (16%)
  local copies, waits for them, and re-layouts  5.86 us (3%)
  other arithmetic  2.04 us (1%)
    all_to_all x2, blocking collectives, within(): return lax.all_to_all(value, 'seq', 0, 0, axis_index_groups=GROUPS8)  55 us
    pallas_call x5, Pallas kernels, attend(): pl.pallas_call(body, grid=(2,), in_specs=[pl.BlockSpec((HALF, rows, HEAD_...  40.3 us
    all_to_all x3, waiting for transfers between devices, within(): return lax.all_to_all(value, 'seq', 0, 0, axis_index_groups=GROUPS8)  25.6 us
    ppermute x1, waiting for transfers between devices, on_device(): shifted1 = lax.ppermute(denoised1, 'queue', ring)  18.7 us
    all_to_all x3, starting transfers between devices, within(): return lax.all_to_all(value, 'seq', 0, 0, axis_index_groups=GROUPS8)  16.5 us
    ppermute x5, starting transfers between devices, across(): lax.ppermute(value, 'seq', [(s, (s + HALF) % (2 * HALF)) for s in range(2...  15.2 us
    pallas_call x3, Pallas kernels, arrange(): pl.pallas_call(body, grid_spec=pltpu.PrefetchScalarGridSpec(num_scalar_pr...  7.13 us
    ppermute x5, waiting for transfers between devices, across(): lax.ppermute(value, 'seq', [(s, (s + HALF) % (2 * HALF)) for s in range(2...  6.68 us
  transfers between devices with their start and end apart: 10, of which 6 were waited for; matrix products, arithmetic and copies ran while one was open for 3% of the time, Pallas kernels for 25%

profile of v4, /device:TPU:1, one launch (start us, length us, event | category | flops | bytes accessed | tf_op | source)
XLA Modules:
  0.0 201.1 jit_solution(17507057694519452319)
XLA Ops:
  0.0 2.8 %send0.1.refs_3_ = bf16[8,288,256]{2,1,0:T(8,128)(2,1)} custom-call(s32[1]{0:T(128)} %bitcast.3.half_ref, bf16[192,4096]{1,0:T(8,128)(2,1)} %bitcast.11, bf16[192,4096]{1,0:T(8,128)(2,1)} %bitcast.14, bf16[192,4096]{1,0:T(8,128)(2,1)} %bitcast.17), custom_call_target="tpu_custom_call" | custom-call | flops 1000 | bytes 1000 | tf_op jit(solution)/shard_map/send0/pallas_call | solution.py:53
  2.8 7.8 %collective-permute-start.1 = (bf16[8,288,256]{2,1,0:T(8,128)(2,1)}, bf16[8,288,256]{2,1,0:T(8,128)(2,1)}, u32[]{:S(2)}, u32[]{:S(2)}) collective-permute-start(bf16[8,288,256]{2,1,0:T(8,128)(2,1)} %send0.1.refs_3_), channel_id=1, source_target_pairs={{0,8},{1,9},{2,10},{3,11},{4,12},{5,13},{6,14},{7,15},{8,0},{9,1},... | collective-permute-start | bytes 3538952 | tf_op jit(solution)/shard_map/ppermute | solution.py:254
  10.6 2.1 %send1.1.refs_3_ = bf16[8,288,256]{2,1,0:T(8,128)(2,1)S(1)} custom-call(s32[1]{0:T(128)} %bitcast.3.half_ref, bf16[192,4096]{1,0:T(8,128)(2,1)} %bitcast.12, bf16[192,4096]{1,0:T(8,128)(2,1)} %bitcast.15, bf16[192,4096]{1,0:T(8,128)(2,1)} %bitcast.18, bf16[8,288,256]{2,1,0:T(8,128)(2,1)} %send0.1.refs_3_), custom_call_target="tpu_custom_call" | custom-call | flops 1000 | bytes 1000 | tf_op jit(solution)/shard_map/send1/pallas_call | solution.py:53
  13.4 22.1 %conditional.5 = (bf16[8,288,256]{2,1,0:T(8,128)(2,1)S(1)}) conditional(s32[]{:T(128)} %bitcast.2, () %tuple.60, bf16[8,288,256]{2,1,0:T(8,128)(2,1)S(1)} %send1.1.refs_3_), branch_computations={%region_0.1_spmd, %region_1.2_spmd} | conditional | bytes 2359304 | solution.py:273
  13.4 22.1 %all_to_all.20 = bf16[8,288,256]{2,1,0:T(8,128)(2,1)S(1)} all-to-all(bf16[8,288,256]{2,1,0:T(8,128)(2,1)S(1)} %param.1), channel_id=1, replica_groups={{0,1,2,3,4,5,6,7},{8,9,10,11,12,13,14,15},{16,17,18,19,20,21,22,23},{24..., dimensions={0} | all-to-all | bytes 2359296 | tf_op jit(solution)/shard_map/cond/branch_1_fun/all_to_all | solution.py:258
  35.5 0.1 slice.8
  35.6 0.1 collective-permute-start.2
  35.7 2.2 %keep.1 = bf16[8,192,768]{2,1,0:T(8,128)(2,1)S(1)} custom-call(s32[1]{0:T(128)} %bitcast.3.half_ref, bf16[192,4096]{1,0:T(8,128)(2,1)} %bitcast.13, bf16[192,4096]{1,0:T(8,128)(2,1)} %bitcast.16, bf16[192,4096]{1,0:T(8,128)(2,1)} %bitcast.19, bf16[8,288,256]{2,1,0:T(8,128)(2,1)S(1)} %send1.1.refs_3_), custom_call_target="tpu_custom_call" | custom-call | flops 1000 | bytes 1000 | tf_op jit(solution)/shard_map/keep/pallas_call | solution.py:53
  37.9 0.8 slice.9
  38.7 34.6 %conditional.6 = (bf16[8,192,768]{2,1,0:T(8,128)(2,1)}, bf16[1536,768]{1,0:T(8,128)(2,1)S(1)}) conditional(s32[]{:T(128)} %bitcast.2, () %tuple.59, bf16[8,192,768]{2,1,0:T(8,128)(2,1)S(1)} %keep.1), branch_computations={%region_2.3_spmd, %region_3.4_spmd} | conditional | bytes 9437200 | solution.py:273
  38.7 33.0 %all_to_all.21 = bf16[8,192,768]{2,1,0:T(8,128)(2,1)} all-to-all(bf16[8,192,768]{2,1,0:T(8,128)(2,1)S(1)} %param.3), channel_id=1, replica_groups={{0,1,2,3,4,5,6,7},{8,9,10,11,12,13,14,15},{16,17,18,19,20,21,22,23},{24..., dimensions={0} | all-to-all | bytes 4718592 | tf_op jit(solution)/shard_map/cond/branch_1_fun/all_to_all | solution.py:258
  71.6 1.7 copy.13
  73.3 5.9 %collective-permute-start.3 = (bf16[8,96,256]{2,1,0:T(8,128)(2,1)}, bf16[8,96,256]{2,1,0:T(8,128)(2,1)S(1)}, u32[]{:S(2)}, u32[]{:S(2)}) collective-permute-start(bf16[8,96,256]{2,1,0:T(8,128)(2,1)} %slice.9), channel_id=1, source_target_pairs={{0,8},{1,9},{2,10},{3,11},{4,12},{5,13},{6,14},{7,15},{8,0},{9,1},... | collective-permute-start | bytes 1179656 | tf_op jit(solution)/shard_map/ppermute | solution.py:254
  79.2 0.0 collective-permute-done.1
  79.2 21.8 %conditional.7 = (bf16[8,288,256]{2,1,0:T(8,128)(2,1)}, f32[8,192,256]{2,1,0:T(8,128)}, f32[8,192,256]{2,1,0:T(8,128)}, f32[8,192,256]{2,1,0:T(8,128)}) conditional(s32[]{:T(128)} %bitcast.2, () %tuple.62, (bf16[8,288,256]{2,1,0:T(8,128)(2,1)}, bf16[8,192,768]{2,1,0:T(8,128)(2,1)}) %tuple.64), branch_computations={%region_4.5_spmd, %region_5.6_spmd} | conditional | flops 1000 | bytes 5898286 | solution.py:273
  79.2 5.2 %all-to-all-start.2 = ((bf16[8,288,256]{2,1,0:T(8,128)(2,1)}), bf16[8,288,256]{2,1,0:T(8,128)(2,1)}, u32[]{:S(2)}, u32[]{:S(2)}) async-start(bf16[8,288,256]{2,1,0:T(8,128)(2,1)} %get-tuple-element.53), calls=%async_computation.2 | async-start | bytes 2359296 | tf_op jit(solution)/shard_map/cond/branch_1_fun/all_to_all | solution.py:258
  84.4 8.9 %near.1 = (f32[8,192,256]{2,1,0:T(8,128)}, f32[8,192,256]{2,1,0:T(8,128)}, f32[8,192,256]{2,1,0:T(8,128)}) custom-call(bf16[8,192,768]{2,1,0:T(8,128)(2,1)} %get-tuple-element.54.q_ref, bf16[1536,768]{1,0:T(8,128)(2,1)} %bitcast.1.refs_0_.refs_1_, bf16[1536,768]{1,0:T(8,128)(2,1)} %bitcast.1.refs_0_.refs_1_), custom_call_target="tpu_custom_call" | custom-call | flops 1000 | bytes 1000 | tf_op jit(solution)/shard_map/cond/branch_1_fun/near/pallas_call | solution.py:182
  93.3 7.7 %all-to-all-done.2 = bf16[8,288,256]{2,1,0:T(8,128)(2,1)} async-done(((bf16[8,288,256]{2,1,0:T(8,128)(2,1)}), bf16[8,288,256]{2,1,0:T(8,128)(2,1)}, u32[]{:S(2)}, u32[]{:S(2)}) %all-to-all-start.2) | async-done | bytes 1179680 | tf_op jit(solution)/shard_map/cond/branch_1_fun/all_to_all | solution.py:258
  101.0 0.0 collective-permute-done.2.refs_4_.refs_5_.refs_2_.refs_3_
  101.0 8.8 %far0.1 = bf16[8,96,256]{2,1,0:T(8,128)(2,1)S(1)} custom-call(bf16[8,288,256]{2,1,0:T(8,128)(2,1)} %get-tuple-element.95.q_ref.refs_2_.refs_3_.refs_0_.refs_1_, bf16[1536,768]{1,0:T(8,128)(2,1)S(1)} %get-tuple-element.96.refs_0_.refs_1_, bf16[1536,768]{1,0:T(8,128)(2,1)S(1)} %get-tuple-element.96.refs_0_.refs_1_, ...), custom_call_target="tpu_custom_call" | custom-call | flops 1000 | bytes 1000 | tf_op jit(solution)/shard_map/far0/pallas_call | solution.py:182
  109.9 0.3 collective-permute-start.4
  110.1 6.7 %collective-permute-done.3.q_ref = bf16[8,96,256]{2,1,0:T(8,128)(2,1)S(1)} collective-permute-done((bf16[8,96,256]{2,1,0:T(8,128)(2,1)}, bf16[8,96,256]{2,1,0:T(8,128)(2,1)S(1)}, u32[]{:S(2)}, u32[]{:S(2)}) %collective-permute-start.3) | collective-permute-done | bytes 393248 | tf_op jit(solution)/shard_map/ppermute | solution.py:254
  116.8 6.9 %near0.1 = bf16[8,96,256]{2,1,0:T(8,128)(2,1)S(1)} custom-call(bf16[8,192,768]{2,1,0:T(8,128)(2,1)} %get-tuple-element.98.q_ref, bf16[8,288,256]{2,1,0:T(8,128)(2,1)} %get-tuple-element.95.q_ref.refs_2_.refs_3_.refs_0_.refs_1_, bf16[8,288,256]{2,1,0:T(8,128)(2,1)} %get-tuple-element.95.q_ref.refs_2_.refs_3_.refs_0_.refs_1_, ...), custom_call_target="tpu_custom_call" | custom-call | flops 1000 | bytes 1000 | tf_op jit(solution)/shard_map/near0/pallas_call | solution.py:182
  123.7 8.9 %far1.1 = bf16[8,96,256]{2,1,0:T(8,128)(2,1)S(1)} custom-call(bf16[8,96,256]{2,1,0:T(8,128)(2,1)S(1)} %collective-permute-done.3.q_ref, bf16[1536,768]{1,0:T(8,128)(2,1)S(1)} %get-tuple-element.96.refs_0_.refs_1_, bf16[1536,768]{1,0:T(8,128)(2,1)S(1)} %get-tuple-element.96.refs_0_.refs_1_, ...), custom_call_target="tpu_custom_call" | custom-call | flops 1000 | bytes 1000 | tf_op jit(solution)/shard_map/far1/pallas_call | solution.py:182
  132.5 1.1 collective-permute-start.5
  133.7 0.0 collective-permute-done.4
  133.7 0.0 copy-start
  133.7 20.2 %conditional.8 = (bf16[8,96,512]{2,1,0:T(8,128)(2,1)}, bf16[8,96,256]{2,1,0:T(8,128)(2,1)S(1)}) conditional(s32[]{:T(128)} %bitcast.2, () %tuple.58, (bf16[8,96,256]{2,1,0:T(8,128)(2,1)S(1)}, bf16[8,96,256]{2,1,0:T(8,128)(2,1)S(1)}, bf16[8,192,768]{2,1,0:T(8,128)(2,1)}, bf16[8,288,256]{2,1,0:T(8,128)(2,1)}, bf16[8,192,256]{2,1,0:T(8,128)(2,1)}, ...), branch_computations={%region_6.7_spmd, %region_7.8_spmd} | conditional | flops 1573864 | bytes 3933208 | solution.py:273
  133.7 1.0 pad_maximum_fusion
  134.7 6.8 %all-to-all-start.3 = ((bf16[8,96,512]{2,1,0:T(8,128)(2,1)}), bf16[8,96,512]{2,1,0:T(8,128)(2,1)}, u32[]{:S(2)}, u32[]{:S(2)}) async-start(bf16[8,96,512]{2,1,0:T(8,128)(2,1)} %pad_maximum_fusion), calls=%async_computation.3 | async-start | bytes 1572864 | tf_op jit(solution)/shard_map/cond/branch_1_fun/all_to_all | solution.py:258
  141.5 6.9 %near1.1 = bf16[8,96,256]{2,1,0:T(8,128)(2,1)S(1)} custom-call(bf16[8,192,768]{2,1,0:T(8,128)(2,1)} %get-tuple-element.60.q_ref, bf16[8,288,256]{2,1,0:T(8,128)(2,1)} %get-tuple-element.61.refs_0_.refs_1_, bf16[8,288,256]{2,1,0:T(8,128)(2,1)} %get-tuple-element.61.refs_0_.refs_1_, bf16[8,192,256]{2,1,0:T(8,128)(2,1)} %get-tuple-element.62.refs_2_.refs_3_, ...), custom_call_target="tpu_custom_call" | custom-call | flops 1000 | bytes 1000 | tf_op jit(solution)/shard_map/cond/branch_1_fun/near1/pallas_call | solution.py:182
  148.4 5.5 %all-to-all-done.3 = bf16[8,96,512]{2,1,0:T(8,128)(2,1)} async-done(((bf16[8,96,512]{2,1,0:T(8,128)(2,1)}), bf16[8,96,512]{2,1,0:T(8,128)(2,1)}, u32[]{:S(2)}, u32[]{:S(2)}) %all-to-all-start.3) | async-done | bytes 786464 | tf_op jit(solution)/shard_map/cond/branch_1_fun/all_to_all | solution.py:258
  153.9 0.0 copy-done
  153.9 2.8 %update0.1 = bf16[96,4096]{1,0:T(8,128)(2,1)} custom-call(s32[1]{0:T(128)} %bitcast.3.half_ref, s32[1]{0:T(128)S(6)} %copy.40.levels, bf16[8,96,512]{2,1,0:T(8,128)(2,1)} %get-tuple-element.105.mixed_ref, bf16[192,4096]{1,0:T(8,128)(2,1)} %bitcast.20, f32[50,2,4096]{2,1,0:T(2,128)S(1)} %copy-done, bf16[192,4096]{1,0:T(8,128)(2,1)} %fresh_ref.1), custom_call_target="tpu_custom_call" | custom-call | flops 1000 | bytes 1000 | tf_op jit(solution)/shard_map/update0/pallas_call | solution.py:233
  156.6 0.0 collective-permute-done.5
  156.6 22.4 %conditional.9 = (bf16[96,4096]{1,0:T(8,128)(2,1)S(1)}, bf16[96,4096]{1,0:T(8,128)(2,1)}, bf16[]{:T(256)}, bf16[]{:T(256)}) conditional(s32[]{:T(128)} %bitcast.2, () %tuple.57, (bf16[8,96,256]{2,1,0:T(8,128)(2,1)S(1)}, bf16[8,96,256]{2,1,0:T(8,128)(2,1)S(1)}, s32[1]{0:T(128)}, s32[1]{0:T(128)}, bf16[192,4096]{1,0:T(8,128)(2,1)}, ...), branch_computations={%region_8.9_spmd, %region_9.10_spmd} | conditional | flops 1573864 | bytes 7079000 | solution.py:273
  156.6 0.1 collective-permute-start
  156.8 1.0 pad_maximum_fusion.1
  157.8 4.6 %all-to-all-start.4 = ((bf16[8,96,512]{2,1,0:T(8,128)(2,1)}), bf16[8,96,512]{2,1,0:T(8,128)(2,1)S(1)}, u32[]{:S(2)}, u32[]{:S(2)}) async-start(bf16[8,96,512]{2,1,0:T(8,128)(2,1)} %pad_maximum_fusion.1), calls=%async_computation.4 | async-start | bytes 1572864 | tf_op jit(solution)/shard_map/cond/branch_1_fun/all_to_all | solution.py:258
  162.4 12.4 %all-to-all-done.4.mixed_ref = bf16[8,96,512]{2,1,0:T(8,128)(2,1)S(1)} async-done(((bf16[8,96,512]{2,1,0:T(8,128)(2,1)}), bf16[8,96,512]{2,1,0:T(8,128)(2,1)S(1)}, u32[]{:S(2)}, u32[]{:S(2)}) %all-to-all-start.4) | async-done | bytes 786464 | tf_op jit(solution)/shard_map/cond/branch_1_fun/all_to_all | solution.py:258
  174.8 2.6 %update1.1 = bf16[96,4096]{1,0:T(8,128)(2,1)S(1)} custom-call(s32[1]{0:T(128)} %get-tuple-element.66.half_ref, s32[1]{0:T(128)} %get-tuple-element.67.levels, bf16[8,96,512]{2,1,0:T(8,128)(2,1)S(1)} %all-to-all-done.4.mixed_ref, bf16[192,4096]{1,0:T(8,128)(2,1)} %get-tuple-element.70.latent_ref, f32[50,2,4096]{2,1,0:T(2,128)S(1)} %get-tuple-element.71.mod_ref, ...), custom_call_target="tpu_custom_call" | custom-call | flops 1000 | bytes 1000 | tf_op jit(solution)/shard_map/cond/branch_1_fun/update1/pallas_call | solution.py:233
  177.4 1.6 collective-permute-done
  179.0 0.0 collective-permute-start.6
  179.0 2.4 %pad.7 = bf16[192,4096]{1,0:T(8,128)(2,1)} pad(bf16[96,4096]{1,0:T(8,128)(2,1)} %get-tuple-element.106, bf16[]{:T(256)} %get-tuple-element.107), padding=0_96x0_0 | pad | bytes 2359298 | tf_op jit(solution)/shard_map/jit(_pad)/pad | solution.py:353
  181.5 18.7 %collective-permute-done.6 = bf16[96,4096]{1,0:T(8,128)(2,1)S(1)} collective-permute-done((bf16[96,4096]{1,0:T(8,128)(2,1)S(1)}, bf16[96,4096]{1,0:T(8,128)(2,1)S(1)}, u32[]{:S(2)}, u32[]{:S(2)}) %collective-permute-start.6) | collective-permute-done | bytes 786464 | tf_op jit(solution)/shard_map/ppermute | solution.py:352
  200.2 0.9 bitcast_dynamic-update-slice_fusion
Async XLA Ops:
  2.8 76.4 %collective-permute-start.1 = (bf16[8,288,256]{2,1,0:T(8,128)(2,1)}, bf16[8,288,256]{2,1,0:T(8,128)(2,1)}, u32[]{:S(2)}, u32[]{:S(2)}) collective-permute-start(bf16[8,288,256]{2,1,0:T(8,128)(2,1)} %send0.1.refs_3_), channel_id=1, source_target_pairs={{0,8},{1,9},{2,10},{3,11},{4,12},{5,13},{6,14},{7,15},{8,0},{9,1},... | collective-permute-start | bytes 3538952 | tf_op jit(solution)/shard_map/ppermute | solution.py:254
  35.6 65.4 %collective-permute-start.2 = (bf16[8,192,256]{2,1,0:T(8,128)(2,1)S(1)}, bf16[8,192,256]{2,1,0:T(8,128)(2,1)}, u32[]{:S(2)}, u32[]{:S(2)}) collective-permute-start(bf16[8,192,256]{2,1,0:T(8,128)(2,1)S(1)} %slice.8), channel_id=1, source_target_pairs={{0,8},{1,9},{2,10},{3,11},{4,12},{5,13},{6,14},{7,15},{8,0},{9,1},... | collective-permute-start | bytes 2359304 | tf_op jit(solution)/shard_map/ppermute | solution.py:254
  73.3 43.5 %collective-permute-start.3 = (bf16[8,96,256]{2,1,0:T(8,128)(2,1)}, bf16[8,96,256]{2,1,0:T(8,128)(2,1)S(1)}, u32[]{:S(2)}, u32[]{:S(2)}) collective-permute-start(bf16[8,96,256]{2,1,0:T(8,128)(2,1)} %slice.9), channel_id=1, source_target_pairs={{0,8},{1,9},{2,10},{3,11},{4,12},{5,13},{6,14},{7,15},{8,0},{9,1},... | collective-permute-start | bytes 1179656 | tf_op jit(solution)/shard_map/ppermute | solution.py:254
  79.2 21.8 %all-to-all-start.2 = ((bf16[8,288,256]{2,1,0:T(8,128)(2,1)}), bf16[8,288,256]{2,1,0:T(8,128)(2,1)}, u32[]{:S(2)}, u32[]{:S(2)}) async-start(bf16[8,288,256]{2,1,0:T(8,128)(2,1)} %get-tuple-element.53), calls=%async_computation.2 | async-start | bytes 2359296 | tf_op jit(solution)/shard_map/cond/branch_1_fun/all_to_all | solution.py:258
  109.9 23.8 %collective-permute-start.4 = (bf16[8,96,256]{2,1,0:T(8,128)(2,1)S(1)}, bf16[8,96,256]{2,1,0:T(8,128)(2,1)S(1)}, u32[]{:S(2)}, u32[]{:S(2)}) collective-permute-start(bf16[8,96,256]{2,1,0:T(8,128)(2,1)S(1)} %far0.1), channel_id=1, source_target_pairs={{0,8},{1,9},{2,10},{3,11},{4,12},{5,13},{6,14},{7,15},{8,0},{9,1},... | collective-permute-start | bytes 1179656 | tf_op jit(solution)/shard_map/ppermute | solution.py:254
  132.5 24.1 %collective-permute-start.5 = (bf16[8,96,256]{2,1,0:T(8,128)(2,1)S(1)}, bf16[8,96,256]{2,1,0:T(8,128)(2,1)S(1)}, u32[]{:S(2)}, u32[]{:S(2)}) collective-permute-start(bf16[8,96,256]{2,1,0:T(8,128)(2,1)S(1)} %far1.1), channel_id=1, source_target_pairs={{0,8},{1,9},{2,10},{3,11},{4,12},{5,13},{6,14},{7,15},{8,0},{9,1},... | collective-permute-start | bytes 1179656 | tf_op jit(solution)/shard_map/ppermute | solution.py:254
  133.7 20.2 %copy-start = (f32[50,2,4096]{2,1,0:T(2,128)S(1)}, f32[50,2,4096]{2,1,0:T(2,128)}, u32[]{:S(2)}) copy-start(f32[50,2,4096]{2,1,0:T(2,128)} %mod_ref.1) | copy-start | bytes 4915204
  134.7 19.2 %all-to-all-start.3 = ((bf16[8,96,512]{2,1,0:T(8,128)(2,1)}), bf16[8,96,512]{2,1,0:T(8,128)(2,1)}, u32[]{:S(2)}, u32[]{:S(2)}) async-start(bf16[8,96,512]{2,1,0:T(8,128)(2,1)} %pad_maximum_fusion), calls=%async_computation.3 | async-start | bytes 1572864 | tf_op jit(solution)/shard_map/cond/branch_1_fun/all_to_all | solution.py:258
  156.6 22.4 %collective-permute-start = (bf16[96,4096]{1,0:T(8,128)(2,1)}, bf16[96,4096]{1,0:T(8,128)(2,1)}, u32[]{:S(2)}, u32[]{:S(2)}) collective-permute-start(bf16[96,4096]{1,0:T(8,128)(2,1)} %get-tuple-element.73), channel_id=1, source_target_pairs={{0,16},{16,32},{32,48},{48,64},{64,80},{80,96},{96,112},{112,128},... | collective-permute-start | bytes 2359304 | tf_op jit(solution)/shard_map/cond/branch_1_fun/ppermute | solution.py:349
  157.8 17.0 %all-to-all-start.4 = ((bf16[8,96,512]{2,1,0:T(8,128)(2,1)}), bf16[8,96,512]{2,1,0:T(8,128)(2,1)S(1)}, u32[]{:S(2)}, u32[]{:S(2)}) async-start(bf16[8,96,512]{2,1,0:T(8,128)(2,1)} %pad_maximum_fusion.1), calls=%async_computation.4 | async-start | bytes 1572864 | tf_op jit(solution)/shard_map/cond/branch_1_fun/all_to_all | solution.py:258
  179.0 21.2 %collective-permute-start.6 = (bf16[96,4096]{1,0:T(8,128)(2,1)S(1)}, bf16[96,4096]{1,0:T(8,128)(2,1)S(1)}, u32[]{:S(2)}, u32[]{:S(2)}) collective-permute-start(bf16[96,4096]{1,0:T(8,128)(2,1)S(1)} %get-tuple-element.108), channel_id=1, source_target_pairs={{0,16},{16,32},{32,48},{48,64},{64,80},{80,96},{96,112},{112,128},... | collective-permute-start | bytes 2359304 | tf_op jit(solution)/shard_map/ppermute | solution.py:352

commit v5 on v4

--- a/solution.py
+++ b/solution.py
@@ -196,7 +196,7 @@
     return result if partial else result[0]
 
 
-def update_body(half_ref, levels, mixed_ref, latent_ref, mod_ref, fresh_ref, o_ref):
+def update_body(first, half_ref, levels, mixed_ref, latent_ref, mod_ref, fresh_ref, o_ref):
     half = half_ref[0]
     step_size = (levels[0] + 1).astype(jnp.float32) / STEPS
     squares = None
@@ -222,7 +222,9 @@
 
     @pl.when(lax.axis_index("queue") == lax.axis_size("queue") - 1)
     def _():
-        o_ref[...] = fresh_ref[...]
+        rows = o_ref.shape[0]
+        start = pl.multiple_of(first + pl.program_id(0) * rows, 16)
+        pltpu.sync_copy(fresh_ref.at[pl.ds(start, rows)], o_ref)
 
 
 def update(half, levels, mixed, latent, mod_table, fresh, first, name):
@@ -231,7 +233,7 @@
     steps = rows // tile
     plain = pl.BlockSpec((tile, FEATURES), lambda i, h, m: (first // tile + i, 0))
     return pl.pallas_call(
-        update_body,
+        functools.partial(update_body, first),
         grid_spec=pltpu.PrefetchScalarGridSpec(
             num_scalar_prefetch=2,
             grid=(steps,),
@@ -239,7 +241,7 @@
                 pl.BlockSpec((HALF, tile, 2 * WIDE), lambda i, h, m: (0, i, 0)),
                 plain,
                 pl.BlockSpec((1, 2, FEATURES), lambda i, h, m: (m[0], 0, 0)),
-                plain,
+                pl.BlockSpec(memory_space=pl.ANY),
             ],
             out_specs=pl.BlockSpec((tile, FEATURES), lambda i, h, m: (i, 0)),
         ),

time: 202 us -> 202 us (level)
  no operation moved by 1% of the time
where the time goes in v5:
time: 202 us; the launch traced here: 201 us
  blocking collectives  55 us (27%)
  waiting for transfers between devices  52.8 us (26%)
  Pallas kernels  52.6 us (26%)
  starting transfers between devices  31.9 us (16%)
  local copies, waits for them, and re-layouts  5.86 us (3%)
  other arithmetic  2.04 us (1%)
    all_to_all x2, blocking collectives, within(): return lax.all_to_all(value, 'seq', 0, 0, axis_index_groups=GROUPS8)  55 us
    pallas_call x5, Pallas kernels, attend(): pl.pallas_call(body, grid=(2,), in_specs=[pl.BlockSpec((HALF, rows, HEAD_...  40.3 us
    all_to_all x3, waiting for transfers between devices, within(): return lax.all_to_all(value, 'seq', 0, 0, axis_index_groups=GROUPS8)  25.6 us
    ppermute x1, waiting for transfers between devices, on_device(): shifted1 = lax.ppermute(denoised1, 'queue', ring)  18.7 us
    all_to_all x3, starting transfers between devices, within(): return lax.all_to_all(value, 'seq', 0, 0, axis_index_groups=GROUPS8)  16.5 us
    ppermute x5, starting transfers between devices, across(): lax.ppermute(value, 'seq', [(s, (s + HALF) % (2 * HALF)) for s in range(2...  15.2 us
    pallas_call x3, Pallas kernels, arrange(): pl.pallas_call(body, grid_spec=pltpu.PrefetchScalarGridSpec(num_scalar_pr...  7.13 us
    ppermute x5, waiting for transfers between devices, across(): lax.ppermute(value, 'seq', [(s, (s + HALF) % (2 * HALF)) for s in range(2...  6.68 us
  transfers between devices with their start and end apart: 10, of which 6 were waited for; matrix products, arithmetic and copies ran while one was open for 3% of the time, Pallas kernels for 25%

profile of v5, /device:TPU:1, one launch (start us, length us, event | category | flops | bytes accessed | tf_op | source)
XLA Modules:
  0.0 201.0 jit_solution(14451132234374566075)
XLA Ops:
  0.0 2.8 %send0.1.refs_3_ = bf16[8,288,256]{2,1,0:T(8,128)(2,1)} custom-call(s32[1]{0:T(128)} %bitcast.3.half_ref, bf16[192,4096]{1,0:T(8,128)(2,1)} %bitcast.11, bf16[192,4096]{1,0:T(8,128)(2,1)} %bitcast.14, bf16[192,4096]{1,0:T(8,128)(2,1)} %bitcast.17), custom_call_target="tpu_custom_call" | custom-call | flops 1000 | bytes 1000 | tf_op jit(solution)/shard_map/send0/pallas_call | solution.py:53
  2.8 7.8 %collective-permute-start.1 = (bf16[8,288,256]{2,1,0:T(8,128)(2,1)}, bf16[8,288,256]{2,1,0:T(8,128)(2,1)}, u32[]{:S(2)}, u32[]{:S(2)}) collective-permute-start(bf16[8,288,256]{2,1,0:T(8,128)(2,1)} %send0.1.refs_3_), channel_id=1, source_target_pairs={{0,8},{1,9},{2,10},{3,11},{4,12},{5,13},{6,14},{7,15},{8,0},{9,1},... | collective-permute-start | bytes 3538952 | tf_op jit(solution)/shard_map/ppermute | solution.py:256
  10.6 2.1 %send1.1.refs_3_ = bf16[8,288,256]{2,1,0:T(8,128)(2,1)S(1)} custom-call(s32[1]{0:T(128)} %bitcast.3.half_ref, bf16[192,4096]{1,0:T(8,128)(2,1)} %bitcast.12, bf16[192,4096]{1,0:T(8,128)(2,1)} %bitcast.15, bf16[192,4096]{1,0:T(8,128)(2,1)} %bitcast.18, bf16[8,288,256]{2,1,0:T(8,128)(2,1)} %send0.1.refs_3_), custom_call_target="tpu_custom_call" | custom-call | flops 1000 | bytes 1000 | tf_op jit(solution)/shard_map/send1/pallas_call | solution.py:53
  13.4 22.1 %conditional.5 = (bf16[8,288,256]{2,1,0:T(8,128)(2,1)S(1)}) conditional(s32[]{:T(128)} %bitcast.2, () %tuple.60, bf16[8,288,256]{2,1,0:T(8,128)(2,1)S(1)} %send1.1.refs_3_), branch_computations={%region_0.1_spmd, %region_1.2_spmd} | conditional | bytes 2359304 | solution.py:275
  13.4 22.1 %all_to_all.20 = bf16[8,288,256]{2,1,0:T(8,128)(2,1)S(1)} all-to-all(bf16[8,288,256]{2,1,0:T(8,128)(2,1)S(1)} %param.1), channel_id=1, replica_groups={{0,1,2,3,4,5,6,7},{8,9,10,11,12,13,14,15},{16,17,18,19,20,21,22,23},{24..., dimensions={0} | all-to-all | bytes 2359296 | tf_op jit(solution)/shard_map/cond/branch_1_fun/all_to_all | solution.py:260
  35.5 0.1 slice.8
  35.6 0.1 collective-permute-start.2
  35.7 2.2 %keep.1 = bf16[8,192,768]{2,1,0:T(8,128)(2,1)S(1)} custom-call(s32[1]{0:T(128)} %bitcast.3.half_ref, bf16[192,4096]{1,0:T(8,128)(2,1)} %bitcast.13, bf16[192,4096]{1,0:T(8,128)(2,1)} %bitcast.16, bf16[192,4096]{1,0:T(8,128)(2,1)} %bitcast.19, bf16[8,288,256]{2,1,0:T(8,128)(2,1)S(1)} %send1.1.refs_3_), custom_call_target="tpu_custom_call" | custom-call | flops 1000 | bytes 1000 | tf_op jit(solution)/shard_map/keep/pallas_call | solution.py:53
  37.9 0.8 slice.9
  38.7 34.6 %conditional.6 = (bf16[8,192,768]{2,1,0:T(8,128)(2,1)}, bf16[1536,768]{1,0:T(8,128)(2,1)S(1)}) conditional(s32[]{:T(128)} %bitcast.2, () %tuple.59, bf16[8,192,768]{2,1,0:T(8,128)(2,1)S(1)} %keep.1), branch_computations={%region_2.3_spmd, %region_3.4_spmd} | conditional | bytes 9437200 | solution.py:275
  38.7 33.0 %all_to_all.21 = bf16[8,192,768]{2,1,0:T(8,128)(2,1)} all-to-all(bf16[8,192,768]{2,1,0:T(8,128)(2,1)S(1)} %param.3), channel_id=1, replica_groups={{0,1,2,3,4,5,6,7},{8,9,10,11,12,13,14,15},{16,17,18,19,20,21,22,23},{24..., dimensions={0} | all-to-all | bytes 4718592 | tf_op jit(solution)/shard_map/cond/branch_1_fun/all_to_all | solution.py:260
  71.6 1.7 copy.13
  73.3 5.9 %collective-permute-start.3 = (bf16[8,96,256]{2,1,0:T(8,128)(2,1)}, bf16[8,96,256]{2,1,0:T(8,128)(2,1)S(1)}, u32[]{:S(2)}, u32[]{:S(2)}) collective-permute-start(bf16[8,96,256]{2,1,0:T(8,128)(2,1)} %slice.9), channel_id=1, source_target_pairs={{0,8},{1,9},{2,10},{3,11},{4,12},{5,13},{6,14},{7,15},{8,0},{9,1},... | collective-permute-start | bytes 1179656 | tf_op jit(solution)/shard_map/ppermute | solution.py:256
  79.2 0.0 collective-permute-done.1
  79.2 21.8 %conditional.7 = (bf16[8,288,256]{2,1,0:T(8,128)(2,1)}, f32[8,192,256]{2,1,0:T(8,128)}, f32[8,192,256]{2,1,0:T(8,128)}, f32[8,192,256]{2,1,0:T(8,128)}) conditional(s32[]{:T(128)} %bitcast.2, () %tuple.62, (bf16[8,288,256]{2,1,0:T(8,128)(2,1)}, bf16[8,192,768]{2,1,0:T(8,128)(2,1)}) %tuple.64), branch_computations={%region_4.5_spmd, %region_5.6_spmd} | conditional | flops 1000 | bytes 5898286 | solution.py:275
  79.2 5.2 %all-to-all-start.2 = ((bf16[8,288,256]{2,1,0:T(8,128)(2,1)}), bf16[8,288,256]{2,1,0:T(8,128)(2,1)}, u32[]{:S(2)}, u32[]{:S(2)}) async-start(bf16[8,288,256]{2,1,0:T(8,128)(2,1)} %get-tuple-element.53), calls=%async_computation.2 | async-start | bytes 2359296 | tf_op jit(solution)/shard_map/cond/branch_1_fun/all_to_all | solution.py:260
  84.4 8.9 %near.1 = (f32[8,192,256]{2,1,0:T(8,128)}, f32[8,192,256]{2,1,0:T(8,128)}, f32[8,192,256]{2,1,0:T(8,128)}) custom-call(bf16[8,192,768]{2,1,0:T(8,128)(2,1)} %get-tuple-element.54.q_ref, bf16[1536,768]{1,0:T(8,128)(2,1)} %bitcast.1.refs_0_.refs_1_, bf16[1536,768]{1,0:T(8,128)(2,1)} %bitcast.1.refs_0_.refs_1_), custom_call_target="tpu_custom_call" | custom-call | flops 1000 | bytes 1000 | tf_op jit(solution)/shard_map/cond/branch_1_fun/near/pallas_call | solution.py:182
  93.3 7.7 %all-to-all-done.2 = bf16[8,288,256]{2,1,0:T(8,128)(2,1)} async-done(((bf16[8,288,256]{2,1,0:T(8,128)(2,1)}), bf16[8,288,256]{2,1,0:T(8,128)(2,1)}, u32[]{:S(2)}, u32[]{:S(2)}) %all-to-all-start.2) | async-done | bytes 1179680 | tf_op jit(solution)/shard_map/cond/branch_1_fun/all_to_all | solution.py:260
  101.0 0.0 collective-permute-done.2.refs_4_.refs_5_.refs_2_.refs_3_
  101.0 8.8 %far0.1 = bf16[8,96,256]{2,1,0:T(8,128)(2,1)S(1)} custom-call(bf16[8,288,256]{2,1,0:T(8,128)(2,1)} %get-tuple-element.95.q_ref.refs_2_.refs_3_.refs_0_.refs_1_, bf16[1536,768]{1,0:T(8,128)(2,1)S(1)} %get-tuple-element.96.refs_0_.refs_1_, bf16[1536,768]{1,0:T(8,128)(2,1)S(1)} %get-tuple-element.96.refs_0_.refs_1_, ...), custom_call_target="tpu_custom_call" | custom-call | flops 1000 | bytes 1000 | tf_op jit(solution)/shard_map/far0/pallas_call | solution.py:182
  109.9 0.3 collective-permute-start.4
  110.1 6.7 %collective-permute-done.3.q_ref = bf16[8,96,256]{2,1,0:T(8,128)(2,1)S(1)} collective-permute-done((bf16[8,96,256]{2,1,0:T(8,128)(2,1)}, bf16[8,96,256]{2,1,0:T(8,128)(2,1)S(1)}, u32[]{:S(2)}, u32[]{:S(2)}) %collective-permute-start.3) | collective-permute-done | bytes 393248 | tf_op jit(solution)/shard_map/ppermute | solution.py:256
  116.8 6.9 %near0.1 = bf16[8,96,256]{2,1,0:T(8,128)(2,1)S(1)} custom-call(bf16[8,192,768]{2,1,0:T(8,128)(2,1)} %get-tuple-element.98.q_ref, bf16[8,288,256]{2,1,0:T(8,128)(2,1)} %get-tuple-element.95.q_ref.refs_2_.refs_3_.refs_0_.refs_1_, bf16[8,288,256]{2,1,0:T(8,128)(2,1)} %get-tuple-element.95.q_ref.refs_2_.refs_3_.refs_0_.refs_1_, ...), custom_call_target="tpu_custom_call" | custom-call | flops 1000 | bytes 1000 | tf_op jit(solution)/shard_map/near0/pallas_call | solution.py:182
  123.7 8.9 %far1.1 = bf16[8,96,256]{2,1,0:T(8,128)(2,1)S(1)} custom-call(bf16[8,96,256]{2,1,0:T(8,128)(2,1)S(1)} %collective-permute-done.3.q_ref, bf16[1536,768]{1,0:T(8,128)(2,1)S(1)} %get-tuple-element.96.refs_0_.refs_1_, bf16[1536,768]{1,0:T(8,128)(2,1)S(1)} %get-tuple-element.96.refs_0_.refs_1_, ...), custom_call_target="tpu_custom_call" | custom-call | flops 1000 | bytes 1000 | tf_op jit(solution)/shard_map/far1/pallas_call | solution.py:182
  132.5 1.1 collective-permute-start.5
  133.7 0.0 collective-permute-done.4
  133.7 0.0 copy-start
  133.7 20.2 %conditional.8 = (bf16[8,96,512]{2,1,0:T(8,128)(2,1)}, bf16[8,96,256]{2,1,0:T(8,128)(2,1)S(1)}) conditional(s32[]{:T(128)} %bitcast.2, () %tuple.58, (bf16[8,96,256]{2,1,0:T(8,128)(2,1)S(1)}, bf16[8,96,256]{2,1,0:T(8,128)(2,1)S(1)}, bf16[8,192,768]{2,1,0:T(8,128)(2,1)}, bf16[8,288,256]{2,1,0:T(8,128)(2,1)}, bf16[8,192,256]{2,1,0:T(8,128)(2,1)}, ...), branch_computations={%region_6.7_spmd, %region_7.8_spmd} | conditional | flops 1573864 | bytes 3933208 | solution.py:275
  133.7 1.0 pad_maximum_fusion
  134.7 6.8 %all-to-all-start.3 = ((bf16[8,96,512]{2,1,0:T(8,128)(2,1)}), bf16[8,96,512]{2,1,0:T(8,128)(2,1)}, u32[]{:S(2)}, u32[]{:S(2)}) async-start(bf16[8,96,512]{2,1,0:T(8,128)(2,1)} %pad_maximum_fusion), calls=%async_computation.3 | async-start | bytes 1572864 | tf_op jit(solution)/shard_map/cond/branch_1_fun/all_to_all | solution.py:260
  141.5 6.9 %near1.1 = bf16[8,96,256]{2,1,0:T(8,128)(2,1)S(1)} custom-call(bf16[8,192,768]{2,1,0:T(8,128)(2,1)} %get-tuple-element.60.q_ref, bf16[8,288,256]{2,1,0:T(8,128)(2,1)} %get-tuple-element.61.refs_0_.refs_1_, bf16[8,288,256]{2,1,0:T(8,128)(2,1)} %get-tuple-element.61.refs_0_.refs_1_, bf16[8,192,256]{2,1,0:T(8,128)(2,1)} %get-tuple-element.62.refs_2_.refs_3_, ...), custom_call_target="tpu_custom_call" | custom-call | flops 1000 | bytes 1000 | tf_op jit(solution)/shard_map/cond/branch_1_fun/near1/pallas_call | solution.py:182
  148.4 5.5 %all-to-all-done.3 = bf16[8,96,512]{2,1,0:T(8,128)(2,1)} async-done(((bf16[8,96,512]{2,1,0:T(8,128)(2,1)}), bf16[8,96,512]{2,1,0:T(8,128)(2,1)}, u32[]{:S(2)}, u32[]{:S(2)}) %all-to-all-start.3) | async-done | bytes 786464 | tf_op jit(solution)/shard_map/cond/branch_1_fun/all_to_all | solution.py:260
  153.9 0.0 copy-done
  153.9 2.6 %update0.1 = bf16[96,4096]{1,0:T(8,128)(2,1)} custom-call(s32[1]{0:T(128)} %bitcast.3.half_ref, s32[1]{0:T(128)S(6)} %copy.40.levels, bf16[8,96,512]{2,1,0:T(8,128)(2,1)} %get-tuple-element.105.mixed_ref, bf16[192,4096]{1,0:T(8,128)(2,1)} %bitcast.20, f32[50,2,4096]{2,1,0:T(2,128)S(1)} %copy-done, bf16[192,4096]{1,0:T(8,128)(2,1)} %fresh_ref.1), custom_call_target="tpu_custom_call" | custom-call | flops 1000 | bytes 1000 | tf_op jit(solution)/shard_map/update0/pallas_call | solution.py:235
  156.5 0.0 collective-permute-done.5
  156.5 22.4 %conditional.9 = (bf16[96,4096]{1,0:T(8,128)(2,1)S(1)}, bf16[96,4096]{1,0:T(8,128)(2,1)}, bf16[]{:T(256)}, bf16[]{:T(256)}) conditional(s32[]{:T(128)} %bitcast.2, () %tuple.57, (bf16[8,96,256]{2,1,0:T(8,128)(2,1)S(1)}, bf16[8,96,256]{2,1,0:T(8,128)(2,1)S(1)}, s32[1]{0:T(128)}, s32[1]{0:T(128)}, bf16[192,4096]{1,0:T(8,128)(2,1)}, ...), branch_computations={%region_8.9_spmd, %region_9.10_spmd} | conditional | flops 1573864 | bytes 7079000 | solution.py:275
  156.5 0.1 collective-permute-start
  156.6 1.0 pad_maximum_fusion.1
  157.7 4.6 %all-to-all-start.4 = ((bf16[8,96,512]{2,1,0:T(8,128)(2,1)}), bf16[8,96,512]{2,1,0:T(8,128)(2,1)S(1)}, u32[]{:S(2)}, u32[]{:S(2)}) async-start(bf16[8,96,512]{2,1,0:T(8,128)(2,1)} %pad_maximum_fusion.1), calls=%async_computation.4 | async-start | bytes 1572864 | tf_op jit(solution)/shard_map/cond/branch_1_fun/all_to_all | solution.py:260
  162.3 12.4 %all-to-all-done.4.mixed_ref = bf16[8,96,512]{2,1,0:T(8,128)(2,1)S(1)} async-done(((bf16[8,96,512]{2,1,0:T(8,128)(2,1)}), bf16[8,96,512]{2,1,0:T(8,128)(2,1)S(1)}, u32[]{:S(2)}, u32[]{:S(2)}) %all-to-all-start.4) | async-done | bytes 786464 | tf_op jit(solution)/shard_map/cond/branch_1_fun/all_to_all | solution.py:260
  174.7 2.5 %update1.1 = bf16[96,4096]{1,0:T(8,128)(2,1)S(1)} custom-call(s32[1]{0:T(128)} %get-tuple-element.66.half_ref, s32[1]{0:T(128)} %get-tuple-element.67.levels, bf16[8,96,512]{2,1,0:T(8,128)(2,1)S(1)} %all-to-all-done.4.mixed_ref, bf16[192,4096]{1,0:T(8,128)(2,1)} %get-tuple-element.70.latent_ref, f32[50,2,4096]{2,1,0:T(2,128)S(1)} %get-tuple-element.71.mod_ref, ...), custom_call_target="tpu_custom_call" | custom-call | flops 1000 | bytes 1000 | tf_op jit(solution)/shard_map/cond/branch_1_fun/update1/pallas_call | solution.py:235
  177.2 1.8 collective-permute-done
  178.9 0.0 collective-permute-start.6
  178.9 2.4 %pad.7 = bf16[192,4096]{1,0:T(8,128)(2,1)} pad(bf16[96,4096]{1,0:T(8,128)(2,1)} %get-tuple-element.106, bf16[]{:T(256)} %get-tuple-element.107), padding=0_96x0_0 | pad | bytes 2359298 | tf_op jit(solution)/shard_map/jit(_pad)/pad | solution.py:355
  181.3 18.7 %collective-permute-done.6 = bf16[96,4096]{1,0:T(8,128)(2,1)S(1)} collective-permute-done((bf16[96,4096]{1,0:T(8,128)(2,1)S(1)}, bf16[96,4096]{1,0:T(8,128)(2,1)S(1)}, u32[]{:S(2)}, u32[]{:S(2)}) %collective-permute-start.6) | collective-permute-done | bytes 786464 | tf_op jit(solution)/shard_map/ppermute | solution.py:354
  200.1 0.9 bitcast_dynamic-update-slice_fusion
Async XLA Ops:
  2.8 76.4 %collective-permute-start.1 = (bf16[8,288,256]{2,1,0:T(8,128)(2,1)}, bf16[8,288,256]{2,1,0:T(8,128)(2,1)}, u32[]{:S(2)}, u32[]{:S(2)}) collective-permute-start(bf16[8,288,256]{2,1,0:T(8,128)(2,1)} %send0.1.refs_3_), channel_id=1, source_target_pairs={{0,8},{1,9},{2,10},{3,11},{4,12},{5,13},{6,14},{7,15},{8,0},{9,1},... | collective-permute-start | bytes 3538952 | tf_op jit(solution)/shard_map/ppermute | solution.py:256
  35.6 65.4 %collective-permute-start.2 = (bf16[8,192,256]{2,1,0:T(8,128)(2,1)S(1)}, bf16[8,192,256]{2,1,0:T(8,128)(2,1)}, u32[]{:S(2)}, u32[]{:S(2)}) collective-permute-start(bf16[8,192,256]{2,1,0:T(8,128)(2,1)S(1)} %slice.8), channel_id=1, source_target_pairs={{0,8},{1,9},{2,10},{3,11},{4,12},{5,13},{6,14},{7,15},{8,0},{9,1},... | collective-permute-start | bytes 2359304 | tf_op jit(solution)/shard_map/ppermute | solution.py:256
  73.3 43.5 %collective-permute-start.3 = (bf16[8,96,256]{2,1,0:T(8,128)(2,1)}, bf16[8,96,256]{2,1,0:T(8,128)(2,1)S(1)}, u32[]{:S(2)}, u32[]{:S(2)}) collective-permute-start(bf16[8,96,256]{2,1,0:T(8,128)(2,1)} %slice.9), channel_id=1, source_target_pairs={{0,8},{1,9},{2,10},{3,11},{4,12},{5,13},{6,14},{7,15},{8,0},{9,1},... | collective-permute-start | bytes 1179656 | tf_op jit(solution)/shard_map/ppermute | solution.py:256
  79.2 21.8 %all-to-all-start.2 = ((bf16[8,288,256]{2,1,0:T(8,128)(2,1)}), bf16[8,288,256]{2,1,0:T(8,128)(2,1)}, u32[]{:S(2)}, u32[]{:S(2)}) async-start(bf16[8,288,256]{2,1,0:T(8,128)(2,1)} %get-tuple-element.53), calls=%async_computation.2 | async-start | bytes 2359296 | tf_op jit(solution)/shard_map/cond/branch_1_fun/all_to_all | solution.py:260
  109.9 23.8 %collective-permute-start.4 = (bf16[8,96,256]{2,1,0:T(8,128)(2,1)S(1)}, bf16[8,96,256]{2,1,0:T(8,128)(2,1)S(1)}, u32[]{:S(2)}, u32[]{:S(2)}) collective-permute-start(bf16[8,96,256]{2,1,0:T(8,128)(2,1)S(1)} %far0.1), channel_id=1, source_target_pairs={{0,8},{1,9},{2,10},{3,11},{4,12},{5,13},{6,14},{7,15},{8,0},{9,1},... | collective-permute-start | bytes 1179656 | tf_op jit(solution)/shard_map/ppermute | solution.py:256
  132.5 24.0 %collective-permute-start.5 = (bf16[8,96,256]{2,1,0:T(8,128)(2,1)S(1)}, bf16[8,96,256]{2,1,0:T(8,128)(2,1)S(1)}, u32[]{:S(2)}, u32[]{:S(2)}) collective-permute-start(bf16[8,96,256]{2,1,0:T(8,128)(2,1)S(1)} %far1.1), channel_id=1, source_target_pairs={{0,8},{1,9},{2,10},{3,11},{4,12},{5,13},{6,14},{7,15},{8,0},{9,1},... | collective-permute-start | bytes 1179656 | tf_op jit(solution)/shard_map/ppermute | solution.py:256
  133.7 20.2 %copy-start = (f32[50,2,4096]{2,1,0:T(2,128)S(1)}, f32[50,2,4096]{2,1,0:T(2,128)}, u32[]{:S(2)}) copy-start(f32[50,2,4096]{2,1,0:T(2,128)} %mod_ref.1) | copy-start | bytes 4915204
  134.7 19.2 %all-to-all-start.3 = ((bf16[8,96,512]{2,1,0:T(8,128)(2,1)}), bf16[8,96,512]{2,1,0:T(8,128)(2,1)}, u32[]{:S(2)}, u32[]{:S(2)}) async-start(bf16[8,96,512]{2,1,0:T(8,128)(2,1)} %pad_maximum_fusion), calls=%async_computation.3 | async-start | bytes 1572864 | tf_op jit(solution)/shard_map/cond/branch_1_fun/all_to_all | solution.py:260
  156.5 22.4 %collective-permute-start = (bf16[96,4096]{1,0:T(8,128)(2,1)}, bf16[96,4096]{1,0:T(8,128)(2,1)}, u32[]{:S(2)}, u32[]{:S(2)}) collective-permute-start(bf16[96,4096]{1,0:T(8,128)(2,1)} %get-tuple-element.73), channel_id=1, source_target_pairs={{0,16},{16,32},{32,48},{48,64},{64,80},{80,96},{96,112},{112,128},... | collective-permute-start | bytes 2359304 | tf_op jit(solution)/shard_map/cond/branch_1_fun/ppermute | solution.py:351
  157.7 17.0 %all-to-all-start.4 = ((bf16[8,96,512]{2,1,0:T(8,128)(2,1)}), bf16[8,96,512]{2,1,0:T(8,128)(2,1)S(1)}, u32[]{:S(2)}, u32[]{:S(2)}) async-start(bf16[8,96,512]{2,1,0:T(8,128)(2,1)} %pad_maximum_fusion.1), calls=%async_computation.4 | async-start | bytes 1572864 | tf_op jit(solution)/shard_map/cond/branch_1_fun/all_to_all | solution.py:260
  178.9 21.2 %collective-permute-start.6 = (bf16[96,4096]{1,0:T(8,128)(2,1)S(1)}, bf16[96,4096]{1,0:T(8,128)(2,1)S(1)}, u32[]{:S(2)}, u32[]{:S(2)}) collective-permute-start(bf16[96,4096]{1,0:T(8,128)(2,1)S(1)} %get-tuple-element.108), channel_id=1, source_target_pairs={{0,16},{16,32},{32,48},{48,64},{64,80},{80,96},{96,112},{112,128},... | collective-permute-start | bytes 2359304 | tf_op jit(solution)/shard_map/ppermute | solution.py:354
